TPU v7x, 256 devices: a whole 4x4x8 slice. The times are simulated.
256 devices in a mesh: gy: 32 (over z, y), gz: 8 (over x, core).
Axes of the slice: x: 4, y: 4, z: 8, core: 2. Of those that a mesh axis runs over, the one named last changes fastest.
Arguments:
- flow_field: float32 [4, 512, 128, 1024], P(None, 'gy', 'gz'), may hold values from -8 to 8
Outputs:
- coefficients: float32 [4, 512, 128, 1024], P(None, 'gy', 'gz')
All inputs are finite; a program needn't handle non-finite values.
Results may differ from a plain program's by a relative error of at most 0.000075.
Values sent between devices are 32-bit elements; how exact they have to be, the bound alone decides.
No kernel may reach another device: no remote copies, remote signals or barrier semaphores. Data moves between devices by JAX's collectives and lax.ppermute only.
A program may use at most 192 MiB of HBM per device.

v0:
```python
import jax
import jax.numpy as jnp
import ml_dtypes
import numpy as np
from jax import lax
from jax.experimental import pallas as pl
from jax.experimental.pallas import tpu as pltpu
from jax.sharding import PartitionSpec as P

ALPHA = -1.586134342059924
BETA = -0.052980118572961
GAMMA = 0.882911075530934
DELTA = 0.443506852043971
KAPPA = 1.149604398860241

F32 = jnp.float32
BF16 = jnp.bfloat16
ROWS = 16


def pair_matrix(length):
    cells = np.eye(length)
    even, odd = cells[0::2].copy(), cells[1::2].copy()
    odd = odd + ALPHA * (even + np.roll(even, -1, 0))
    even = even + BETA * (odd + np.roll(odd, 1, 0))
    odd = odd + GAMMA * (even + np.roll(even, -1, 0))
    even = even + DELTA * (odd + np.roll(odd, 1, 0))
    return even * KAPPA, odd / KAPPA


def alternated(length):
    low, high = pair_matrix(length)
    table = np.zeros((length, length))
    table[0::2], table[1::2] = low, high
    return table


def chain_blocks():
    count = 8
    length = count * ROWS
    first = alternated(length)
    second = alternated(length // 2) @ first[0::2]
    third = alternated(length // 4) @ second[0::2]
    result = []
    for table, per in ((first, 16), (second, 8), (third, 4)):
        here = table[4 * per : 5 * per]
        result.append({k: here[:, (4 + k) * ROWS : (5 + k) * ROWS] for k in (-2, -1, 0, 1, 2)})
    return result


def factor(block, rank):
    left, size, right = np.linalg.svd(block, full_matrices=False)
    assert np.all(size[rank:] < 1e-12)
    return left[:, :rank] * size[:rank], right[:rank]


def split_const(table):
    table = np.asarray(table, np.float64)
    high = table.astype(ml_dtypes.bfloat16)
    low = (table - high.astype(np.float64)).astype(ml_dtypes.bfloat16)
    return high, low


def stack(*parts):
    return np.concatenate(parts, 0)


def tables(nx):
    first, second, third = chain_blocks()
    eye = np.eye
    sides = (-1, 1)
    out = {}
    give0, send0, give1, send1, give2a, give2b, send2 = {}, {}, {}, {}, {}, {}, {}
    give2, send2d, give22, send22 = {}, {}, {}, {}
    for s in sides:
        give0[s], send0[s] = factor(first[s], 2)
        give1[s], send1[s] = factor(second[s], 3)
        give2a[s] = third[s] @ send1[s].T
        give2b[s], send2[s] = factor(third[s] - give2a[s] @ send1[s], 2)
        give2[s], send2d[s] = factor(third[s], 4)
        give22[s], send22[s] = factor(third[2 * s], 2)
    out["send0"] = send0

    low, high = pair_matrix(nx)
    out["tx"] = np.concatenate([low[128:256, 128:640], high[128:256, 128:640]], 0).T
    low, high = pair_matrix(nx // 2)
    tx1 = np.concatenate([low, high], 0).T
    low, high = pair_matrix(nx // 4)
    tx2 = np.concatenate([low, high], 0).T
    out["tx1"], out["tx2"] = tx1, tx2
    out["tx12"] = tx1[:, : nx // 4] @ tx2

    def planes(send):
        return np.einsum("pz,ab->paBz".replace("B", "b"), send, eye(ROWS)).reshape(-1, ROWS * ROWS)

    out["zsend"] = stack(
        *[planes(send1[s]) for s in sides],
        *[planes(send2[s]) for s in sides],
        *[planes(send22[s]) for s in sides],
    )
    out["zown"] = stack(np.kron(eye(ROWS), second[0]), np.kron(eye(ROWS), third[0]))

    def back(give):
        return np.einsum("zp,ab->azpb", give, eye(ROWS)).reshape(ROWS * give.shape[0], -1)

    out["zgive1"] = np.concatenate([back(give1[s]) for s in sides], 1)
    out["zgive2"] = np.concatenate(
        [back(give2a[s]) for s in sides] + [back(give2b[s]) for s in sides] + [back(give22[s]) for s in sides], 1
    )
    out["ychain1"] = stack(np.kron(second[0], eye(8)), *[np.kron(send1[s], eye(8)) for s in sides])
    out["ychain2"] = stack(
        np.kron(third[0], eye(4)),
        *[np.kron(send2d[s], eye(4)) for s in sides],
        *[np.kron(send22[s], eye(4)) for s in sides],
    )
    out["ygive1"] = np.concatenate([np.kron(give1[s], eye(8)) for s in sides], 1)
    out["ygive2"] = np.concatenate(
        [np.kron(give2[s], eye(4)) for s in sides] + [np.kron(give22[s], eye(4)) for s in sides], 1
    )
    own = np.concatenate([np.kron(first[0], first[0])] + [np.kron(give0[s], first[0]) for s in sides], 1)
    sends = []
    for s in sides:
        for p in range(2):
            plane = send0[s][p][None]
            sends.append(
                np.concatenate([np.kron(first[0], plane)] + [np.kron(give0[t], plane) for t in sides], 1)
            )
    out["level0"] = stack(own, *sends)
    out["zgive0"] = np.concatenate([back(give0[s]) for s in sides], 1)
    return out


def split(value):
    high = value.astype(BF16)
    low = (value - high.astype(F32)).astype(BF16)
    return high, low


def dot(a, b):
    return jnp.dot(a, b, preferred_element_type=F32)


def left(table, rows):
    return dot(table[0], rows[0]) + (dot(table[0], rows[1]) + dot(table[1], rows[0]))


def right(rows, table):
    return dot(rows[0], table[0]) + (dot(rows[0], table[1]) + dot(rows[1], table[0]))


def both(high_ref, low_ref):
    return high_ref[...], low_ref[...]


def place(table, rows):
    high, low = split(rows)
    return dot(table, high) + dot(table, low)


def even_cells(width, shape):
    row = lax.broadcasted_iota(jnp.int32, shape, 0)
    return ((row | (row // width)) & 1) == 0


def lift_x(rows, table, nx, store):
    blocks = nx // 256
    for j in range(blocks):
        window = []
        for part in rows:
            if j == 0:
                window.append(jnp.concatenate([part[:, nx - 128 :], part[:, :384]], 1))
            elif j == blocks - 1:
                window.append(jnp.concatenate([part[:, nx - 384 :], part[:, :128]], 1))
            else:
                window.append(part[:, 256 * j - 128 : 256 * j + 384])
        store(j, right(window, table))


def send_y_kernel(send0, head_ref, tail_ref, to_right_ref, to_left_ref):
    for p in range(2):
        to_right_ref[0, p] = sum(float(send0[-1][p, 12 + k]) * tail_ref[0, k] for k in range(4))
        to_left_ref[0, p] = sum(float(send0[1][p, k]) * head_ref[0, k] for k in range(3))


def lift_kernel(nx, x_ref, txh, txl, zsh, zsl, t1h, t1l, t12h, t12l, uh_ref, ul_ref, r1_ref, l1_ref, r2_ref, l2_ref):
    half = nx // 2
    quarter = nx // 4

    def store(j, value):
        for k, at in enumerate((128 * j, half + 128 * j)):
            high, low = split(value[:, 128 * k : 128 * k + 128])
            uh_ref[0, :, at : at + 128] = high
            ul_ref[0, :, at : at + 128] = low

    lift_x(split(x_ref[0]), both(txh, txl), nx, store)
    planes = split(left(both(zsh, zsl), (uh_ref[0, :, :half], ul_ref[0, :, :half])))
    near = right([v[:96] for v in planes], both(t1h, t1l))
    far = right([v[96:] for v in planes], both(t12h, t12l))
    for k, (ref, ref2) in enumerate(((r1_ref, r2_ref), (l1_ref, l2_ref))):
        ref[0, :48] = near[48 * k : 48 * k + 48]
        for p in range(2):
            lanes = slice(quarter * p, quarter * p + quarter)
            ref[0, 48:, lanes] = far[32 * k + 16 * p : 32 * k + 16 * p + 16]
            ref2[0, :, lanes] = far[64 + 32 * k + 16 * p : 64 + 32 * k + 16 * p + 16]


def own_kernel(nx, uh_ref, ul_ref, zoh, zol, t1h, t1l, t12h, t12l, a1_ref, a2_ref):
    half = nx // 2
    rows = split(left(both(zoh, zol), (uh_ref[0, :, :half], ul_ref[0, :, :half])))
    a1_ref[0] = right([v[:128] for v in rows], both(t1h, t1l))
    a2_ref[0] = right([v[128:] for v in rows], both(t12h, t12l))


def chain_kernel(
    nx, a1_ref, a2_ref, l1_ref, r1_ref, l2_ref, r2_ref,
    g1h, g1l, g2h, g2l, t2h, t2l, c1h, c1l, c2h, c2l,
    o1_ref, o2_ref, to_r_ref, to_l_ref, to_r2_ref, to_l2_ref,
):
    quarter = nx // 4
    near = split(jnp.concatenate([l1_ref[0, :48], r1_ref[0, :48]], 0))
    a1 = split(a1_ref[0] + left(both(g1h, g1l), near))
    deep = [right([v[:, :quarter] for v in near], both(t2h, t2l))]
    for ref in (l1_ref, r1_ref):
        deep += [ref[0, 48:, :quarter], ref[0, 48:, quarter:]]
    for ref in (l2_ref, r2_ref):
        deep += [ref[0, :, :quarter], ref[0, :, quarter:]]
    a2 = split(a2_ref[0] + left(both(g2h, g2l), split(jnp.concatenate(deep, 0))))
    first = left(both(c1h, c1l), a1)
    second = left(both(c2h, c2l), a2)
    o1_ref[0] = first[:64]
    o2_ref[0] = second[:16]
    for k, (ref, ref2) in enumerate(((to_r_ref, to_r2_ref), (to_l_ref, to_l2_ref))):
        ref[0, :24] = first[64 + 24 * k : 88 + 24 * k]
        ref[0, 24:, :quarter] = second[16 + 16 * k : 24 + 16 * k]
        ref[0, 24:, quarter:] = second[24 + 16 * k : 32 + 16 * k]
        ref2[0] = second[48 + 8 * k : 56 + 8 * k]


def level0_kernel(nx, uh_ref, ul_ref, l_ref, r_ref, txh, txl, mh, ml, out_ref, to_r_ref, to_l_ref, high_ref, low_ref):
    half = nx // 2
    high_ref[:256] = uh_ref[0]
    low_ref[:256] = ul_ref[0]

    def store(j, value):
        for k, at in enumerate((128 * j, half + 128 * j)):
            high, low = split(value[:, 128 * k : 128 * k + 128])
            high_ref[256:, at : at + 128] = high
            low_ref[256:, at : at + 128] = low

    halo = jnp.concatenate([l_ref[0, 0], l_ref[0, 1], r_ref[0, 0], r_ref[0, 1]], 0)
    lift_x(split(halo), both(txh, txl), nx, store)
    rows = left(both(mh, ml), both(high_ref, low_ref))
    out_ref[0] = rows[:256]
    to_r_ref[0] = rows[256:288]
    to_l_ref[0] = rows[288:]


def last_kernel(
    nx, part_ref, o1_ref, o2_ref, l0_ref, r0_ref, l1_ref, r1_ref, l2_ref, r2_ref,
    g0h, g0l, g1h, g1l, g2h, g2l, e1, e2, out_ref,
):
    half = nx // 2
    quarter = nx // 4
    halo = split(jnp.concatenate([l0_ref[0], r0_ref[0]], 0))
    rows = part_ref[0] + left(both(g0h, g0l), halo)
    near = split(jnp.concatenate([l1_ref[0, :24], r1_ref[0, :24]], 0))
    first = o1_ref[0] + left(both(g1h, g1l), near)
    deep = []
    for ref in (l1_ref, r1_ref):
        deep += [ref[0, 24:, :quarter], ref[0, 24:, quarter:]]
    deep += [l2_ref[0], r2_ref[0]]
    second = o2_ref[0] + left(both(g2h, g2l), split(jnp.concatenate(deep, 0)))
    placed = place(e2[...], second)
    inner = jnp.where(even_cells(8, (64, quarter)), placed, first[:, :quarter])
    placed = place(e1[...], jnp.concatenate([inner, first[:, quarter:]], 1))
    window = jnp.where(even_cells(ROWS, (256, half)), placed, rows[:, :half])
    out_ref[0, :, :half] = window
    out_ref[0, :, half:] = rows[:, half:]


def call(body, ins, outs, consts, flops, scratch=()):
    count = ins[0].shape[0]

    def cut(shape):
        rest = len(shape) - 1
        return pl.BlockSpec((1,) + tuple(shape[1:]), lambda c: (c,) + (0,) * rest)

    def whole(shape):
        return pl.BlockSpec(tuple(shape), lambda c: (0,) * len(shape))

    moved = sum(a.size * a.dtype.itemsize for a in ins)
    moved += sum(int(np.prod(s)) * jnp.dtype(d).itemsize for s, d in outs)
    return pl.pallas_call(
        body,
        grid=(count,),
        in_specs=[cut(a.shape) for a in ins] + [whole(a.shape) for a in consts],
        out_specs=[cut(s) for s, _ in outs],
        out_shape=[jax.ShapeDtypeStruct(s, d) for s, d in outs],
        scratch_shapes=list(scratch),
        compiler_params=pltpu.CompilerParams(vmem_limit_bytes=40 * 1024 * 1024),
        cost_estimate=pl.CostEstimate(flops=flops, bytes_accessed=moved, transcendentals=0),
    )(*ins, *consts)


def move(value, axis, step):
    count = lax.axis_size(axis)
    return lax.ppermute(value, axis, [(i, (i + step) % count) for i in range(count)])


def local(flow_field):
    comps, ny, nz, nx = flow_field.shape
    assert ny == ROWS and nz == ROWS and nx % 512 == 0
    assert lax.axis_size("gy") >= 5 and lax.axis_size("gz") >= 5
    half, quarter = nx // 2, nx // 4
    table = tables(nx)
    send0 = table.pop("send0")
    pairs = {k: [jnp.asarray(p) for p in split_const(v)] for k, v in table.items()}

    def consts(*names):
        return [p for n in names for p in pairs[n]]

    spread = []
    for width in (ROWS, ROWS // 2):
        every = np.eye(width)[:, 0::2]
        spread.append(jnp.asarray(np.kron(every, every).astype(ml_dtypes.bfloat16)))

    flat = flow_field.reshape(comps, ROWS * ROWS, nx)

    edge = (1, 4, ROWS, nx)
    y_right, y_left = pl.pallas_call(
        lambda *refs: send_y_kernel(send0, *refs),
        grid=(comps,),
        in_specs=[pl.BlockSpec(edge, lambda c: (c, 0, 0, 0)), pl.BlockSpec(edge, lambda c: (c, 3, 0, 0))],
        out_specs=[pl.BlockSpec((1, 2, ROWS, nx), lambda c: (c, 0, 0, 0))] * 2,
        out_shape=[jax.ShapeDtypeStruct((comps, 2, ROWS, nx), F32)] * 2,
        cost_estimate=pl.CostEstimate(flops=1 << 22, bytes_accessed=1 << 22, transcendentals=0),
    )(flow_field, flow_field)
    from_left0 = move(y_right, "gy", 1)
    from_right0 = move(y_left, "gy", -1)

    near = (comps, 64, half)
    far = (comps, 16, half)
    uh, ul, z_right, z_left, z_right2, z_left2 = call(
        lambda *refs: lift_kernel(nx, *refs),
        [flat],
        [((comps, 256, nx), BF16)] * 2 + [(near, F32)] * 2 + [(far, F32)] * 2,
        consts("tx", "zsend", "tx1", "tx12"),
        1 << 33,
    )
    z_from_left2 = move(z_right2, "gz", 2)
    z_from_left = move(z_right, "gz", 1)
    z_from_right = move(z_left, "gz", -1)
    z_from_right2 = move(z_left2, "gz", -2)

    a1, a2 = call(
        lambda *refs: own_kernel(nx, *refs),
        [uh, ul],
        [((comps, 128, half), F32), ((comps, 64, quarter), F32)],
        consts("zown", "tx1", "tx12"),
        1 << 32,
    )
    o1, o2, y1_right, y1_left, y2_right, y2_left = call(
        lambda *refs: chain_kernel(nx, *refs),
        [a1, a2, z_from_left, z_from_right, z_from_left2, z_from_right2],
        [((comps, 64, half), F32), ((comps, 16, quarter), F32)]
        + [((comps, 32, half), F32)] * 2
        + [((comps, 8, quarter), F32)] * 2,
        consts("zgive1", "zgive2", "tx2", "ychain1", "ychain2"),
        1 << 31,
    )
    y_from_left2 = move(y2_right, "gy", 2)
    y_from_left = move(y1_right, "gy", 1)
    y_from_right = move(y1_left, "gy", -1)
    y_from_right2 = move(y2_left, "gy", -2)

    part, z0_right, z0_left = call(
        lambda *refs: level0_kernel(nx, *refs),
        [uh, ul, from_left0, from_right0],
        [((comps, 256, nx), F32)] + [((comps, 32, nx), F32)] * 2,
        consts("tx", "level0"),
        1 << 33,
        [pltpu.VMEM((320, nx), BF16)] * 2,
    )
    z0_from_left = move(z0_right, "gz", 1)
    z0_from_right = move(z0_left, "gz", -1)

    (result,) = call(
        lambda *refs: last_kernel(nx, *refs),
        [part, o1, o2, z0_from_left, z0_from_right, y_from_left, y_from_right, y_from_left2, y_from_right2],
        [((comps, ROWS * ROWS, nx), F32)],
        consts("zgive0", "ygive1", "ygive2") + spread,
        1 << 31,
    )
    return result.reshape(flow_field.shape)


def solution(mesh):
    placed = P(None, "gy", "gz", None)
    return jax.shard_map(local, mesh=mesh, in_specs=(placed,), out_specs=placed, check_vma=False)
```

profile of v0, /device:TPU:0, one launch (start us, length us, event | category | flops | bytes accessed | tf_op | source)
XLA Modules:
  0.0 70.2 jit_solution(5929476743253954849)
XLA Ops:
  0.0 0.0 copy-start.14
  0.0 0.0 copy-start.19
  0.0 0.0 copy-start.20
  0.1 3.8 %shard_map.290 = (f32[4,2,16,1024]{3,2,1,0:T(8,128)}, f32[4,2,16,1024]{3,2,1,0:T(8,128)}) custom-call(f32[4,16,16,1024]{3,2,1,0:T(8,128)} %refs_1_.2, f32[4,16,16,1024]{3,2,1,0:T(8,128)} %refs_1_.2), custom_call_target="tpu_custom_call" | custom-call | flops 4194304 | bytes 4194304 | tf_op jit(solution)/shard_map/pallas_call | solution.py:330
  3.9 6.6 %collective-permute-start.1 = (f32[4,2,16,1024]{3,2,1,0:T(8,128)}, f32[4,2,16,1024]{3,2,1,0:T(8,128)S(1)}, u32[]{:S(2)}, u32[]{:S(2)}) collective-permute-start(f32[4,2,16,1024]{3,2,1,0:T(8,128)} %get-tuple-element.27), channel_id=1, source_target_pairs={{0,248},{8,0},{16,8},{24,16},{32,24},{40,32},{48,40},{56,48},{64,5... | collective-permute-start | bytes 1572872 | tf_op jit(solution)/shard_map/ppermute | solution.py:307
  10.6 2.2 %copy-done = f32[4,16,16,1024]{3,2,1,0:T(8,128)S(1)} copy-done((f32[4,16,16,1024]{3,2,1,0:T(8,128)S(1)}, f32[4,16,16,1024]{3,2,1,0:T(8,128)}, u32[]{:S(2)}) %copy-start) | copy-done | bytes 4194328
  12.7 7.7 %shard_map.289 = (bf16[4,256,1024]{2,1,0:T(8,128)(2,1)S(1)}, bf16[4,256,1024]{2,1,0:T(8,128)(2,1)S(1)}, f32[4,64,512]{2,1,0:T(8,128)S(1)}, f32[4,64,512]{2,1,0:T...) custom-call(f32[4,256,1024]{2,1,0:T(8,128)S(1)} %bitcast.2, bf16[512,256]{1,0:T(8,128)(2,1)S(1)} %copy-done.14, ...), custom_call_target="tpu_custom_call" | custom-call | flops 8589934592 | bytes 9699328 | tf_op jit(solution)/shard_map/pallas_call | solution.py:293
  20.5 1.3 %copy-done.31 = bf16[4,256,1024]{2,1,0:T(8,128)(2,1)} copy-done((bf16[4,256,1024]{2,1,0:T(8,128)(2,1)}, bf16[4,256,1024]{2,1,0:T(8,128)(2,1)S(1)}, u32[]{:S(2)}) %copy-start.31) | copy-done | bytes 2097176
  21.8 1.5 %collective-permute-start.4 = (f32[4,16,512]{2,1,0:T(8,128)S(1)}, f32[4,16,512]{2,1,0:T(8,128)S(1)}, u32[]{:S(2)}, u32[]{:S(2)}) collective-permute-start(f32[4,16,512]{2,1,0:T(8,128)S(1)} %get-tuple-element.33), channel_id=1, source_target_pairs={{0,2},{1,3},{2,4},{3,5},{4,6},{5,7},{6,0},{7,1},{8,10},{9,11},{10,... | collective-permute-start | bytes 393224 | tf_op jit(solution)/shard_map/ppermute | solution.py:307
  23.3 1.7 %collective-permute-start.5 = (f32[4,16,512]{2,1,0:T(8,128)S(1)}, f32[4,16,512]{2,1,0:T(8,128)S(1)}, u32[]{:S(2)}, u32[]{:S(2)}) collective-permute-start(f32[4,16,512]{2,1,0:T(8,128)S(1)} %get-tuple-element.34), channel_id=1, source_target_pairs={{0,6},{1,7},{2,0},{3,1},{4,2},{5,3},{6,4},{7,5},{8,14},{9,15},{10,... | collective-permute-start | bytes 393224 | tf_op jit(solution)/shard_map/ppermute | solution.py:307
  25.0 3.0 %collective-permute-start.3 = (f32[4,64,512]{2,1,0:T(8,128)S(1)}, f32[4,64,512]{2,1,0:T(8,128)S(1)}, u32[]{:S(2)}, u32[]{:S(2)}) collective-permute-start(f32[4,64,512]{2,1,0:T(8,128)S(1)} %get-tuple-element.32), channel_id=1, source_target_pairs={{0,7},{1,0},{2,1},{3,2},{4,3},{5,4},{6,5},{7,6},{8,15},{9,8},{10,9... | collective-permute-start | bytes 1572872 | tf_op jit(solution)/shard_map/ppermute | solution.py:307
  28.0 1.6 %copy-done.32 = bf16[4,256,1024]{2,1,0:T(8,128)(2,1)S(1)} copy-done((bf16[4,256,1024]{2,1,0:T(8,128)(2,1)S(1)}, bf16[4,256,1024]{2,1,0:T(8,128)(2,1)}, u32[]{:S(2)}) %copy-start.32) | copy-done | bytes 2097176
  29.6 7.0 %shard_map.291 = (f32[4,256,1024]{2,1,0:T(8,128)S(1)}, f32[4,32,1024]{2,1,0:T(8,128)S(1)}, f32[4,32,1024]{2,1,0:T(8,128)S(1)}) custom-call(bf16[4,256,1024]{2,1,0:T(8,128)(2,1)S(1)} %get-tuple-element.24.refs_0_, bf16[4,256,1024]{2,1,0:T(8,128)(2,1)S(1)} %copy-done.32, f32[4,2,16,1024]{3,2,1,0:T(8,128)S(1)} %collective-permute-done.refs_2_, ...), custom_call_target="tpu_custom_call" | custom-call | flops 8589934592 | bytes 10485760 | tf_op jit(solution)/shard_map/pallas_call | solution.py:293
  36.6 0.0 collective-permute-start.6
  36.7 0.0 copy-start.18
  36.7 0.0 copy-start.23
  36.8 2.9 %collective-permute-start.7 = (f32[4,32,1024]{2,1,0:T(8,128)S(1)}, f32[4,32,1024]{2,1,0:T(8,128)S(1)}, u32[]{:S(2)}, u32[]{:S(2)}) collective-permute-start(f32[4,32,1024]{2,1,0:T(8,128)S(1)} %get-tuple-element.38), channel_id=1, source_target_pairs={{0,7},{1,0},{2,1},{3,2},{4,3},{5,4},{6,5},{7,6},{8,15},{9,8},{10,9... | collective-permute-start | bytes 1572872 | tf_op jit(solution)/shard_map/ppermute | solution.py:307
  39.7 3.6 %shard_map.292 = (f32[4,128,512]{2,1,0:T(8,128)S(1)}, f32[4,64,256]{2,1,0:T(8,128)S(1)}) custom-call(bf16[4,256,1024]{2,1,0:T(8,128)(2,1)S(1)} %get-tuple-element.24.refs_0_, bf16[4,256,1024]{2,1,0:T(8,128)(2,1)S(1)} %copy-done.33, bf16[192,256]{1,0:T(8,128)(2,1)S(1)} %copy-done.22, bf16[192,256]{1,0:T(8,128)(2,1)S(1)} %copy-done.21, ...), custom_call_target="tpu_custom_call" | custom-call | flops 4294967296 | bytes 5505024 | tf_op jit(solution)/shard_map/pallas_call | solution.py:293
  43.5 3.0 %shard_map.293 = (f32[4,64,512]{2,1,0:T(8,128)S(1)}, f32[4,16,256]{2,1,0:T(8,128)S(1)}, f32[4,32,512]{2,1,0:T(8,128)S(1)}, f32[4,32,512]{2,1,0:T(8,128)S(1)}, f3...) custom-call(f32[4,128,512]{2,1,0:T(8,128)S(1)} %get-tuple-element.29.refs_0_, ...), custom_call_target="tpu_custom_call" | custom-call | flops 2147483648 | bytes 3801088 | tf_op jit(solution)/shard_map/pallas_call | solution.py:293
  46.5 0.1 collective-permute-start.8
  46.6 5.3 %collective-permute-start.9 = (f32[4,32,512]{2,1,0:T(8,128)S(1)}, f32[4,32,512]{2,1,0:T(8,128)S(1)}, u32[]{:S(2)}, u32[]{:S(2)}) collective-permute-start(f32[4,32,512]{2,1,0:T(8,128)S(1)} %get-tuple-element.40), channel_id=1, source_target_pairs={{0,248},{8,0},{16,8},{24,16},{32,24},{40,32},{48,40},{56,48},{64,5... | collective-permute-start | bytes 786440 | tf_op jit(solution)/shard_map/ppermute | solution.py:307
  52.0 7.5 %collective-permute-done.10.refs_7_ = f32[4,8,256]{2,1,0:T(8,128)S(1)} collective-permute-done((f32[4,8,256]{2,1,0:T(8,128)S(1)}, f32[4,8,256]{2,1,0:T(8,128)S(1)}, u32[]{:S(2)}, u32[]{:S(2)}) %collective-permute-start.10) | collective-permute-done | bytes 32800 | tf_op jit(solution)/shard_map/ppermute | solution.py:307
  59.5 5.4 %collective-permute-done.11.refs_8_ = f32[4,8,256]{2,1,0:T(8,128)S(1)} collective-permute-done((f32[4,8,256]{2,1,0:T(8,128)S(1)}, f32[4,8,256]{2,1,0:T(8,128)S(1)}, u32[]{:S(2)}, u32[]{:S(2)}) %collective-permute-start.11) | collective-permute-done | bytes 32800 | tf_op jit(solution)/shard_map/ppermute | solution.py:307
  65.0 5.1 %shard_map.294 = f32[4,256,1024]{2,1,0:T(8,128)} custom-call(f32[4,256,1024]{2,1,0:T(8,128)S(1)} %get-tuple-element.28.refs_0_, f32[4,64,512]{2,1,0:T(8,128)S(1)} %get-tuple-element.35.refs_1_, f32[4,16,256]{2,1,0:T(8,128)S(1)} %get-tuple-element.36.refs_2_, f32[4,32,1024]{2,1,0:T(8,128)S(1)} %collective-permute-done.6.refs_3_, ...), custom_call_target="tpu_custom_call" | custom-call | flops 2147483648 | bytes 10616832 | tf_op jit(solution)/shard_map/pallas_call | solution.py:293
  (74 shorter events, 0.2 us)
Async XLA Ops:
  0.0 10.5 %copy-start.13 = (bf16[512,256]{1,0:T(8,128)(2,1)S(1)}, bf16[512,256]{1,0:T(8,128)(2,1)}, u32[]{:S(2)}) copy-start(bf16[512,256]{1,0:T(8,128)(2,1)} %constant.61.clone.refs_2_.refs_5_) | copy-start | bytes 786436
  0.0 10.5 %copy-start.14 = (bf16[512,256]{1,0:T(8,128)(2,1)S(1)}, bf16[512,256]{1,0:T(8,128)(2,1)}, u32[]{:S(2)}) copy-start(bf16[512,256]{1,0:T(8,128)(2,1)} %constant.60.clone.refs_1_.refs_4_) | copy-start | bytes 786436
  3.9 21.2 %collective-permute-start = (f32[4,2,16,1024]{3,2,1,0:T(8,128)}, f32[4,2,16,1024]{3,2,1,0:T(8,128)S(1)}, u32[]{:S(2)}, u32[]{:S(2)}) collective-permute-start(f32[4,2,16,1024]{3,2,1,0:T(8,128)} %get-tuple-element.26), channel_id=1, source_target_pairs={{0,8},{8,16},{16,24},{24,32},{32,40},{40,48},{48,56},{56,64},{64,7... | collective-permute-start | bytes 1572872 | tf_op jit(solution)/shard_map/ppermute | solution.py:307
  3.9 24.1 %collective-permute-start.1 = (f32[4,2,16,1024]{3,2,1,0:T(8,128)}, f32[4,2,16,1024]{3,2,1,0:T(8,128)S(1)}, u32[]{:S(2)}, u32[]{:S(2)}) collective-permute-start(f32[4,2,16,1024]{3,2,1,0:T(8,128)} %get-tuple-element.27), channel_id=1, source_target_pairs={{0,248},{8,0},{16,8},{24,16},{32,24},{40,32},{48,40},{56,48},{64,5... | collective-permute-start | bytes 1572872 | tf_op jit(solution)/shard_map/ppermute | solution.py:307
  12.7 15.3 %copy-start.15 = (bf16[320,320]{1,0:T(8,128)(2,1)S(1)}, bf16[320,320]{1,0:T(8,128)(2,1)}, u32[]{:S(2)}) copy-start(bf16[320,320]{1,0:T(8,128)(2,1)} %constant.85.clone.refs_7_) | copy-start | bytes 614404
  12.7 15.3 %copy-start.16 = (bf16[320,320]{1,0:T(8,128)(2,1)S(1)}, bf16[320,320]{1,0:T(8,128)(2,1)}, u32[]{:S(2)}) copy-start(bf16[320,320]{1,0:T(8,128)(2,1)} %constant.84.clone.refs_6_) | copy-start | bytes 614404
  21.8 14.9 %collective-permute-start.4 = (f32[4,16,512]{2,1,0:T(8,128)S(1)}, f32[4,16,512]{2,1,0:T(8,128)S(1)}, u32[]{:S(2)}, u32[]{:S(2)}) collective-permute-start(f32[4,16,512]{2,1,0:T(8,128)S(1)} %get-tuple-element.33), channel_id=1, source_target_pairs={{0,2},{1,3},{2,4},{3,5},{4,6},{5,7},{6,0},{7,1},{8,10},{9,11},{10,... | collective-permute-start | bytes 393224 | tf_op jit(solution)/shard_map/ppermute | solution.py:307
  23.3 20.1 %collective-permute-start.5 = (f32[4,16,512]{2,1,0:T(8,128)S(1)}, f32[4,16,512]{2,1,0:T(8,128)S(1)}, u32[]{:S(2)}, u32[]{:S(2)}) collective-permute-start(f32[4,16,512]{2,1,0:T(8,128)S(1)} %get-tuple-element.34), channel_id=1, source_target_pairs={{0,6},{1,7},{2,0},{3,1},{4,2},{5,3},{6,4},{7,5},{8,14},{9,15},{10,... | collective-permute-start | bytes 393224 | tf_op jit(solution)/shard_map/ppermute | solution.py:307
  25.0 18.4 %collective-permute-start.2 = (f32[4,64,512]{2,1,0:T(8,128)S(1)}, f32[4,64,512]{2,1,0:T(8,128)S(1)}, u32[]{:S(2)}, u32[]{:S(2)}) collective-permute-start(f32[4,64,512]{2,1,0:T(8,128)S(1)} %get-tuple-element.31), channel_id=1, source_target_pairs={{0,1},{1,2},{2,3},{3,4},{4,5},{5,6},{6,7},{7,0},{8,9},{9,10},{10,1... | collective-permute-start | bytes 1572872 | tf_op jit(solution)/shard_map/ppermute | solution.py:307
  25.0 18.4 %collective-permute-start.3 = (f32[4,64,512]{2,1,0:T(8,128)S(1)}, f32[4,64,512]{2,1,0:T(8,128)S(1)}, u32[]{:S(2)}, u32[]{:S(2)}) collective-permute-start(f32[4,64,512]{2,1,0:T(8,128)S(1)} %get-tuple-element.32), channel_id=1, source_target_pairs={{0,7},{1,0},{2,1},{3,2},{4,3},{5,4},{6,5},{7,6},{8,15},{9,8},{10,9... | collective-permute-start | bytes 1572872 | tf_op jit(solution)/shard_map/ppermute | solution.py:307
  36.6 28.3 %collective-permute-start.6 = (f32[4,32,1024]{2,1,0:T(8,128)S(1)}, f32[4,32,1024]{2,1,0:T(8,128)S(1)}, u32[]{:S(2)}, u32[]{:S(2)}) collective-permute-start(f32[4,32,1024]{2,1,0:T(8,128)S(1)} %get-tuple-element.37), channel_id=1, source_target_pairs={{0,1},{1,2},{2,3},{3,4},{4,5},{5,6},{6,7},{7,0},{8,9},{9,10},{10,1... | collective-permute-start | bytes 1572872 | tf_op jit(solution)/shard_map/ppermute | solution.py:307
  36.8 28.1 %collective-permute-start.7 = (f32[4,32,1024]{2,1,0:T(8,128)S(1)}, f32[4,32,1024]{2,1,0:T(8,128)S(1)}, u32[]{:S(2)}, u32[]{:S(2)}) collective-permute-start(f32[4,32,1024]{2,1,0:T(8,128)S(1)} %get-tuple-element.38), channel_id=1, source_target_pairs={{0,7},{1,0},{2,1},{3,2},{4,3},{5,4},{6,5},{7,6},{8,15},{9,8},{10,9... | collective-permute-start | bytes 1572872 | tf_op jit(solution)/shard_map/ppermute | solution.py:307
  43.3 21.7 %copy-start.1 = (bf16[256,64]{1,0:T(8,128)(2,1)S(1)}, bf16[256,64]{1,0:T(8,128)(2,1)}, u32[]{:S(2)}) copy-start(bf16[256,64]{1,0:T(8,128)(2,1)} %constant.88.clone.refs_15_) | copy-start | bytes 98308
  43.3 21.6 %copy-start.2 = (bf16[256,64]{1,0:T(8,128)(2,1)S(1)}, bf16[256,64]{1,0:T(8,128)(2,1)}, u32[]{:S(2)}) copy-start(bf16[256,64]{1,0:T(8,128)(2,1)} %constant.87.clone.refs_10_) | copy-start | bytes 98308
  43.3 21.6 %copy-start.3 = (bf16[256,64]{1,0:T(8,128)(2,1)S(1)}, bf16[256,64]{1,0:T(8,128)(2,1)}, u32[]{:S(2)}) copy-start(bf16[256,64]{1,0:T(8,128)(2,1)} %constant.86.clone.refs_9_) | copy-start | bytes 98308
  43.3 21.6 %copy-start.4 = (bf16[64,16]{1,0:T(8,128)(2,1)S(1)}, bf16[64,16]{1,0:T(8,128)(2,1)}, u32[]{:S(2)}) copy-start(bf16[64,16]{1,0:T(8,128)(2,1)} %constant.89.clone.refs_16_) | copy-start | bytes 6148
  43.3 21.6 %copy-start.5 = (bf16[64,48]{1,0:T(8,128)(2,1)S(1)}, bf16[64,48]{1,0:T(8,128)(2,1)}, u32[]{:S(2)}) copy-start(bf16[64,48]{1,0:T(8,128)(2,1)} %constant.81.clone.refs_12_) | copy-start | bytes 18436
  43.4 21.6 %copy-start.6 = (bf16[64,48]{1,0:T(8,128)(2,1)S(1)}, bf16[64,48]{1,0:T(8,128)(2,1)}, u32[]{:S(2)}) copy-start(bf16[64,48]{1,0:T(8,128)(2,1)} %constant.80.clone.refs_11_) | copy-start | bytes 18436
  43.4 21.6 %copy-start.7 = (bf16[16,48]{1,0:T(8,128)(2,1)S(1)}, bf16[16,48]{1,0:T(8,128)(2,1)}, u32[]{:S(2)}) copy-start(bf16[16,48]{1,0:T(8,128)(2,1)} %constant.83.clone.refs_14_) | copy-start | bytes 4612
  43.4 21.6 %copy-start.8 = (bf16[16,48]{1,0:T(8,128)(2,1)S(1)}, bf16[16,48]{1,0:T(8,128)(2,1)}, u32[]{:S(2)}) copy-start(bf16[16,48]{1,0:T(8,128)(2,1)} %constant.82.clone.refs_13_) | copy-start | bytes 4612
  46.5 18.4 %collective-permute-start.8 = (f32[4,32,512]{2,1,0:T(8,128)S(1)}, f32[4,32,512]{2,1,0:T(8,128)S(1)}, u32[]{:S(2)}, u32[]{:S(2)}) collective-permute-start(f32[4,32,512]{2,1,0:T(8,128)S(1)} %get-tuple-element.39), channel_id=1, source_target_pairs={{0,8},{8,16},{16,24},{24,32},{32,40},{40,48},{48,56},{56,64},{64,7... | collective-permute-start | bytes 786440 | tf_op jit(solution)/shard_map/ppermute | solution.py:307
  46.6 18.3 %collective-permute-start.9 = (f32[4,32,512]{2,1,0:T(8,128)S(1)}, f32[4,32,512]{2,1,0:T(8,128)S(1)}, u32[]{:S(2)}, u32[]{:S(2)}) collective-permute-start(f32[4,32,512]{2,1,0:T(8,128)S(1)} %get-tuple-element.40), channel_id=1, source_target_pairs={{0,248},{8,0},{16,8},{24,16},{32,24},{40,32},{48,40},{56,48},{64,5... | collective-permute-start | bytes 786440 | tf_op jit(solution)/shard_map/ppermute | solution.py:307
  52.0 7.5 %collective-permute-start.10 = (f32[4,8,256]{2,1,0:T(8,128)S(1)}, f32[4,8,256]{2,1,0:T(8,128)S(1)}, u32[]{:S(2)}, u32[]{:S(2)}) collective-permute-start(f32[4,8,256]{2,1,0:T(8,128)S(1)} %get-tuple-element.41), channel_id=1, source_target_pairs={{0,16},{8,24},{16,32},{24,40},{32,48},{40,56},{48,64},{56,72},{64,... | collective-permute-start | bytes 98312 | tf_op jit(solution)/shard_map/ppermute | solution.py:307
  59.5 5.4 %collective-permute-start.11 = (f32[4,8,256]{2,1,0:T(8,128)S(1)}, f32[4,8,256]{2,1,0:T(8,128)S(1)}, u32[]{:S(2)}, u32[]{:S(2)}) collective-permute-start(f32[4,8,256]{2,1,0:T(8,128)S(1)} %get-tuple-element.42), channel_id=1, source_target_pairs={{0,240},{8,248},{16,0},{24,8},{32,16},{40,24},{48,32},{56,40},{64,... | collective-permute-start | bytes 98312 | tf_op jit(solution)/shard_map/ppermute | solution.py:307
  (22 other events, 165.9 us)
where the time goes:
time: 70.4 us; the launch traced here: 70.2 us
  Pallas kernels  30.3 us (43%)
  starting transfers between devices  21.2 us (30%)
  waiting for transfers between devices  13 us (18%)
  local copies, waits for them, and re-layouts  5.26 us (7%)
    pallas_call x5, Pallas kernels, call(): pl.pallas_call(body, grid=(count,), in_specs=[cut(a.shape) for a in ins]...  26.5 us
    ppermute x12, starting transfers between devices, move(): lax.ppermute(value, axis, [(i, (i + step) % count) for i in range(count)])  21.2 us
    ppermute x12, waiting for transfers between devices, move(): lax.ppermute(value, axis, [(i, (i + step) % count) for i in range(count)])  13 us
    unnamed x68, local copies, waits for them, and re-layouts  5.26 us
    pallas_call x1, Pallas kernels, local(): pl.pallas_call(lambda *refs: send_y_kernel(send0, *refs), grid=(comps,),...  3.81 us
  transfers between devices with their start and end apart: 12, of which 2 were waited for; matrix products, arithmetic and copies ran while one was open for 0% of the time, Pallas kernels for 30%

commit v1 on v0

v1 whole, which is shorter than its diff:
```python
import jax
import jax.numpy as jnp
import ml_dtypes
import numpy as np
from jax import lax
from jax.experimental import pallas as pl
from jax.experimental.pallas import tpu as pltpu
from jax.sharding import PartitionSpec as P

ALPHA = -1.586134342059924
BETA = -0.052980118572961
GAMMA = 0.882911075530934
DELTA = 0.443506852043971
KAPPA = 1.149604398860241

F32 = jnp.float32
BF16 = jnp.bfloat16
VMEM_LIMIT = 32 * 1024 * 1024
ROWS = 16


def pair_matrix(length):
    cells = np.eye(length)
    even, odd = cells[0::2].copy(), cells[1::2].copy()
    odd = odd + ALPHA * (even + np.roll(even, -1, 0))
    even = even + BETA * (odd + np.roll(odd, 1, 0))
    odd = odd + GAMMA * (even + np.roll(even, -1, 0))
    even = even + DELTA * (odd + np.roll(odd, 1, 0))
    return even * KAPPA, odd / KAPPA


def alternated(length):
    low, high = pair_matrix(length)
    table = np.zeros((length, length))
    table[0::2], table[1::2] = low, high
    return table


def chain_blocks():
    count = 8
    length = count * ROWS
    first = alternated(length)
    second = alternated(length // 2) @ first[0::2]
    third = alternated(length // 4) @ second[0::2]
    result = []
    for table, per in ((first, 16), (second, 8), (third, 4)):
        here = table[4 * per : 5 * per]
        result.append({k: here[:, (4 + k) * ROWS : (5 + k) * ROWS] for k in (-2, -1, 0, 1, 2)})
    return result


def factor(block, rank):
    left, size, right = np.linalg.svd(block, full_matrices=False)
    assert np.all(size[rank:] < 1e-12)
    return left[:, :rank] * size[:rank], right[:rank]


def split_const(table):
    table = np.asarray(table, np.float64)
    high = table.astype(ml_dtypes.bfloat16)
    low = (table - high.astype(np.float64)).astype(ml_dtypes.bfloat16)
    return high, low


def stack(*parts):
    return np.concatenate(parts, 0)


def tables(nx):
    first, second, third = chain_blocks()
    eye = np.eye
    sides = (-1, 1)
    out = {}
    give1, send1, give2a, give2b, send2 = {}, {}, {}, {}, {}
    give2, send2d, give22, send22 = {}, {}, {}, {}
    for s in sides:
        give1[s], send1[s] = factor(second[s], 3)
        give2a[s] = third[s] @ send1[s].T
        give2b[s], send2[s] = factor(third[s] - give2a[s] @ send1[s], 2)
        give2[s], send2d[s] = factor(third[s], 4)
        give22[s], send22[s] = factor(third[2 * s], 2)

    low, high = pair_matrix(nx)
    out["tx"] = np.concatenate([low[128:256, 256:512], high[128:256, 256:512]], 0).T
    blocks = nx // 256
    rims = np.zeros((8 * blocks, nx))
    for j in range(blocks):
        block = np.concatenate([low[128 * j : 128 * j + 128], high[128 * j : 128 * j + 128]], 0).T
        after = (j + 1) % blocks
        rims[8 * j : 8 * j + 4, 256 * j : 256 * j + 256] = block[(256 * j - np.arange(4, 0, -1)) % nx]
        rims[8 * after + 4 : 8 * after + 8, 256 * j : 256 * j + 256] = block[256 * after : 256 * after + 4]
    low, high = pair_matrix(nx // 2)
    tx1 = np.concatenate([low, high], 0).T
    low, high = pair_matrix(nx // 4)
    tx2 = np.concatenate([low, high], 0).T
    out["tx1"] = tx1
    out["tx12"] = tx1[:, : nx // 4] @ tx2

    def planes(send):
        return np.einsum("pz,ab->paBz".replace("B", "b"), send, eye(ROWS)).reshape(-1, ROWS * ROWS)

    out["zsend"] = stack(*[planes(send1[s]) for s in sides], *[planes(send2[s]) for s in sides])
    out["zown"] = stack(
        np.kron(eye(ROWS), second[0]), np.kron(eye(ROWS), third[0]), *[planes(send22[s]) for s in sides]
    )

    def back(give):
        return np.einsum("zp,ab->azpb", give, eye(ROWS)).reshape(ROWS * give.shape[0], -1)

    zgive1 = np.concatenate([back(give1[s]) for s in sides], 1)
    zgive2a = np.concatenate([back(give2a[s]) for s in sides], 1)
    zgive2b = np.concatenate([back(give2b[s]) for s in sides] + [back(give22[s]) for s in sides], 1)
    out["ychain1"] = stack(np.kron(second[0], eye(8)), *[np.kron(send1[s], eye(8)) for s in sides])
    out["ychain2"] = stack(
        np.kron(third[0], eye(4)),
        *[np.kron(send2d[s], eye(4)) for s in sides],
        *[np.kron(send22[s], eye(4)) for s in sides],
    )
    out["chain1"] = stack(out["ychain1"] @ zgive1, out["ychain2"] @ zgive2a)
    out["chain2"] = out["ychain2"] @ zgive2b
    out["ygive1"] = np.concatenate([np.kron(give1[s], eye(8)) for s in sides], 1)
    out["ygive2"] = np.concatenate(
        [np.kron(give2[s], eye(4)) for s in sides] + [np.kron(give22[s], eye(4)) for s in sides], 1
    )
    pairs = {name: split_const(table) for name, table in out.items()}
    high, low = split_const(rims)
    pairs["rims"] = (np.concatenate([high, high, low, np.zeros_like(high)], 0),)
    return pairs


def split(value):
    high = value.astype(BF16)
    low = (value - high.astype(F32)).astype(BF16)
    return high, low


def dot(a, b):
    return jnp.dot(a, b, preferred_element_type=F32)


def left(table, rows):
    return dot(table[0], rows[0]) + (dot(table[0], rows[1]) + dot(table[1], rows[0]))


def right(rows, table):
    return dot(rows[0], table[0]) + (dot(rows[0], table[1]) + dot(rows[1], table[0]))


def both(high_ref, low_ref):
    return high_ref[...], low_ref[...]


def lift_line(cells, before, after):
    even, odd = list(cells[0::2]), list(cells[1::2])
    count = len(even)
    even.append(after[0])
    odd = [odd[n] + ALPHA * (even[n] + even[n + 1]) for n in range(count)]
    odd_before = before[0] + ALPHA * even[0]
    even_before = before[1] + BETA * odd_before
    odd_around = [odd_before] + odd + [after[1]]
    even = [even[n] + BETA * (odd_around[n + 1] + odd_around[n]) for n in range(count + 1)]
    odd = [odd[n] + GAMMA * (even[n] + even[n + 1]) for n in range(count)]
    odd_around = [odd_before + GAMMA * (even_before + even[0])] + odd
    even = [even[n] + DELTA * (odd_around[n + 1] + odd_around[n]) for n in range(count)]
    result = []
    for n in range(count):
        result += [even[n] * KAPPA, odd[n] * (1.0 / KAPPA)]
    return result


def give_right(cells):
    a, b, c, d = cells
    return d + ALPHA * c, c + BETA * (b + ALPHA * (a + c))


def give_left(cells):
    a, b, c = cells
    return a, b + ALPHA * (a + c)


def lift_x(cells, table, rims_ref, store):
    count, nx = cells.shape
    lane = lax.broadcasted_iota(jnp.int32, (count, 128), 1)
    rims = None
    for j in range(nx // 256):
        at = 256 * j
        before = cells[:, nx - 128 :] if j == 0 else cells[:, at - 128 : at]
        rim = jnp.where(lane >= 124, before, jnp.where(lane < 4, cells[:, at : at + 128], 0.0))
        rim = pltpu.roll(rim, 4 + 8 * j, 1)
        rims = rim if rims is None else rims + rim
    width = nx // 32
    high = rims.astype(BF16).astype(F32)
    rims = (high + pltpu.roll(rims - high, width, 1) + pltpu.roll(high, 2 * width, 1)).astype(BF16)
    parts = split(cells)
    for j in range(nx // 256):
        lanes = slice(256 * j, 256 * j + 256)
        store(j, right([part[:, lanes] for part in parts], table) + dot(rims, rims_ref[:, lanes]))


def edge_kernel(x_ref, to_right_ref, to_left_ref, rows_ref, sems):
    comps = x_ref.shape[0]
    copies = []
    for c in range(comps):
        copies.append(pltpu.make_async_copy(x_ref.at[c, pl.ds(0, 3)], rows_ref.at[c, pl.ds(0, 3)], sems.at[c, 0]))
        copies.append(pltpu.make_async_copy(x_ref.at[c, pl.ds(12, 4)], rows_ref.at[c, pl.ds(3, 4)], sems.at[c, 1]))
    for copy in copies:
        copy.start()
    for c in range(comps):
        copies[2 * c].wait()
        to_left_ref[c, 0], to_left_ref[c, 1] = give_left([rows_ref[c, k] for k in range(3)])
        copies[2 * c + 1].wait()
        to_right_ref[c, 0], to_right_ref[c, 1] = give_right([rows_ref[c, k] for k in range(3, 7)])


def lift_kernel(
    x_ref, txh, txl, rims, zsh, zsl, t12h, t12l,
    u_ref, high_ref, low_ref, r1_ref, l1_ref, cells_ref, far_ref, sems,
):
    comps, _, nx = x_ref.shape
    blocks, quarter = nx // 256, nx // 4

    def copy(c):
        return pltpu.make_async_copy(x_ref.at[c], cells_ref.at[c], sems.at[c])

    copy(0).start()
    copy(1).start()

    def step(c, _):
        copy(c).wait()

        @pl.when(c + 2 < comps)
        def _():
            copy(c + 2).start()

        def store(j, value):
            u_ref[c, j] = value[:, :128]
            u_ref[c, blocks + j] = value[:, 128:]
            high, low = split(value[:, :128])
            high_ref[c, :, 128 * j : 128 * j + 128] = high
            low_ref[c, :, 128 * j : 128 * j + 128] = low

        lift_x(cells_ref[c], both(txh, txl), rims, store)
        rows = left(both(zsh, zsl), (high_ref[c], low_ref[c]))
        r1_ref[c, :48] = rows[:48]
        l1_ref[c, :48] = rows[48:96]
        far_ref[c] = rows[96:]
        return 0

    lax.fori_loop(0, comps, step, 0)
    far = right(split(far_ref[...].reshape(64 * comps, nx // 2)), both(t12h, t12l))
    for c in range(comps):
        for k, ref in enumerate((r1_ref, l1_ref)):
            for p in range(2):
                at = 64 * c + 32 * k + 16 * p
                ref[c, 48:, quarter * p : quarter * p + quarter] = far[at : at + 16]


def own_kernel(
    high_ref, low_ref, zoh, zol, t12h, t12l, c1h, c1l, c2h, c2l, first_ref, second_ref, r2_ref, l2_ref, far_ref
):
    comps, _, half = high_ref.shape
    quarter = half // 2

    def step(c, _):
        rows = left(both(zoh, zol), (high_ref[c], low_ref[c]))
        first_ref[c] = left(both(c1h, c1l), split(rows[:128]))
        far_ref[c] = rows[128:]
        return 0

    lax.fori_loop(0, comps, step, 0)
    far = right(split(far_ref[...].reshape(128 * comps, half)), both(t12h, t12l))
    for c in range(comps):
        second_ref[c] = left(both(c2h, c2l), split(far[128 * c : 128 * c + 64]))
        for k, ref in enumerate((r2_ref, l2_ref)):
            for p in range(2):
                at = 128 * c + 64 + 32 * k + 16 * p
                ref[c, :, quarter * p : quarter * p + quarter] = far[at : at + 16]


def chain_kernel(
    first_ref, second_ref, l1_ref, r1_ref, l2_ref, r2_ref,
    g1h, g1l, g2h, g2l, t12h, t12l,
    o1_ref, o2_ref, to_r_ref, to_l_ref, to_r2_ref, to_l2_ref, far_ref,
):
    comps, _, half = first_ref.shape
    quarter = half // 2

    def step(c, _):
        near = split(jnp.concatenate([l1_ref[c, :48], r1_ref[c, :48]], 0))
        rows = left(both(g1h, g1l), near)
        far_ref[c] = rows[112:]
        first = first_ref[c] + rows[:112]
        o1_ref[c] = first[:64]
        to_r_ref[c, :24] = first[64:88]
        to_l_ref[c, :24] = first[88:]
        return 0

    lax.fori_loop(0, comps, step, 0)
    far = right(split(far_ref[...].reshape(64 * comps, half)), both(t12h, t12l))
    for c in range(comps):
        deep = []
        for ref in (l1_ref, r1_ref):
            deep += [ref[c, 48:, :quarter], ref[c, 48:, quarter:]]
        for ref in (l2_ref, r2_ref):
            deep += [ref[c, :, :quarter], ref[c, :, quarter:]]
        second = left(both(g2h, g2l), split(jnp.concatenate(deep, 0)))
        second = second_ref[c] + (far[64 * c : 64 * c + 64] + second)
        o2_ref[c] = second[:16]
        for k, (ref, ref2) in enumerate(((to_r_ref, to_r2_ref), (to_l_ref, to_l2_ref))):
            ref[c, 24:, :quarter] = second[16 + 16 * k : 24 + 16 * k]
            ref[c, 24:, quarter:] = second[24 + 16 * k : 32 + 16 * k]
            ref2[c] = second[48 + 8 * k : 56 + 8 * k]


def along_y_kernel(u_ref, l_ref, r_ref, txh, txl, rims, b_ref, to_r_ref, to_l_ref, halo_ref):
    comps, lanes = u_ref.shape[:2]
    blocks = lanes // 2

    def store(j, value):
        halo_ref[j] = value[:, :128]
        halo_ref[blocks + j] = value[:, 128:]

    rows = [ref[c, p] for c in range(comps) for ref in (l_ref, r_ref) for p in range(2)]
    lift_x(jnp.concatenate(rows, 0), both(txh, txl), rims, store)

    def step(n, _):
        c, k = n // lanes, n % lanes
        u, b, halo = u_ref.at[c, k], b_ref.at[c, k], halo_ref.at[k]
        for part in range(2):
            cells = [u[16 * y + 8 * part : 16 * y + 8 * part + 8] for y in range(ROWS)]
            around = [halo[pl.ds(pl.multiple_of(64 * c + 16 * p + 8 * part, 8), 8)] for p in range(4)]
            for y, value in enumerate(lift_line(cells, around[:2], around[2:])):
                b[pl.ds(128 * part + y, 8, stride=ROWS)] = value

        def plane(z):
            return b[16 * z : 16 * z + 16]

        to_r_ref[c, k, 0], to_r_ref[c, k, 1] = give_right([plane(z) for z in range(12, 16)])
        to_l_ref[c, k, 0], to_l_ref[c, k, 1] = give_left([plane(z) for z in range(3)])
        return 0

    lax.fori_loop(0, comps * lanes, step, 0)


def along_z_kernel(b_ref, l_ref, r_ref, out_ref, even_ref, done_ref, sems):
    comps, lanes = b_ref.shape[:2]

    def copy(c, k):
        return pltpu.make_async_copy(
            done_ref.at[c, k], out_ref.at[c, :, pl.ds(pl.multiple_of(128 * k, 128), 128)], sems.at[c]
        )

    def step(n, _):
        c, k = n // lanes, n % lanes
        b, done = b_ref.at[c, k], done_ref.at[c, k]
        for part in range(2):
            cells = [b[16 * z + 8 * part : 16 * z + 8 * part + 8] for z in range(ROWS)]
            around = [ref[c, k, p, 8 * part : 8 * part + 8] for ref in (l_ref, r_ref) for p in range(2)]
            for z, value in enumerate(lift_line(cells, around[:2], around[2:])):
                done[pl.ds(128 * part + z, 8, stride=ROWS)] = value
        copy(c, k).start()

        @pl.when(k < lanes // 2)
        def _():
            for y in range(ROWS // 2):
                even_ref[c, k, 16 * y : 16 * y + 16] = done[32 * y : 32 * y + 16]

        return 0

    lax.fori_loop(0, comps * lanes, step, 0)
    for c in range(comps):
        for k in range(lanes):
            copy(c, k).wait()


def last_kernel(
    _, even_ref, o1_ref, o2_ref, l1_ref, r1_ref, l2_ref, r2_ref,
    g1h, g1l, g2h, g2l, t1h, t1l, out_ref, done_ref, sems,
):
    comps, lanes = even_ref.shape[:2]
    half = 128 * lanes
    quarter = half // 2
    window, deepest = [], []
    for c in range(comps):
        near = split(jnp.concatenate([l1_ref[c, :24], r1_ref[c, :24]], 0))
        window.append(o1_ref[c] + left(both(g1h, g1l), near))
        deep = []
        for ref in (l1_ref, r1_ref):
            deep += [ref[c, 24:, :quarter], ref[c, 24:, quarter:]]
        deep += [l2_ref[c], r2_ref[c]]
        deepest.append(o2_ref[c] + left(both(g2h, g2l), split(jnp.concatenate(deep, 0))))
    window = right(split(jnp.concatenate(window, 0)), both(t1h, t1l))
    copies = []
    for c in range(comps):
        for k in range(lanes):
            at = slice(128 * k, 128 * k + 128)
            done = done_ref.at[c, k]
            done[...] = even_ref[c, k]
            for y in range(8):
                done[pl.ds(16 * y, 8, stride=2)] = window[64 * c + 8 * y : 64 * c + 8 * y + 8, at]
            if 128 * k < quarter:
                for y in range(4):
                    done[pl.ds(32 * y, 4, stride=4)] = deepest[c][4 * y : 4 * y + 4, at]
            for y in range(8):
                copies.append(
                    pltpu.make_async_copy(done.at[pl.ds(16 * y, 16)], out_ref.at[c, pl.ds(32 * y, 16), at], sems.at[c])
                )
                copies[-1].start()
    for copy in copies:
        copy.wait()


def call(body, ins, outs, scratch=(), flops=0, hbm_in=(), hbm_out=(), aliases=None):
    def spec(n, hbm):
        return pl.BlockSpec(memory_space=pltpu.HBM if n in hbm else pltpu.VMEM)

    moved = sum(a.size * a.dtype.itemsize for a in ins)
    moved += sum(int(np.prod(s)) * jnp.dtype(d).itemsize for s, d in outs)
    return pl.pallas_call(
        body,
        in_specs=[spec(n, hbm_in) for n in range(len(ins))],
        out_specs=[spec(n, hbm_out) for n in range(len(outs))],
        out_shape=[jax.ShapeDtypeStruct(s, d) for s, d in outs],
        scratch_shapes=list(scratch),
        input_output_aliases=aliases or {},
        compiler_params=pltpu.CompilerParams(vmem_limit_bytes=VMEM_LIMIT),
        cost_estimate=pl.CostEstimate(flops=flops, bytes_accessed=moved, transcendentals=0),
    )(*ins)


def move(value, axis, step):
    count = lax.axis_size(axis)
    return lax.ppermute(value, axis, [(i, (i + step) % count) for i in range(count)])


def local(flow_field):
    comps, ny, nz, nx = flow_field.shape
    assert ny == ROWS and nz == ROWS and nx % 1024 == 0
    assert lax.axis_size("gy") >= 5 and lax.axis_size("gz") >= 5
    half, quarter, lanes = nx // 2, nx // 4, nx // 128
    pairs = {k: [jnp.asarray(p) for p in v] for k, v in tables(nx).items()}
    field = pltpu.with_memory_space_constraint(flow_field, pltpu.HBM)
    flat = pltpu.with_memory_space_constraint(flow_field.reshape(comps, ROWS * ROWS, nx), pltpu.HBM)

    def consts(*names):
        return [p for n in names for p in pairs[n]]

    def dma(*shape):
        return pltpu.SemaphoreType.DMA(shape)

    edge = ((comps, 2, ROWS, nx), F32)
    y_right, y_left = call(
        edge_kernel,
        [field],
        [edge] * 2,
        [pltpu.VMEM((comps, 7, ROWS, nx), F32), dma(comps, 2)],
        hbm_in=(0,),
    )
    from_left0 = move(y_right, "gy", 1)
    from_right0 = move(y_left, "gy", -1)

    near = ((comps, 64, half), F32)
    far = ((comps, 16, half), F32)
    cells = ((comps, lanes, ROWS * ROWS, 128), F32)
    u, high, low, z_right, z_left = call(
        lift_kernel,
        [flat] + consts("tx", "rims", "zsend", "tx12"),
        [cells] + [((comps, ROWS * ROWS, half), BF16)] * 2 + [near] * 2,
        [pltpu.VMEM((comps, ROWS * ROWS, nx), F32), pltpu.VMEM((comps, 64, half), F32), dma(comps)],
        flops=1 << 33,
        hbm_in=(0,),
    )
    z_from_left = move(z_right, "gz", 1)
    z_from_right = move(z_left, "gz", -1)

    first, second, z_right2, z_left2 = call(
        own_kernel,
        [high, low] + consts("zown", "tx12", "ychain1", "ychain2"),
        [((comps, 112, half), F32), ((comps, 64, quarter), F32)] + [far] * 2,
        [pltpu.VMEM((comps, 128, half), F32)],
        flops=1 << 32,
    )
    z_from_left2 = move(z_right2, "gz", 2)
    z_from_right2 = move(z_left2, "gz", -2)

    planes = ((comps, lanes, 2, ROWS, 128), F32)
    b, z0_right, z0_left = call(
        along_y_kernel,
        [u, from_left0, from_right0] + consts("tx", "rims"),
        [cells] + [planes] * 2,
        [pltpu.VMEM((lanes, 64 * comps, 128), F32)],
        flops=1 << 32,
    )
    z0_from_left = move(z0_right, "gz", 1)
    z0_from_right = move(z0_left, "gz", -1)

    o1, o2, y1_right, y1_left, y2_right, y2_left = call(
        chain_kernel,
        [first, second, z_from_left, z_from_right, z_from_left2, z_from_right2] + consts("chain1", "chain2", "tx12"),
        [((comps, 64, half), F32), ((comps, 16, quarter), F32)]
        + [((comps, 32, half), F32)] * 2
        + [((comps, 8, quarter), F32)] * 2,
        [pltpu.VMEM((comps, 64, half), F32)],
        flops=1 << 31,
    )
    y_from_left2 = move(y2_right, "gy", 2)
    y_from_left = move(y1_right, "gy", 1)
    y_from_right = move(y1_left, "gy", -1)
    y_from_right2 = move(y2_left, "gy", -2)

    whole = ((comps, ROWS * ROWS, nx), F32)
    result, even = call(
        along_z_kernel,
        [b, z0_from_left, z0_from_right],
        [whole, ((comps, lanes // 2, ROWS * ROWS // 2, 128), F32)],
        [pltpu.VMEM((comps, lanes, ROWS * ROWS, 128), F32), dma(comps)],
        flops=1 << 32,
        hbm_out=(0,),
    )
    (result,) = call(
        last_kernel,
        [result, even, o1, o2, y_from_left, y_from_right, y_from_left2, y_from_right2]
        + consts("ygive1", "ygive2", "tx1"),
        [whole],
        [pltpu.VMEM((comps, lanes // 2, ROWS * ROWS // 2, 128), F32), dma(comps)],
        flops=1 << 30,
        hbm_in=(0,),
        hbm_out=(0,),
        aliases={0: 0},
    )
    return result.reshape(flow_field.shape)


def solution(mesh):
    placed = P(None, "gy", "gz", None)
    return jax.shard_map(local, mesh=mesh, in_specs=(placed,), out_specs=placed, check_vma=False)
```

time: 70.4 us -> 62 us (0.88)
  the two profiles are of different devices: /device:TPU:0 before, /device:TPU:6 now
where the time goes in v1:
time: 62 us; the launch traced here: 61.9 us
  starting transfers between devices  25.6 us (41%)
  Pallas kernels  20.7 us (33%)
  waiting for transfers between devices  15.1 us (24%)
    ppermute x12, starting transfers between devices, move(): lax.ppermute(value, axis, [(i, (i + step) % count) for i in range(count)])  25.6 us
    pallas_call x7, Pallas kernels, call(): pl.pallas_call(body, in_specs=[spec(n, hbm_in) for n in range(len(ins))],...  20.7 us
    ppermute x12, waiting for transfers between devices, move(): lax.ppermute(value, axis, [(i, (i + step) % count) for i in range(count)])  15.1 us
  transfers between devices with their start and end apart: 12, of which 3 were waited for; matrix products, arithmetic and copies ran while one was open for 0% of the time, Pallas kernels for 28%

profile of v1, /device:TPU:6, one launch (start us, length us, event | category | flops | bytes accessed | tf_op | source)
XLA Modules:
  0.0 61.9 jit_solution(902155862260511954)
XLA Ops:
  0.0 0.0 copy-start.7
  0.0 0.0 copy-start.13
  0.0 0.0 copy-start.14
  0.1 1.7 %shard_map.227 = (f32[4,2,16,1024]{3,2,1,0:T(8,128)S(1)}, f32[4,2,16,1024]{3,2,1,0:T(8,128)S(1)}) custom-call(f32[4,16,16,1024]{3,2,1,0:T(8,128)} %x_ref.1), custom_call_target="tpu_custom_call" | custom-call | bytes 5242880 | tf_op jit(solution)/shard_map/pallas_call | solution.py:419
  1.7 1.7 %collective-permute-start = (f32[4,2,16,1024]{3,2,1,0:T(8,128)S(1)}, f32[4,2,16,1024]{3,2,1,0:T(8,128)S(1)}, u32[]{:S(2)}, u32[]{:S(2)}) collective-permute-start(f32[4,2,16,1024]{3,2,1,0:T(8,128)S(1)} %get-tuple-element.28), channel_id=1, source_target_pairs={{0,8},{8,16},{16,24},{24,32},{32,40},{40,48},{48,56},{56,64},{64,7... | collective-permute-start | bytes 1572872 | tf_op jit(solution)/shard_map/ppermute | solution.py:433
  3.4 6.8 %collective-permute-start.1 = (f32[4,2,16,1024]{3,2,1,0:T(8,128)S(1)}, f32[4,2,16,1024]{3,2,1,0:T(8,128)S(1)}, u32[]{:S(2)}, u32[]{:S(2)}) collective-permute-start(f32[4,2,16,1024]{3,2,1,0:T(8,128)S(1)} %get-tuple-element.29), channel_id=1, source_target_pairs={{0,248},{8,0},{16,8},{24,16},{32,24},{40,32},{48,40},{56,48},{64,5... | collective-permute-start | bytes 1572872 | tf_op jit(solution)/shard_map/ppermute | solution.py:433
  10.3 5.6 %shard_map.226 = (f32[4,8,256,128]{3,2,1,0:T(8,128)S(1)}, bf16[4,256,512]{2,1,0:T(8,128)(2,1)S(1)}, bf16[4,256,512]{2,1,0:T(8,128)(2,1)S(1)}, f32[4,64,512]{2,1,0:T(8,128)S(1)}, f32[4,64,512]{2,1,0:T(8,128)S(1)}) custom-call(f32[4,256,1024]{2,1,0:T(8,128)} %bitcast.2, bf16[256,256]{1,0:T(8,128)(2,1)S(1)} %copy-done.11, bf16[256,256]{1,0:T(8,128)(2,1)S(1)} %copy-done.12, ...), custom_call_target="tpu_custom_call" | custom-call | flops 8589934592 | bytes 12746752 | tf_op jit(solution)/shard_map/pallas_call | solution.py:419
  15.9 0.0 collective-permute-start.4
  15.9 1.7 %collective-permute-start.5 = (f32[4,64,512]{2,1,0:T(8,128)S(1)}, f32[4,64,512]{2,1,0:T(8,128)S(1)}, u32[]{:S(2)}, u32[]{:S(2)}) collective-permute-start(f32[4,64,512]{2,1,0:T(8,128)S(1)} %get-tuple-element.40), channel_id=1, source_target_pairs={{0,7},{1,0},{2,1},{3,2},{4,3},{5,4},{6,5},{7,6},{8,15},{9,8},{10,9... | collective-permute-start | bytes 1572872 | tf_op jit(solution)/shard_map/ppermute | solution.py:433
  17.6 4.4 %collective-permute-done.l_ref = f32[4,2,16,1024]{3,2,1,0:T(8,128)S(1)} collective-permute-done((f32[4,2,16,1024]{3,2,1,0:T(8,128)S(1)}, f32[4,2,16,1024]{3,2,1,0:T(8,128)S(1)}, u32[]{:S(2)}, u32[]{:S(2)}) %collective-permute-start) | collective-permute-done | bytes 524320 | tf_op jit(solution)/shard_map/ppermute | solution.py:433
  22.1 3.4 %shard_map.228 = (f32[4,8,256,128]{3,2,1,0:T(8,128)S(1)}, f32[4,8,2,16,128]{4,3,2,1,0:T(8,128)S(1)}, f32[4,8,2,16,128]{4,3,2,1,0:T(8,128)S(1)}) custom-call(f32[4,8,256,128]{3,2,1,0:T(8,128)S(1)} %get-tuple-element.27.u_ref, f32[4,2,16,1024]{3,2,1,0:T(8,128)S(1)} %collective-permute-done.l_ref, f32[4,2,16,1024]{3,2,1,0:T(8,128)S(1)} %collective-permute-done.1.r_ref, ...), custom_call_target="tpu_custom_call" | custom-call | flops 4294967296 | bytes 11010048 | tf_op jit(solution)/shard_map/pallas_call | solution.py:419
  25.5 0.0 collective-permute-start.2
  25.6 1.7 %collective-permute-start.3 = (f32[4,8,2,16,128]{4,3,2,1,0:T(8,128)S(1)}, f32[4,8,2,16,128]{4,3,2,1,0:T(8,128)S(1)}, u32[]{:S(2)}, u32[]{:S(2)}) collective-permute-start(f32[4,8,2,16,128]{4,3,2,1,0:T(8,128)S(1)} %get-tuple-element.32), channel_id=1, source_target_pairs={{0,7},{1,0},{2,1},{3,2},{4,3},{5,4},{6,5},{7,6},{8,15},{9,8},{10,9... | collective-permute-start | bytes 1572872 | tf_op jit(solution)/shard_map/ppermute | solution.py:433
  27.4 3.1 %shard_map.230 = (f32[4,112,512]{2,1,0:T(8,128)S(1)}, f32[4,64,256]{2,1,0:T(8,128)S(1)}, f32[4,16,512]{2,1,0:T(8,128)S(1)}, f32[4,16,512]{2,1,0:T(8,128)S(1)}) custom-call(bf16[4,256,512]{2,1,0:T(8,128)(2,1)S(1)} %get-tuple-element.35.high_ref, bf16[4,256,512]{2,1,0:T(8,128)(2,1)S(1)} %get-tuple-element.36.low_ref, bf16[256,256]{1,0:T(8,128)(2,1)S(1)} %copy-done.9, ...), custom_call_target="tpu_custom_call" | custom-call | flops 4294967296 | bytes 4399104 | tf_op jit(solution)/shard_map/pallas_call | solution.py:419
  30.5 1.8 %collective-permute-start.6 = (f32[4,16,512]{2,1,0:T(8,128)S(1)}, f32[4,16,512]{2,1,0:T(8,128)S(1)}, u32[]{:S(2)}, u32[]{:S(2)}) collective-permute-start(f32[4,16,512]{2,1,0:T(8,128)S(1)} %get-tuple-element.41), channel_id=1, source_target_pairs={{0,2},{1,3},{2,4},{3,5},{4,6},{5,7},{6,0},{7,1},{8,10},{9,11},{10,... | collective-permute-start | bytes 393224 | tf_op jit(solution)/shard_map/ppermute | solution.py:433
  32.2 4.7 %collective-permute-done.6.l2_ref = f32[4,16,512]{2,1,0:T(8,128)S(1)} collective-permute-done((f32[4,16,512]{2,1,0:T(8,128)S(1)}, f32[4,16,512]{2,1,0:T(8,128)S(1)}, u32[]{:S(2)}, u32[]{:S(2)}) %collective-permute-start.6) | collective-permute-done | bytes 131104 | tf_op jit(solution)/shard_map/ppermute | solution.py:433
  37.0 0.8 %collective-permute-start.7 = (f32[4,16,512]{2,1,0:T(8,128)S(1)}, f32[4,16,512]{2,1,0:T(8,128)S(1)}, u32[]{:S(2)}, u32[]{:S(2)}) collective-permute-start(f32[4,16,512]{2,1,0:T(8,128)S(1)} %get-tuple-element.42), channel_id=1, source_target_pairs={{0,6},{1,7},{2,0},{3,1},{4,2},{5,3},{6,4},{7,5},{8,14},{9,15},{10,... | collective-permute-start | bytes 393224 | tf_op jit(solution)/shard_map/ppermute | solution.py:433
  37.8 5.9 %collective-permute-done.7.r2_ref = f32[4,16,512]{2,1,0:T(8,128)S(1)} collective-permute-done((f32[4,16,512]{2,1,0:T(8,128)S(1)}, f32[4,16,512]{2,1,0:T(8,128)S(1)}, u32[]{:S(2)}, u32[]{:S(2)}) %collective-permute-start.7) | collective-permute-done | bytes 131104 | tf_op jit(solution)/shard_map/ppermute | solution.py:433
  43.7 1.6 %shard_map.231 = (f32[4,64,512]{2,1,0:T(8,128)S(1)}, f32[4,16,256]{2,1,0:T(8,128)S(1)}, f32[4,32,512]{2,1,0:T(8,128)S(1)}, f32[4,32,512]{2,1,0:T(8,128)S(1)}, f3...) custom-call(f32[4,112,512]{2,1,0:T(8,128)S(1)} %get-tuple-element.37.first_ref, ...), custom_call_target="tpu_custom_call" | custom-call | flops 2147483648 | bytes 4294656 | tf_op jit(solution)/shard_map/pallas_call | solution.py:419
  45.4 0.1 collective-permute-start.8
  45.4 5.3 %collective-permute-start.9 = (f32[4,32,512]{2,1,0:T(8,128)S(1)}, f32[4,32,512]{2,1,0:T(8,128)S(1)}, u32[]{:S(2)}, u32[]{:S(2)}) collective-permute-start(f32[4,32,512]{2,1,0:T(8,128)S(1)} %get-tuple-element.46), channel_id=1, source_target_pairs={{0,248},{8,0},{16,8},{24,16},{32,24},{40,32},{48,40},{56,48},{64,5... | collective-permute-start | bytes 786440 | tf_op jit(solution)/shard_map/ppermute | solution.py:433
  50.8 5.6 %collective-permute-start.11 = (f32[4,8,256]{2,1,0:T(8,128)S(1)}, f32[4,8,256]{2,1,0:T(8,128)S(1)}, u32[]{:S(2)}, u32[]{:S(2)}) collective-permute-start(f32[4,8,256]{2,1,0:T(8,128)S(1)} %get-tuple-element.48), channel_id=1, source_target_pairs={{0,240},{8,248},{16,0},{24,8},{32,16},{40,24},{48,32},{56,40},{64,... | collective-permute-start | bytes 98312 | tf_op jit(solution)/shard_map/ppermute | solution.py:433
  56.5 3.3 %shard_map.229 = (f32[4,256,1024]{2,1,0:T(8,128)}, f32[4,4,128,128]{3,2,1,0:T(8,128)S(1)}) custom-call(f32[4,8,256,128]{3,2,1,0:T(8,128)S(1)} %get-tuple-element.30.b_ref, f32[4,8,2,16,128]{4,3,2,1,0:T(8,128)S(1)} %collective-permute-done.2.l_ref, f32[4,8,2,16,128]{4,3,2,1,0:T(8,128)S(1)} %collective-permute-done.3.r_ref), custom_call_target="tpu_custom_call" | custom-call | flops 4294967296 | bytes 10485760 | tf_op jit(solution)/shard_map/pallas_call | solution.py:419
  59.9 2.0 %shard_map.232 = f32[4,256,1024]{2,1,0:T(8,128)} custom-call(f32[4,256,1024]{2,1,0:T(8,128)} %get-tuple-element.33._, f32[4,4,128,128]{3,2,1,0:T(8,128)S(1)} %get-tuple-element.34.even_ref, f32[4,64,512]{2,1,0:T(8,128)S(1)} %get-tuple-element.43.o1_ref, f32[4,16,256]{2,1,0:T(8,128)S(1)} %get-tuple-element.44.o2_ref, ...), custom_call_target="tpu_custom_call", output_to_operand_aliasing={{}: (0, {})} | custom-call | flops 1073741824 | bytes 11680768 | tf_op jit(solution)/shard_map/pallas_call | solution.py:419
  (53 shorter events, 0.1 us)
Async XLA Ops:
  0.0 10.2 %copy-start.11 = (bf16[256,256]{1,0:T(8,128)(2,1)S(1)}, bf16[256,256]{1,0:T(8,128)(2,1)}, u32[]{:S(2)}) copy-start(bf16[256,256]{1,0:T(8,128)(2,1)} %constant.46.clone.txh) | copy-start | bytes 393220
  0.0 10.2 %copy-start.12 = (bf16[256,256]{1,0:T(8,128)(2,1)S(1)}, bf16[256,256]{1,0:T(8,128)(2,1)}, u32[]{:S(2)}) copy-start(bf16[256,256]{1,0:T(8,128)(2,1)} %constant.47.clone.txl) | copy-start | bytes 393220
  0.0 10.2 %copy-start.6 = (bf16[512,256]{1,0:T(8,128)(2,1)S(1)}, bf16[512,256]{1,0:T(8,128)(2,1)}, u32[]{:S(2)}) copy-start(bf16[512,256]{1,0:T(8,128)(2,1)} %constant.50.clone.t12h) | copy-start | bytes 786436
  0.0 10.2 %copy-start.7 = (bf16[512,256]{1,0:T(8,128)(2,1)S(1)}, bf16[512,256]{1,0:T(8,128)(2,1)}, u32[]{:S(2)}) copy-start(bf16[512,256]{1,0:T(8,128)(2,1)} %constant.51.clone.t12l) | copy-start | bytes 786436
  0.0 10.2 %copy-start.13 = (bf16[160,256]{1,0:T(8,128)(2,1)S(1)}, bf16[160,256]{1,0:T(8,128)(2,1)}, u32[]{:S(2)}) copy-start(bf16[160,256]{1,0:T(8,128)(2,1)} %constant.52.clone.zsh) | copy-start | bytes 245764
  0.0 10.2 %copy-start.14 = (bf16[160,256]{1,0:T(8,128)(2,1)S(1)}, bf16[160,256]{1,0:T(8,128)(2,1)}, u32[]{:S(2)}) copy-start(bf16[160,256]{1,0:T(8,128)(2,1)} %constant.53.clone.zsl) | copy-start | bytes 245764
  0.0 10.2 %copy-start.8 = (bf16[128,1024]{1,0:T(8,128)(2,1)S(1)}, bf16[128,1024]{1,0:T(8,128)(2,1)}, u32[]{:S(2)}) copy-start(bf16[128,1024]{1,0:T(8,128)(2,1)} %constant.68.clone.rims) | copy-start | bytes 786436
  1.7 20.3 %collective-permute-start = (f32[4,2,16,1024]{3,2,1,0:T(8,128)S(1)}, f32[4,2,16,1024]{3,2,1,0:T(8,128)S(1)}, u32[]{:S(2)}, u32[]{:S(2)}) collective-permute-start(f32[4,2,16,1024]{3,2,1,0:T(8,128)S(1)} %get-tuple-element.28), channel_id=1, source_target_pairs={{0,8},{8,16},{16,24},{24,32},{32,40},{40,48},{48,56},{56,64},{64,7... | collective-permute-start | bytes 1572872 | tf_op jit(solution)/shard_map/ppermute | solution.py:433
  3.4 18.7 %collective-permute-start.1 = (f32[4,2,16,1024]{3,2,1,0:T(8,128)S(1)}, f32[4,2,16,1024]{3,2,1,0:T(8,128)S(1)}, u32[]{:S(2)}, u32[]{:S(2)}) collective-permute-start(f32[4,2,16,1024]{3,2,1,0:T(8,128)S(1)} %get-tuple-element.29), channel_id=1, source_target_pairs={{0,248},{8,0},{16,8},{24,16},{32,24},{40,32},{48,40},{56,48},{64,5... | collective-permute-start | bytes 1572872 | tf_op jit(solution)/shard_map/ppermute | solution.py:433
  15.9 27.8 %collective-permute-start.4 = (f32[4,64,512]{2,1,0:T(8,128)S(1)}, f32[4,64,512]{2,1,0:T(8,128)S(1)}, u32[]{:S(2)}, u32[]{:S(2)}) collective-permute-start(f32[4,64,512]{2,1,0:T(8,128)S(1)} %get-tuple-element.39), channel_id=1, source_target_pairs={{0,1},{1,2},{2,3},{3,4},{4,5},{5,6},{6,7},{7,0},{8,9},{9,10},{10,1... | collective-permute-start | bytes 1572872 | tf_op jit(solution)/shard_map/ppermute | solution.py:433
  15.9 27.8 %collective-permute-start.5 = (f32[4,64,512]{2,1,0:T(8,128)S(1)}, f32[4,64,512]{2,1,0:T(8,128)S(1)}, u32[]{:S(2)}, u32[]{:S(2)}) collective-permute-start(f32[4,64,512]{2,1,0:T(8,128)S(1)} %get-tuple-element.40), channel_id=1, source_target_pairs={{0,7},{1,0},{2,1},{3,2},{4,3},{5,4},{6,5},{7,6},{8,15},{9,8},{10,9... | collective-permute-start | bytes 1572872 | tf_op jit(solution)/shard_map/ppermute | solution.py:433
  22.1 5.2 %copy-start.17 = (bf16[112,128]{1,0:T(8,128)(2,1)S(1)}, bf16[112,128]{1,0:T(8,128)(2,1)}, u32[]{:S(2)}) copy-start(bf16[112,128]{1,0:T(8,128)(2,1)} %constant.56.clone.c1h) | copy-start | bytes 86020
  25.5 25.3 %collective-permute-start.2 = (f32[4,8,2,16,128]{4,3,2,1,0:T(8,128)S(1)}, f32[4,8,2,16,128]{4,3,2,1,0:T(8,128)S(1)}, u32[]{:S(2)}, u32[]{:S(2)}) collective-permute-start(f32[4,8,2,16,128]{4,3,2,1,0:T(8,128)S(1)} %get-tuple-element.31), channel_id=1, source_target_pairs={{0,1},{1,2},{2,3},{3,4},{4,5},{5,6},{6,7},{7,0},{8,9},{9,10},{10,1... | collective-permute-start | bytes 1572872 | tf_op jit(solution)/shard_map/ppermute | solution.py:433
  25.6 30.9 %collective-permute-start.3 = (f32[4,8,2,16,128]{4,3,2,1,0:T(8,128)S(1)}, f32[4,8,2,16,128]{4,3,2,1,0:T(8,128)S(1)}, u32[]{:S(2)}, u32[]{:S(2)}) collective-permute-start(f32[4,8,2,16,128]{4,3,2,1,0:T(8,128)S(1)} %get-tuple-element.32), channel_id=1, source_target_pairs={{0,7},{1,0},{2,1},{3,2},{4,3},{5,4},{6,5},{7,6},{8,15},{9,8},{10,9... | collective-permute-start | bytes 1572872 | tf_op jit(solution)/shard_map/ppermute | solution.py:433
  27.3 16.4 %copy-start.15 = (bf16[176,96]{1,0:T(8,128)(2,1)S(1)}, bf16[176,96]{1,0:T(8,128)(2,1)}, u32[]{:S(2)}) copy-start(bf16[176,96]{1,0:T(8,128)(2,1)} %constant.60.clone.g1h) | copy-start | bytes 101380
  27.3 16.4 %copy-start.16 = (bf16[176,96]{1,0:T(8,128)(2,1)S(1)}, bf16[176,96]{1,0:T(8,128)(2,1)}, u32[]{:S(2)}) copy-start(bf16[176,96]{1,0:T(8,128)(2,1)} %constant.61.clone.g1l) | copy-start | bytes 101380
  27.3 16.4 %copy-start.19 = (bf16[64,128]{1,0:T(8,128)(2,1)S(1)}, bf16[64,128]{1,0:T(8,128)(2,1)}, u32[]{:S(2)}) copy-start(bf16[64,128]{1,0:T(8,128)(2,1)} %constant.62.clone.g2h) | copy-start | bytes 49156
  27.4 16.3 %copy-start.20 = (bf16[64,128]{1,0:T(8,128)(2,1)S(1)}, bf16[64,128]{1,0:T(8,128)(2,1)}, u32[]{:S(2)}) copy-start(bf16[64,128]{1,0:T(8,128)(2,1)} %constant.63.clone.g2l) | copy-start | bytes 49156
  30.5 6.5 %collective-permute-start.6 = (f32[4,16,512]{2,1,0:T(8,128)S(1)}, f32[4,16,512]{2,1,0:T(8,128)S(1)}, u32[]{:S(2)}, u32[]{:S(2)}) collective-permute-start(f32[4,16,512]{2,1,0:T(8,128)S(1)} %get-tuple-element.41), channel_id=1, source_target_pairs={{0,2},{1,3},{2,4},{3,5},{4,6},{5,7},{6,0},{7,1},{8,10},{9,11},{10,... | collective-permute-start | bytes 393224 | tf_op jit(solution)/shard_map/ppermute | solution.py:433
  37.0 6.7 %collective-permute-start.7 = (f32[4,16,512]{2,1,0:T(8,128)S(1)}, f32[4,16,512]{2,1,0:T(8,128)S(1)}, u32[]{:S(2)}, u32[]{:S(2)}) collective-permute-start(f32[4,16,512]{2,1,0:T(8,128)S(1)} %get-tuple-element.42), channel_id=1, source_target_pairs={{0,6},{1,7},{2,0},{3,1},{4,2},{5,3},{6,4},{7,5},{8,14},{9,15},{10,... | collective-permute-start | bytes 393224 | tf_op jit(solution)/shard_map/ppermute | solution.py:433
  45.4 14.5 %collective-permute-start.8 = (f32[4,32,512]{2,1,0:T(8,128)S(1)}, f32[4,32,512]{2,1,0:T(8,128)S(1)}, u32[]{:S(2)}, u32[]{:S(2)}) collective-permute-start(f32[4,32,512]{2,1,0:T(8,128)S(1)} %get-tuple-element.45), channel_id=1, source_target_pairs={{0,8},{8,16},{16,24},{24,32},{32,40},{40,48},{48,56},{56,64},{64,7... | collective-permute-start | bytes 786440 | tf_op jit(solution)/shard_map/ppermute | solution.py:433
  45.4 14.4 %collective-permute-start.9 = (f32[4,32,512]{2,1,0:T(8,128)S(1)}, f32[4,32,512]{2,1,0:T(8,128)S(1)}, u32[]{:S(2)}, u32[]{:S(2)}) collective-permute-start(f32[4,32,512]{2,1,0:T(8,128)S(1)} %get-tuple-element.46), channel_id=1, source_target_pairs={{0,248},{8,0},{16,8},{24,16},{32,24},{40,32},{48,40},{56,48},{64,5... | collective-permute-start | bytes 786440 | tf_op jit(solution)/shard_map/ppermute | solution.py:433
  50.8 9.0 %collective-permute-start.10 = (f32[4,8,256]{2,1,0:T(8,128)S(1)}, f32[4,8,256]{2,1,0:T(8,128)S(1)}, u32[]{:S(2)}, u32[]{:S(2)}) collective-permute-start(f32[4,8,256]{2,1,0:T(8,128)S(1)} %get-tuple-element.47), channel_id=1, source_target_pairs={{0,16},{8,24},{16,32},{24,40},{32,48},{40,56},{48,64},{56,72},{64,... | collective-permute-start | bytes 98312 | tf_op jit(solution)/shard_map/ppermute | solution.py:433
  50.8 9.0 %collective-permute-start.11 = (f32[4,8,256]{2,1,0:T(8,128)S(1)}, f32[4,8,256]{2,1,0:T(8,128)S(1)}, u32[]{:S(2)}, u32[]{:S(2)}) collective-permute-start(f32[4,8,256]{2,1,0:T(8,128)S(1)} %get-tuple-element.48), channel_id=1, source_target_pairs={{0,240},{8,248},{16,0},{24,8},{32,16},{40,24},{48,32},{56,40},{64,... | collective-permute-start | bytes 98312 | tf_op jit(solution)/shard_map/ppermute | solution.py:433
  (11 other events, 46.7 us)

commit v2 on v1

--- a/solution.py
+++ b/solution.py
@@ -99,10 +99,8 @@
     def planes(send):
         return np.einsum("pz,ab->paBz".replace("B", "b"), send, eye(ROWS)).reshape(-1, ROWS * ROWS)
 
-    out["zsend"] = stack(*[planes(send1[s]) for s in sides], *[planes(send2[s]) for s in sides])
-    out["zown"] = stack(
-        np.kron(eye(ROWS), second[0]), np.kron(eye(ROWS), third[0]), *[planes(send22[s]) for s in sides]
-    )
+    out["zsend"] = stack(*[planes(send[s]) for send in (send1, send2, send22) for s in sides])
+    out["zown"] = stack(np.kron(eye(ROWS), second[0]), np.kron(eye(ROWS), third[0]))
 
     def back(give):
         return np.einsum("zp,ab->azpb", give, eye(ROWS)).reshape(ROWS * give.shape[0], -1)
@@ -214,7 +212,7 @@
 
 def lift_kernel(
     x_ref, txh, txl, rims, zsh, zsl, t12h, t12l,
-    u_ref, high_ref, low_ref, r1_ref, l1_ref, cells_ref, far_ref, sems,
+    u_ref, high_ref, low_ref, r1_ref, l1_ref, r2_ref, l2_ref, cells_ref, far_ref, sems,
 ):
     comps, _, nx = x_ref.shape
     blocks, quarter = nx // 256, nx // 4
@@ -247,19 +245,21 @@
         return 0
 
     lax.fori_loop(0, comps, step, 0)
-    far = right(split(far_ref[...].reshape(64 * comps, nx // 2)), both(t12h, t12l))
-    for c in range(comps):
-        for k, ref in enumerate((r1_ref, l1_ref)):
+    far = right(split(far_ref[...].reshape(128 * comps, nx // 2)), both(t12h, t12l))
+    for c in range(comps):
+        for k, (ref, ref2) in enumerate(((r1_ref, r2_ref), (l1_ref, l2_ref))):
             for p in range(2):
-                at = 64 * c + 32 * k + 16 * p
-                ref[c, 48:, quarter * p : quarter * p + quarter] = far[at : at + 16]
+                lanes = slice(quarter * p, quarter * p + quarter)
+                at = 128 * c + 32 * k + 16 * p
+                ref[c, 48:, lanes] = far[at : at + 16]
+                ref2[c, :, lanes] = far[at + 64 : at + 80]
 
 
 def own_kernel(
-    high_ref, low_ref, zoh, zol, t12h, t12l, c1h, c1l, c2h, c2l, first_ref, second_ref, r2_ref, l2_ref, far_ref
+    high_ref, low_ref, zoh, zol, t12h, t12l, c1h, c1l, c2h, c2l, first_ref, second_ref, token_ref, far_ref,
 ):
     comps, _, half = high_ref.shape
-    quarter = half // 2
+    token_ref[...] = jnp.zeros_like(token_ref)
 
     def step(c, _):
         rows = left(both(zoh, zol), (high_ref[c], low_ref[c]))
@@ -268,13 +268,9 @@
         return 0
 
     lax.fori_loop(0, comps, step, 0)
-    far = right(split(far_ref[...].reshape(128 * comps, half)), both(t12h, t12l))
-    for c in range(comps):
-        second_ref[c] = left(both(c2h, c2l), split(far[128 * c : 128 * c + 64]))
-        for k, ref in enumerate((r2_ref, l2_ref)):
-            for p in range(2):
-                at = 128 * c + 64 + 32 * k + 16 * p
-                ref[c, :, quarter * p : quarter * p + quarter] = far[at : at + 16]
+    far = right(split(far_ref[...].reshape(64 * comps, half)), both(t12h, t12l))
+    for c in range(comps):
+        second_ref[c] = left(both(c2h, c2l), split(far[64 * c : 64 * c + 64]))
 
 
 def chain_kernel(
@@ -312,7 +308,7 @@
             ref2[c] = second[48 + 8 * k : 56 + 8 * k]
 
 
-def along_y_kernel(u_ref, l_ref, r_ref, txh, txl, rims, b_ref, to_r_ref, to_l_ref, halo_ref):
+def along_y_kernel(_, _2, _3, u_ref, l_ref, r_ref, txh, txl, rims, b_ref, to_r_ref, to_l_ref, halo_ref):
     comps, lanes = u_ref.shape[:2]
     blocks = lanes // 2
 
@@ -462,31 +458,31 @@
     near = ((comps, 64, half), F32)
     far = ((comps, 16, half), F32)
     cells = ((comps, lanes, ROWS * ROWS, 128), F32)
-    u, high, low, z_right, z_left = call(
+    u, high, low, z_right, z_left, z_right2, z_left2 = call(
         lift_kernel,
         [flat] + consts("tx", "rims", "zsend", "tx12"),
-        [cells] + [((comps, ROWS * ROWS, half), BF16)] * 2 + [near] * 2,
-        [pltpu.VMEM((comps, ROWS * ROWS, nx), F32), pltpu.VMEM((comps, 64, half), F32), dma(comps)],
+        [cells] + [((comps, ROWS * ROWS, half), BF16)] * 2 + [near] * 2 + [far] * 2,
+        [pltpu.VMEM((comps, ROWS * ROWS, nx), F32), pltpu.VMEM((comps, 128, half), F32), dma(comps)],
         flops=1 << 33,
         hbm_in=(0,),
     )
+    z_from_left2 = move(z_right2, "gz", 2)
     z_from_left = move(z_right, "gz", 1)
     z_from_right = move(z_left, "gz", -1)
-
-    first, second, z_right2, z_left2 = call(
+    z_from_right2 = move(z_left2, "gz", -2)
+
+    first, second, token = call(
         own_kernel,
         [high, low] + consts("zown", "tx12", "ychain1", "ychain2"),
-        [((comps, 112, half), F32), ((comps, 64, quarter), F32)] + [far] * 2,
-        [pltpu.VMEM((comps, 128, half), F32)],
+        [((comps, 112, half), F32), ((comps, 64, quarter), F32)] + [((8, 128), F32)],
+        [pltpu.VMEM((comps, 64, half), F32)],
         flops=1 << 32,
     )
-    z_from_left2 = move(z_right2, "gz", 2)
-    z_from_right2 = move(z_left2, "gz", -2)
 
     planes = ((comps, lanes, 2, ROWS, 128), F32)
     b, z0_right, z0_left = call(
         along_y_kernel,
-        [u, from_left0, from_right0] + consts("tx", "rims"),
+        [token, z_from_left2, z_from_right2, u, from_left0, from_right0] + consts("tx", "rims"),
         [cells] + [planes] * 2,
         [pltpu.VMEM((lanes, 64 * comps, 128), F32)],
         flops=1 << 32,

time: 62 us -> 52 us (0.84)
  the two profiles are of different devices: /device:TPU:6 before, /device:TPU:2 now
where the time goes in v2:
time: 52 us; the launch traced here: 51.3 us
  starting transfers between devices  25.1 us (48%)
  Pallas kernels  21 us (40%)
  waiting for transfers between devices  4.79 us (9%)
    ppermute x12, starting transfers between devices, move(): lax.ppermute(value, axis, [(i, (i + step) % count) for i in range(count)])  25.1 us
    pallas_call x7, Pallas kernels, call(): pl.pallas_call(body, in_specs=[spec(n, hbm_in) for n in range(len(ins))],...  21 us
    ppermute x12, waiting for transfers between devices, move(): lax.ppermute(value, axis, [(i, (i + step) % count) for i in range(count)])  4.79 us
  transfers between devices with their start and end apart: 12, of which 2 were waited for; matrix products, arithmetic and copies ran while one was open for 0% of the time, Pallas kernels for 34%

profile of v2, /device:TPU:2, one launch (start us, length us, event | category | flops | bytes accessed | tf_op | source)
XLA Modules:
  0.0 51.3 jit_solution(74386356844130869)
XLA Ops:
  0.0 0.0 copy-start.9
  0.0 0.0 copy-start.10
  0.0 0.0 copy-start.11
  0.1 1.7 %shard_map.228 = (f32[4,2,16,1024]{3,2,1,0:T(8,128)S(1)}, f32[4,2,16,1024]{3,2,1,0:T(8,128)S(1)}) custom-call(f32[4,16,16,1024]{3,2,1,0:T(8,128)} %x_ref.1), custom_call_target="tpu_custom_call" | custom-call | bytes 5242880 | tf_op jit(solution)/shard_map/pallas_call | solution.py:415
  1.7 1.7 %collective-permute-start.2 = (f32[4,2,16,1024]{3,2,1,0:T(8,128)S(1)}, f32[4,2,16,1024]{3,2,1,0:T(8,128)S(1)}, u32[]{:S(2)}, u32[]{:S(2)}) collective-permute-start(f32[4,2,16,1024]{3,2,1,0:T(8,128)S(1)} %get-tuple-element.34), channel_id=1, source_target_pairs={{0,8},{8,16},{16,24},{24,32},{32,40},{40,48},{48,56},{56,64},{64,7... | collective-permute-start | bytes 1572872 | tf_op jit(solution)/shard_map/ppermute | solution.py:429
  3.4 6.8 %collective-permute-start.3 = (f32[4,2,16,1024]{3,2,1,0:T(8,128)S(1)}, f32[4,2,16,1024]{3,2,1,0:T(8,128)S(1)}, u32[]{:S(2)}, u32[]{:S(2)}) collective-permute-start(f32[4,2,16,1024]{3,2,1,0:T(8,128)S(1)} %get-tuple-element.35), channel_id=1, source_target_pairs={{0,248},{8,0},{16,8},{24,16},{32,24},{40,32},{48,40},{56,48},{64,5... | collective-permute-start | bytes 1572872 | tf_op jit(solution)/shard_map/ppermute | solution.py:429
  10.3 0.0 copy-start.13
  10.3 6.1 %shard_map.226 = (f32[4,8,256,128]{3,2,1,0:T(8,128)S(1)}, bf16[4,256,512]{2,1,0:T(8,128)(2,1)S(1)}, bf16[4,256,512]{2,1,0:T(8,128)(2,1)S(1)}, f32[4,64,512]{2,1,...) custom-call(f32[4,256,1024]{2,1,0:T(8,128)} %bitcast.2, ...), custom_call_target="tpu_custom_call" | custom-call | flops 8589934592 | bytes 13074432 | tf_op jit(solution)/shard_map/pallas_call | solution.py:415
  16.5 1.6 %collective-permute-start = (f32[4,16,512]{2,1,0:T(8,128)S(1)}, f32[4,16,512]{2,1,0:T(8,128)S(1)}, u32[]{:S(2)}, u32[]{:S(2)}) collective-permute-start(f32[4,16,512]{2,1,0:T(8,128)S(1)} %get-tuple-element.31), channel_id=1, source_target_pairs={{0,2},{1,3},{2,4},{3,5},{4,6},{5,7},{6,0},{7,1},{8,10},{9,11},{10,... | collective-permute-start | bytes 393224 | tf_op jit(solution)/shard_map/ppermute | solution.py:429
  18.1 0.5 %collective-permute-start.1 = (f32[4,16,512]{2,1,0:T(8,128)S(1)}, f32[4,16,512]{2,1,0:T(8,128)S(1)}, u32[]{:S(2)}, u32[]{:S(2)}) collective-permute-start(f32[4,16,512]{2,1,0:T(8,128)S(1)} %get-tuple-element.32), channel_id=1, source_target_pairs={{0,6},{1,7},{2,0},{3,1},{4,2},{5,3},{6,4},{7,5},{8,14},{9,15},{10,... | collective-permute-start | bytes 393224 | tf_op jit(solution)/shard_map/ppermute | solution.py:429
  18.6 2.8 %shard_map.227 = (f32[4,112,512]{2,1,0:T(8,128)S(1)}, f32[4,64,256]{2,1,0:T(8,128)S(1)}, f32[8,128]{1,0:T(8,128)S(1)}) custom-call(bf16[4,256,512]{2,1,0:T(8,128)(2,1)S(1)} %get-tuple-element.28.high_ref, bf16[4,256,512]{2,1,0:T(8,128)(2,1)S(1)} %get-tuple-element.29.low_ref, bf16[192,256]{1,0:T(8,128)(2,1)S(1)} %copy-done.14, ...), custom_call_target="tpu_custom_call" | custom-call | flops 4294967296 | bytes 4075520 | tf_op jit(solution)/shard_map/pallas_call | solution.py:415
  21.5 0.0 collective-permute-done._2.l2_ref
  21.5 1.7 %collective-permute-start.7 = (f32[4,64,512]{2,1,0:T(8,128)S(1)}, f32[4,64,512]{2,1,0:T(8,128)S(1)}, u32[]{:S(2)}, u32[]{:S(2)}) collective-permute-start(f32[4,64,512]{2,1,0:T(8,128)S(1)} %get-tuple-element.44), channel_id=1, source_target_pairs={{0,7},{1,0},{2,1},{3,2},{4,3},{5,4},{6,5},{7,6},{8,15},{9,8},{10,9... | collective-permute-start | bytes 1572872 | tf_op jit(solution)/shard_map/ppermute | solution.py:429
  23.3 3.4 %shard_map.229 = (f32[4,8,256,128]{3,2,1,0:T(8,128)S(1)}, f32[4,8,2,16,128]{4,3,2,1,0:T(8,128)S(1)}, f32[4,8,2,16,128]{4,3,2,1,0:T(8,128)S(1)}) custom-call(f32[8,128]{1,0:T(8,128)S(1)} %get-tuple-element.30._, f32[4,16,512]{2,1,0:T(8,128)S(1)} %collective-permute-done._2.l2_ref, f32[4,16,512]{2,1,0:T(8,128)S(1)} %collective-permute-done.1._3.r2_ref, ...), custom_call_target="tpu_custom_call" | custom-call | flops 4294967296 | bytes 11276288 | tf_op jit(solution)/shard_map/pallas_call | solution.py:415
  26.7 0.0 collective-permute-start.4
  26.8 1.7 %collective-permute-start.5 = (f32[4,8,2,16,128]{4,3,2,1,0:T(8,128)S(1)}, f32[4,8,2,16,128]{4,3,2,1,0:T(8,128)S(1)}, u32[]{:S(2)}, u32[]{:S(2)}) collective-permute-start(f32[4,8,2,16,128]{4,3,2,1,0:T(8,128)S(1)} %get-tuple-element.38), channel_id=1, source_target_pairs={{0,7},{1,0},{2,1},{3,2},{4,3},{5,4},{6,5},{7,6},{8,15},{9,8},{10,9... | collective-permute-start | bytes 1572872 | tf_op jit(solution)/shard_map/ppermute | solution.py:429
  28.5 1.4 %collective-permute-done.7.r1_ref = f32[4,64,512]{2,1,0:T(8,128)S(1)} collective-permute-done((f32[4,64,512]{2,1,0:T(8,128)S(1)}, f32[4,64,512]{2,1,0:T(8,128)S(1)}, u32[]{:S(2)}, u32[]{:S(2)}) %collective-permute-start.7) | collective-permute-done | bytes 524320 | tf_op jit(solution)/shard_map/ppermute | solution.py:429
  30.0 1.6 %shard_map.231 = (f32[4,64,512]{2,1,0:T(8,128)S(1)}, f32[4,16,256]{2,1,0:T(8,128)S(1)}, f32[4,32,512]{2,1,0:T(8,128)S(1)}, f32[4,32,512]{2,1,0:T(8,128)S(1)}, f3...) custom-call(f32[4,112,512]{2,1,0:T(8,128)S(1)} %get-tuple-element.41.first_ref, ...), custom_call_target="tpu_custom_call" | custom-call | flops 2147483648 | bytes 4294656 | tf_op jit(solution)/shard_map/pallas_call | solution.py:415
  31.6 0.1 collective-permute-start.10
  31.7 5.6 %collective-permute-start.11 = (f32[4,8,256]{2,1,0:T(8,128)S(1)}, f32[4,8,256]{2,1,0:T(8,128)S(1)}, u32[]{:S(2)}, u32[]{:S(2)}) collective-permute-start(f32[4,8,256]{2,1,0:T(8,128)S(1)} %get-tuple-element.50), channel_id=1, source_target_pairs={{0,240},{8,248},{16,0},{24,8},{32,16},{40,24},{48,32},{56,40},{64,... | collective-permute-start | bytes 98312 | tf_op jit(solution)/shard_map/ppermute | solution.py:429
  37.3 5.3 %collective-permute-start.9 = (f32[4,32,512]{2,1,0:T(8,128)S(1)}, f32[4,32,512]{2,1,0:T(8,128)S(1)}, u32[]{:S(2)}, u32[]{:S(2)}) collective-permute-start(f32[4,32,512]{2,1,0:T(8,128)S(1)} %get-tuple-element.48), channel_id=1, source_target_pairs={{0,248},{8,0},{16,8},{24,16},{32,24},{40,32},{48,40},{56,48},{64,5... | collective-permute-start | bytes 786440 | tf_op jit(solution)/shard_map/ppermute | solution.py:429
  42.7 3.3 %shard_map.230 = (f32[4,256,1024]{2,1,0:T(8,128)}, f32[4,4,128,128]{3,2,1,0:T(8,128)S(1)}) custom-call(f32[4,8,256,128]{3,2,1,0:T(8,128)S(1)} %get-tuple-element.36.b_ref, f32[4,8,2,16,128]{4,3,2,1,0:T(8,128)S(1)} %collective-permute-done.4.l_ref, f32[4,8,2,16,128]{4,3,2,1,0:T(8,128)S(1)} %collective-permute-done.5.r_ref), custom_call_target="tpu_custom_call" | custom-call | flops 4294967296 | bytes 10485760 | tf_op jit(solution)/shard_map/pallas_call | solution.py:415
  46.0 3.3 %collective-permute-done.8.l1_ref = f32[4,32,512]{2,1,0:T(8,128)S(1)} collective-permute-done((f32[4,32,512]{2,1,0:T(8,128)S(1)}, f32[4,32,512]{2,1,0:T(8,128)S(1)}, u32[]{:S(2)}, u32[]{:S(2)}) %collective-permute-start.8) | collective-permute-done | bytes 262176 | tf_op jit(solution)/shard_map/ppermute | solution.py:429
  49.4 2.0 %shard_map.232 = f32[4,256,1024]{2,1,0:T(8,128)} custom-call(f32[4,256,1024]{2,1,0:T(8,128)} %get-tuple-element.39._, f32[4,4,128,128]{3,2,1,0:T(8,128)S(1)} %get-tuple-element.40.even_ref, f32[4,64,512]{2,1,0:T(8,128)S(1)} %get-tuple-element.45.o1_ref, f32[4,16,256]{2,1,0:T(8,128)S(1)} %get-tuple-element.46.o2_ref, ...), custom_call_target="tpu_custom_call", output_to_operand_aliasing={{}: (0, {})} | custom-call | flops 1073741824 | bytes 11680768 | tf_op jit(solution)/shard_map/pallas_call | solution.py:415
  (53 shorter events, 0.1 us)
Async XLA Ops:
  0.0 10.2 %copy-start.6 = (bf16[512,256]{1,0:T(8,128)(2,1)S(1)}, bf16[512,256]{1,0:T(8,128)(2,1)}, u32[]{:S(2)}) copy-start(bf16[512,256]{1,0:T(8,128)(2,1)} %constant.51.clone.t12l) | copy-start | bytes 786436
  0.0 10.2 %copy-start.7 = (bf16[512,256]{1,0:T(8,128)(2,1)S(1)}, bf16[512,256]{1,0:T(8,128)(2,1)}, u32[]{:S(2)}) copy-start(bf16[512,256]{1,0:T(8,128)(2,1)} %constant.50.clone.t12h) | copy-start | bytes 786436
  0.0 10.2 %copy-start.8 = (bf16[128,1024]{1,0:T(8,128)(2,1)S(1)}, bf16[128,1024]{1,0:T(8,128)(2,1)}, u32[]{:S(2)}) copy-start(bf16[128,1024]{1,0:T(8,128)(2,1)} %constant.68.clone.rims) | copy-start | bytes 786436
  0.0 10.2 %copy-start.9 = (bf16[256,256]{1,0:T(8,128)(2,1)S(1)}, bf16[256,256]{1,0:T(8,128)(2,1)}, u32[]{:S(2)}) copy-start(bf16[256,256]{1,0:T(8,128)(2,1)} %constant.47.clone.txl) | copy-start | bytes 393220
  0.0 10.2 %copy-start.10 = (bf16[256,256]{1,0:T(8,128)(2,1)S(1)}, bf16[256,256]{1,0:T(8,128)(2,1)}, u32[]{:S(2)}) copy-start(bf16[256,256]{1,0:T(8,128)(2,1)} %constant.46.clone.txh) | copy-start | bytes 393220
  0.0 10.2 %copy-start.11 = (bf16[224,256]{1,0:T(8,128)(2,1)S(1)}, bf16[224,256]{1,0:T(8,128)(2,1)}, u32[]{:S(2)}) copy-start(bf16[224,256]{1,0:T(8,128)(2,1)} %constant.53.clone.zsl) | copy-start | bytes 344068
  0.0 10.2 %copy-start.12 = (bf16[224,256]{1,0:T(8,128)(2,1)S(1)}, bf16[224,256]{1,0:T(8,128)(2,1)}, u32[]{:S(2)}) copy-start(bf16[224,256]{1,0:T(8,128)(2,1)} %constant.52.clone.zsh) | copy-start | bytes 344068
  1.7 21.5 %collective-permute-start.2 = (f32[4,2,16,1024]{3,2,1,0:T(8,128)S(1)}, f32[4,2,16,1024]{3,2,1,0:T(8,128)S(1)}, u32[]{:S(2)}, u32[]{:S(2)}) collective-permute-start(f32[4,2,16,1024]{3,2,1,0:T(8,128)S(1)} %get-tuple-element.34), channel_id=1, source_target_pairs={{0,8},{8,16},{16,24},{24,32},{32,40},{40,48},{48,56},{56,64},{64,7... | collective-permute-start | bytes 1572872 | tf_op jit(solution)/shard_map/ppermute | solution.py:429
  3.4 19.8 %collective-permute-start.3 = (f32[4,2,16,1024]{3,2,1,0:T(8,128)S(1)}, f32[4,2,16,1024]{3,2,1,0:T(8,128)S(1)}, u32[]{:S(2)}, u32[]{:S(2)}) collective-permute-start(f32[4,2,16,1024]{3,2,1,0:T(8,128)S(1)} %get-tuple-element.35), channel_id=1, source_target_pairs={{0,248},{8,0},{16,8},{24,16},{32,24},{40,32},{48,40},{56,48},{64,5... | collective-permute-start | bytes 1572872 | tf_op jit(solution)/shard_map/ppermute | solution.py:429
  10.3 8.3 %copy-start.13 = (bf16[192,256]{1,0:T(8,128)(2,1)S(1)}, bf16[192,256]{1,0:T(8,128)(2,1)}, u32[]{:S(2)}) copy-start(bf16[192,256]{1,0:T(8,128)(2,1)} %constant.55.clone.zol) | copy-start | bytes 294916
  10.3 8.3 %copy-start.14 = (bf16[192,256]{1,0:T(8,128)(2,1)S(1)}, bf16[192,256]{1,0:T(8,128)(2,1)}, u32[]{:S(2)}) copy-start(bf16[192,256]{1,0:T(8,128)(2,1)} %constant.54.clone.zoh) | copy-start | bytes 294916
  10.3 8.3 %copy-start.17 = (bf16[112,128]{1,0:T(8,128)(2,1)S(1)}, bf16[112,128]{1,0:T(8,128)(2,1)}, u32[]{:S(2)}) copy-start(bf16[112,128]{1,0:T(8,128)(2,1)} %constant.57.clone.c1l) | copy-start | bytes 86020
  10.3 8.3 %copy-start.18 = (bf16[112,128]{1,0:T(8,128)(2,1)S(1)}, bf16[112,128]{1,0:T(8,128)(2,1)}, u32[]{:S(2)}) copy-start(bf16[112,128]{1,0:T(8,128)(2,1)} %constant.56.clone.c1h) | copy-start | bytes 86020
  10.3 8.3 %copy-start.21 = (bf16[64,64]{1,0:T(8,128)(2,1)S(1)}, bf16[64,64]{1,0:T(8,128)(2,1)}, u32[]{:S(2)}) copy-start(bf16[64,64]{1,0:T(8,128)(2,1)} %constant.59.clone.c2l) | copy-start | bytes 24580
  16.5 5.0 %collective-permute-start = (f32[4,16,512]{2,1,0:T(8,128)S(1)}, f32[4,16,512]{2,1,0:T(8,128)S(1)}, u32[]{:S(2)}, u32[]{:S(2)}) collective-permute-start(f32[4,16,512]{2,1,0:T(8,128)S(1)} %get-tuple-element.31), channel_id=1, source_target_pairs={{0,2},{1,3},{2,4},{3,5},{4,6},{5,7},{6,0},{7,1},{8,10},{9,11},{10,... | collective-permute-start | bytes 393224 | tf_op jit(solution)/shard_map/ppermute | solution.py:429
  18.1 5.2 %collective-permute-start.1 = (f32[4,16,512]{2,1,0:T(8,128)S(1)}, f32[4,16,512]{2,1,0:T(8,128)S(1)}, u32[]{:S(2)}, u32[]{:S(2)}) collective-permute-start(f32[4,16,512]{2,1,0:T(8,128)S(1)} %get-tuple-element.32), channel_id=1, source_target_pairs={{0,6},{1,7},{2,0},{3,1},{4,2},{5,3},{6,4},{7,5},{8,14},{9,15},{10,... | collective-permute-start | bytes 393224 | tf_op jit(solution)/shard_map/ppermute | solution.py:429
  18.6 9.9 %collective-permute-start.6 = (f32[4,64,512]{2,1,0:T(8,128)S(1)}, f32[4,64,512]{2,1,0:T(8,128)S(1)}, u32[]{:S(2)}, u32[]{:S(2)}) collective-permute-start(f32[4,64,512]{2,1,0:T(8,128)S(1)} %get-tuple-element.43), channel_id=1, source_target_pairs={{0,1},{1,2},{2,3},{3,4},{4,5},{5,6},{6,7},{7,0},{8,9},{9,10},{10,1... | collective-permute-start | bytes 1572872 | tf_op jit(solution)/shard_map/ppermute | solution.py:429
  21.5 8.4 %collective-permute-start.7 = (f32[4,64,512]{2,1,0:T(8,128)S(1)}, f32[4,64,512]{2,1,0:T(8,128)S(1)}, u32[]{:S(2)}, u32[]{:S(2)}) collective-permute-start(f32[4,64,512]{2,1,0:T(8,128)S(1)} %get-tuple-element.44), channel_id=1, source_target_pairs={{0,7},{1,0},{2,1},{3,2},{4,3},{5,4},{6,5},{7,6},{8,15},{9,8},{10,9... | collective-permute-start | bytes 1572872 | tf_op jit(solution)/shard_map/ppermute | solution.py:429
  26.7 10.6 %collective-permute-start.4 = (f32[4,8,2,16,128]{4,3,2,1,0:T(8,128)S(1)}, f32[4,8,2,16,128]{4,3,2,1,0:T(8,128)S(1)}, u32[]{:S(2)}, u32[]{:S(2)}) collective-permute-start(f32[4,8,2,16,128]{4,3,2,1,0:T(8,128)S(1)} %get-tuple-element.37), channel_id=1, source_target_pairs={{0,1},{1,2},{2,3},{3,4},{4,5},{5,6},{6,7},{7,0},{8,9},{9,10},{10,1... | collective-permute-start | bytes 1572872 | tf_op jit(solution)/shard_map/ppermute | solution.py:429
  26.8 15.9 %collective-permute-start.5 = (f32[4,8,2,16,128]{4,3,2,1,0:T(8,128)S(1)}, f32[4,8,2,16,128]{4,3,2,1,0:T(8,128)S(1)}, u32[]{:S(2)}, u32[]{:S(2)}) collective-permute-start(f32[4,8,2,16,128]{4,3,2,1,0:T(8,128)S(1)} %get-tuple-element.38), channel_id=1, source_target_pairs={{0,7},{1,0},{2,1},{3,2},{4,3},{5,4},{6,5},{7,6},{8,15},{9,8},{10,9... | collective-permute-start | bytes 1572872 | tf_op jit(solution)/shard_map/ppermute | solution.py:429
  31.6 14.4 %collective-permute-start.10 = (f32[4,8,256]{2,1,0:T(8,128)S(1)}, f32[4,8,256]{2,1,0:T(8,128)S(1)}, u32[]{:S(2)}, u32[]{:S(2)}) collective-permute-start(f32[4,8,256]{2,1,0:T(8,128)S(1)} %get-tuple-element.49), channel_id=1, source_target_pairs={{0,16},{8,24},{16,32},{24,40},{32,48},{40,56},{48,64},{56,72},{64,... | collective-permute-start | bytes 98312 | tf_op jit(solution)/shard_map/ppermute | solution.py:429
  31.7 14.4 %collective-permute-start.11 = (f32[4,8,256]{2,1,0:T(8,128)S(1)}, f32[4,8,256]{2,1,0:T(8,128)S(1)}, u32[]{:S(2)}, u32[]{:S(2)}) collective-permute-start(f32[4,8,256]{2,1,0:T(8,128)S(1)} %get-tuple-element.50), channel_id=1, source_target_pairs={{0,240},{8,248},{16,0},{24,8},{32,16},{40,24},{48,32},{56,40},{64,... | collective-permute-start | bytes 98312 | tf_op jit(solution)/shard_map/ppermute | solution.py:429
  37.3 12.0 %collective-permute-start.8 = (f32[4,32,512]{2,1,0:T(8,128)S(1)}, f32[4,32,512]{2,1,0:T(8,128)S(1)}, u32[]{:S(2)}, u32[]{:S(2)}) collective-permute-start(f32[4,32,512]{2,1,0:T(8,128)S(1)} %get-tuple-element.47), channel_id=1, source_target_pairs={{0,8},{8,16},{16,24},{24,32},{32,40},{40,48},{48,56},{56,64},{64,7... | collective-permute-start | bytes 786440 | tf_op jit(solution)/shard_map/ppermute | solution.py:429
  37.3 12.0 %collective-permute-start.9 = (f32[4,32,512]{2,1,0:T(8,128)S(1)}, f32[4,32,512]{2,1,0:T(8,128)S(1)}, u32[]{:S(2)}, u32[]{:S(2)}) collective-permute-start(f32[4,32,512]{2,1,0:T(8,128)S(1)} %get-tuple-element.48), channel_id=1, source_target_pairs={{0,248},{8,0},{16,8},{24,16},{32,24},{40,32},{48,40},{56,48},{64,5... | collective-permute-start | bytes 786440 | tf_op jit(solution)/shard_map/ppermute | solution.py:429
  (11 other events, 75.1 us)

commit v3 on v2

--- a/solution.py
+++ b/solution.py
@@ -276,7 +276,7 @@
 def chain_kernel(
     first_ref, second_ref, l1_ref, r1_ref, l2_ref, r2_ref,
     g1h, g1l, g2h, g2l, t12h, t12l,
-    o1_ref, o2_ref, to_r_ref, to_l_ref, to_r2_ref, to_l2_ref, far_ref,
+    o1_ref, o2_ref, to_r_ref, to_l_ref, away_ref, far_ref,
 ):
     comps, _, half = first_ref.shape
     quarter = half // 2
@@ -302,13 +302,13 @@
         second = left(both(g2h, g2l), split(jnp.concatenate(deep, 0)))
         second = second_ref[c] + (far[64 * c : 64 * c + 64] + second)
         o2_ref[c] = second[:16]
-        for k, (ref, ref2) in enumerate(((to_r_ref, to_r2_ref), (to_l_ref, to_l2_ref))):
+        for k, ref in enumerate((to_r_ref, to_l_ref)):
             ref[c, 24:, :quarter] = second[16 + 16 * k : 24 + 16 * k]
             ref[c, 24:, quarter:] = second[24 + 16 * k : 32 + 16 * k]
-            ref2[c] = second[48 + 8 * k : 56 + 8 * k]
-
-
-def along_y_kernel(_, _2, _3, u_ref, l_ref, r_ref, txh, txl, rims, b_ref, to_r_ref, to_l_ref, halo_ref):
+        away_ref[c] = second[48:]
+
+
+def along_y_kernel(_, u_ref, l_ref, r_ref, txh, txl, rims, b_ref, to_r_ref, to_l_ref, halo_ref):
     comps, lanes = u_ref.shape[:2]
     blocks = lanes // 2
 
@@ -336,6 +336,26 @@
         return 0
 
     lax.fori_loop(0, comps * lanes, step, 0)
+
+
+def after(values, earlier):
+    count = len(values)
+
+    def body(*refs):
+        pass
+
+    return pl.pallas_call(
+        body,
+        in_specs=[pl.BlockSpec(memory_space=pl.ANY)] * (count + len(earlier)),
+        out_specs=[pl.BlockSpec(memory_space=pl.ANY)] * count,
+        out_shape=[jax.ShapeDtypeStruct(v.shape, v.dtype) for v in values],
+        input_output_aliases={n: n for n in range(count)},
+    )(*values, *earlier)
+
+
+def away_kernel(_, away_ref, to_r2_ref, to_l2_ref):
+    to_r2_ref[...] = away_ref[:, :8]
+    to_l2_ref[...] = away_ref[:, 8:]
 
 
 def along_z_kernel(b_ref, l_ref, r_ref, out_ref, even_ref, done_ref, sems):
@@ -466,10 +486,9 @@
         flops=1 << 33,
         hbm_in=(0,),
     )
-    z_from_left2 = move(z_right2, "gz", 2)
     z_from_left = move(z_right, "gz", 1)
     z_from_right = move(z_left, "gz", -1)
-    z_from_right2 = move(z_left2, "gz", -2)
+    z_from_left2 = move(z_right2, "gz", 2)
 
     first, second, token = call(
         own_kernel,
@@ -479,29 +498,34 @@
         flops=1 << 32,
     )
 
+    (z_left2,) = after([z_left2], [token, z_from_left2])
+    z_from_right2 = move(z_left2, "gz", -2)
+
     planes = ((comps, lanes, 2, ROWS, 128), F32)
     b, z0_right, z0_left = call(
         along_y_kernel,
-        [token, z_from_left2, z_from_right2, u, from_left0, from_right0] + consts("tx", "rims"),
+        [token, u, from_left0, from_right0] + consts("tx", "rims"),
         [cells] + [planes] * 2,
         [pltpu.VMEM((lanes, 64 * comps, 128), F32)],
         flops=1 << 32,
     )
+    z0_right, z0_left = after([z0_right, z0_left], [z_from_right2])
     z0_from_left = move(z0_right, "gz", 1)
     z0_from_right = move(z0_left, "gz", -1)
 
-    o1, o2, y1_right, y1_left, y2_right, y2_left = call(
+    o1, o2, y1_right, y1_left, away = call(
         chain_kernel,
         [first, second, z_from_left, z_from_right, z_from_left2, z_from_right2] + consts("chain1", "chain2", "tx12"),
         [((comps, 64, half), F32), ((comps, 16, quarter), F32)]
         + [((comps, 32, half), F32)] * 2
-        + [((comps, 8, quarter), F32)] * 2,
+        + [((comps, 16, quarter), F32)],
         [pltpu.VMEM((comps, 64, half), F32)],
         flops=1 << 31,
     )
-    y_from_left2 = move(y2_right, "gy", 2)
     y_from_left = move(y1_right, "gy", 1)
     y_from_right = move(y1_left, "gy", -1)
+    y2_right, y2_left = call(away_kernel, [z0_from_left, away], [((comps, 8, quarter), F32)] * 2)
+    y_from_left2 = move(y2_right, "gy", 2)
     y_from_right2 = move(y2_left, "gy", -2)
 
     whole = ((comps, ROWS * ROWS, nx), F32)

time: 52 us -> 70.5 us (1.36)
  local copies, waits for them, and re-layouts: 0.14 us -> 21.2 us
  waiting for transfers between devices: 4.79 us -> 0.03 us
  starting transfers between devices: 25.1 us -> 26.3 us
  Pallas kernels: 21 us -> 21.9 us
    unnamed x46 -> x88, local copies, waits for them, and re-layouts: 0.14 us -> 21.2 us
    ppermute x12, waiting for transfers between devices: 4.79 us -> 0.03 us  [move(): lax.ppermute(value, axis, [(i, (i + step) % count) for i in range(count)])]
    ppermute x12, starting transfers between devices: 25.1 us -> 26.3 us  [move(): lax.ppermute(value, axis, [(i, (i + step) % count) for i in range(count)])]
    pallas_call x7 -> x8, Pallas kernels: 21 us -> 21.9 us  [call(): pl.pallas_call(body, in_specs=[spec(n, hbm_in) for n in range(len(ins))],...]
  transfers between devices with their start and end apart: 12 -> 12, of which waited for: 2 -> 0; matrix products, arithmetic and copies ran while one was open for 0% -> 0% of each run, Pallas kernels for 34% -> 25%
where the time goes in v3:
time: 70.5 us; the launch traced here: 69.9 us
  starting transfers between devices  26.3 us (37%)
  Pallas kernels  21.9 us (31%)
  local copies, waits for them, and re-layouts  21.2 us (30%)
    ppermute x12, starting transfers between devices, move(): lax.ppermute(value, axis, [(i, (i + step) % count) for i in range(count)])  26.3 us
    pallas_call x8, Pallas kernels, call(): pl.pallas_call(body, in_specs=[spec(n, hbm_in) for n in range(len(ins))],...  21.9 us
    unnamed x88, local copies, waits for them, and re-layouts  21.2 us
  transfers between devices with their start and end apart: 12, of which 0 were waited for; matrix products, arithmetic and copies ran while one was open for 0% of the time, Pallas kernels for 25%

profile of v3, /device:TPU:2, one launch (start us, length us, event | category | flops | bytes accessed | tf_op | source)
XLA Modules:
  0.0 69.9 jit_solution(11230425964105386525)
XLA Ops:
  0.1 2.6 %shard_map.228 = (f32[4,2,16,1024]{3,2,1,0:T(8,128)}, f32[4,2,16,1024]{3,2,1,0:T(8,128)}) custom-call(f32[4,16,16,1024]{3,2,1,0:T(8,128)} %x_ref.1), custom_call_target="tpu_custom_call" | custom-call | bytes 5242880 | tf_op jit(solution)/shard_map/pallas_call | solution.py:435
  2.7 1.7 %collective-permute-start = (f32[4,2,16,1024]{3,2,1,0:T(8,128)}, f32[4,2,16,1024]{3,2,1,0:T(8,128)S(1)}, u32[]{:S(2)}, u32[]{:S(2)}) collective-permute-start(f32[4,2,16,1024]{3,2,1,0:T(8,128)} %get-tuple-element.35), channel_id=1, source_target_pairs={{0,8},{8,16},{16,24},{24,32},{32,40},{40,48},{48,56},{56,64},{64,7... | collective-permute-start | bytes 1572872 | tf_op jit(solution)/shard_map/ppermute | solution.py:449
  4.3 6.8 %collective-permute-start.1 = (f32[4,2,16,1024]{3,2,1,0:T(8,128)}, f32[4,2,16,1024]{3,2,1,0:T(8,128)S(1)}, u32[]{:S(2)}, u32[]{:S(2)}) collective-permute-start(f32[4,2,16,1024]{3,2,1,0:T(8,128)} %get-tuple-element.36), channel_id=1, source_target_pairs={{0,248},{8,0},{16,8},{24,16},{32,24},{40,32},{48,40},{56,48},{64,5... | collective-permute-start | bytes 1572872 | tf_op jit(solution)/shard_map/ppermute | solution.py:449
  11.3 6.1 %shard_map.226 = (f32[4,8,256,128]{3,2,1,0:T(8,128)S(1)}, bf16[4,256,512]{2,1,0:T(8,128)(2,1)S(1)}, bf16[4,256,512]{2,1,0:T(8,128)(2,1)S(1)}, f32[4,64,512]{2,1,...) custom-call(f32[4,256,1024]{2,1,0:T(8,128)} %bitcast.2, ...), custom_call_target="tpu_custom_call" | custom-call | flops 8589934592 | bytes 13074432 | tf_op jit(solution)/shard_map/pallas_call | solution.py:435
  17.4 2.0 %copy-done.38 = f32[4,8,256,128]{3,2,1,0:T(8,128)} copy-done((f32[4,8,256,128]{3,2,1,0:T(8,128)}, f32[4,8,256,128]{3,2,1,0:T(8,128)S(1)}, u32[]{:S(2)}) %copy-start.38) | copy-done | bytes 4194328
  19.4 1.5 %collective-permute-start.2 = (f32[4,16,512]{2,1,0:T(8,128)S(1)}, f32[4,16,512]{2,1,0:T(8,128)S(1)}, u32[]{:S(2)}, u32[]{:S(2)}) collective-permute-start(f32[4,16,512]{2,1,0:T(8,128)S(1)} %get-tuple-element.41), channel_id=1, source_target_pairs={{0,2},{1,3},{2,4},{3,5},{4,6},{5,7},{6,0},{7,1},{8,10},{9,11},{10,... | collective-permute-start | bytes 393224 | tf_op jit(solution)/shard_map/ppermute | solution.py:449
  20.9 1.7 %collective-permute-start.7 = (f32[4,64,512]{2,1,0:T(8,128)S(1)}, f32[4,64,512]{2,1,0:T(8,128)S(1)}, u32[]{:S(2)}, u32[]{:S(2)}) collective-permute-start(f32[4,64,512]{2,1,0:T(8,128)S(1)} %get-tuple-element.49), channel_id=1, source_target_pairs={{0,7},{1,0},{2,1},{3,2},{4,3},{5,4},{6,5},{7,6},{8,15},{9,8},{10,9... | collective-permute-start | bytes 1572872 | tf_op jit(solution)/shard_map/ppermute | solution.py:449
  22.7 2.8 %shard_map.227 = (f32[4,112,512]{2,1,0:T(8,128)S(1)}, f32[4,64,256]{2,1,0:T(8,128)S(1)}, f32[8,128]{1,0:T(8,128)S(1)}) custom-call(bf16[4,256,512]{2,1,0:T(8,128)(2,1)S(1)} %get-tuple-element.31.high_ref, bf16[4,256,512]{2,1,0:T(8,128)(2,1)S(1)} %get-tuple-element.32.low_ref, bf16[192,256]{1,0:T(8,128)(2,1)S(1)} %copy-done.27, ...), custom_call_target="tpu_custom_call" | custom-call | flops 4294967296 | bytes 4075520 | tf_op jit(solution)/shard_map/pallas_call | solution.py:435
  26.2 1.0 %copy-done.40 = f32[4,112,512]{2,1,0:T(8,128)} copy-done((f32[4,112,512]{2,1,0:T(8,128)}, f32[4,112,512]{2,1,0:T(8,128)S(1)}, u32[]{:S(2)}) %copy-start.40) | copy-done | bytes 917528
  28.5 1.7 %collective-permute-start.3 = (f32[4,16,512]{2,1,0:T(8,128)}, f32[4,16,512]{2,1,0:T(8,128)S(1)}, u32[]{:S(2)}, u32[]{:S(2)}) collective-permute-start(f32[4,16,512]{2,1,0:T(8,128)} %shard_map.230), channel_id=1, source_target_pairs={{0,6},{1,7},{2,0},{3,1},{4,2},{5,3},{6,4},{7,5},{8,14},{9,15},{10,... | collective-permute-start | bytes 393224 | tf_op jit(solution)/shard_map/ppermute | solution.py:449
  30.9 0.9 %copy-done.20 = bf16[128,1024]{1,0:T(8,128)(2,1)S(1)} copy-done((bf16[128,1024]{1,0:T(8,128)(2,1)S(1)}, bf16[128,1024]{1,0:T(8,128)(2,1)}, u32[]{:S(2)}) %copy-start.20) | copy-done | bytes 262168
  32.8 2.2 %copy-done.39 = f32[4,8,256,128]{3,2,1,0:T(8,128)S(1)} copy-done((f32[4,8,256,128]{3,2,1,0:T(8,128)S(1)}, f32[4,8,256,128]{3,2,1,0:T(8,128)}, u32[]{:S(2)}) %copy-start.39) | copy-done | bytes 4194328
  35.0 3.4 %shard_map.229 = (f32[4,8,256,128]{3,2,1,0:T(8,128)S(1)}, f32[4,8,2,16,128]{4,3,2,1,0:T(8,128)S(1)}, f32[4,8,2,16,128]{4,3,2,1,0:T(8,128)S(1)}) custom-call(f32[8,128]{1,0:T(8,128)S(1)} %copy-done.14, f32[4,8,256,128]{3,2,1,0:T(8,128)S(1)} %copy-done.39, f32[4,2,16,1024]{3,2,1,0:T(8,128)S(1)} %collective-permute-done.l_ref, ...), custom_call_target="tpu_custom_call" | custom-call | flops 4294967296 | bytes 11014144 | tf_op jit(solution)/shard_map/pallas_call | solution.py:435
  40.0 2.0 %copy-done.36 = f32[4,8,256,128]{3,2,1,0:T(8,128)} copy-done((f32[4,8,256,128]{3,2,1,0:T(8,128)}, f32[4,8,256,128]{3,2,1,0:T(8,128)S(1)}, u32[]{:S(2)}) %copy-start.36) | copy-done | bytes 4194328
  42.7 1.7 %collective-permute-start.5 = (f32[4,8,2,16,128]{4,3,2,1,0:T(8,128)}, f32[4,8,2,16,128]{4,3,2,1,0:T(8,128)S(1)}, u32[]{:S(2)}, u32[]{:S(2)}) collective-permute-start(f32[4,8,2,16,128]{4,3,2,1,0:T(8,128)} %get-tuple-element.43), channel_id=1, source_target_pairs={{0,7},{1,0},{2,1},{3,2},{4,3},{5,4},{6,5},{7,6},{8,15},{9,8},{10,9... | collective-permute-start | bytes 1572872 | tf_op jit(solution)/shard_map/ppermute | solution.py:449
  45.3 0.9 %copy-done.16 = bf16[512,256]{1,0:T(8,128)(2,1)S(1)} copy-done((bf16[512,256]{1,0:T(8,128)(2,1)S(1)}, bf16[512,256]{1,0:T(8,128)(2,1)}, u32[]{:S(2)}) %copy-start.16) | copy-done | bytes 262168
  46.3 0.9 %copy-done.18 = bf16[512,256]{1,0:T(8,128)(2,1)S(1)} copy-done((bf16[512,256]{1,0:T(8,128)(2,1)S(1)}, bf16[512,256]{1,0:T(8,128)(2,1)}, u32[]{:S(2)}) %copy-start.18) | copy-done | bytes 262168
  49.5 1.2 %copy-done.41 = f32[4,112,512]{2,1,0:T(8,128)S(1)} copy-done((f32[4,112,512]{2,1,0:T(8,128)S(1)}, f32[4,112,512]{2,1,0:T(8,128)}, u32[]{:S(2)}) %copy-start.41) | copy-done | bytes 917528
  50.7 0.9 %copy-done.43 = f32[4,64,256]{2,1,0:T(8,128)S(1)} copy-done((f32[4,64,256]{2,1,0:T(8,128)S(1)}, f32[4,64,256]{2,1,0:T(8,128)}, u32[]{:S(2)}) %copy-start.43) | copy-done | bytes 262168
  51.7 1.6 %shard_map.233 = (f32[4,64,512]{2,1,0:T(8,128)S(1)}, f32[4,16,256]{2,1,0:T(8,128)S(1)}, f32[4,32,512]{2,1,0:T(8,128)S(1)}, f32[4,32,512]{2,1,0:T(8,128)S(1)}, f32[4,16,256]{2,1,0:T(8,128)S(1)}) custom-call(f32[4,112,512]{2,1,0:T(8,128)S(1)} %copy-done.41, f32[4,64,256]{2,1,0:T(8,128)S(1)} %copy-done.43, f32[4,64,512]{2,1,0:T(8,128)S(1)} %collective-permute-done.6.l1_ref, ...), custom_call_target="tpu_custom_call" | custom-call | flops 2147483648 | bytes 4294656 | tf_op jit(solution)/shard_map/pallas_call | solution.py:435
  53.4 5.3 %collective-permute-start.9 = (f32[4,32,512]{2,1,0:T(8,128)S(1)}, f32[4,32,512]{2,1,0:T(8,128)S(1)}, u32[]{:S(2)}, u32[]{:S(2)}) collective-permute-start(f32[4,32,512]{2,1,0:T(8,128)S(1)} %get-tuple-element.53), channel_id=1, source_target_pairs={{0,248},{8,0},{16,8},{24,16},{32,24},{40,32},{48,40},{56,48},{64,5... | collective-permute-start | bytes 786440 | tf_op jit(solution)/shard_map/ppermute | solution.py:449
  58.8 5.6 %collective-permute-start.11 = (f32[4,8,256]{2,1,0:T(8,128)S(1)}, f32[4,8,256]{2,1,0:T(8,128)S(1)}, u32[]{:S(2)}, u32[]{:S(2)}) collective-permute-start(f32[4,8,256]{2,1,0:T(8,128)S(1)} %get-tuple-element.56), channel_id=1, source_target_pairs={{0,240},{8,248},{16,0},{24,8},{32,16},{40,24},{48,32},{56,40},{64,... | collective-permute-start | bytes 98312 | tf_op jit(solution)/shard_map/ppermute | solution.py:449
  64.5 3.3 %shard_map.232 = (f32[4,256,1024]{2,1,0:T(8,128)}, f32[4,4,128,128]{3,2,1,0:T(8,128)S(1)}) custom-call(f32[4,8,256,128]{3,2,1,0:T(8,128)S(1)} %copy-done.37, f32[4,8,2,16,128]{4,3,2,1,0:T(8,128)S(1)} %collective-permute-done.4.l_ref._, f32[4,8,2,16,128]{4,3,2,1,0:T(8,128)S(1)} %collective-permute-done.5.r_ref), custom_call_target="tpu_custom_call" | custom-call | flops 4294967296 | bytes 10485760 | tf_op jit(solution)/shard_map/pallas_call | solution.py:435
  67.9 2.0 %shard_map.235 = f32[4,256,1024]{2,1,0:T(8,128)} custom-call(f32[4,256,1024]{2,1,0:T(8,128)} %get-tuple-element.44._, f32[4,4,128,128]{3,2,1,0:T(8,128)S(1)} %get-tuple-element.45.even_ref, f32[4,64,512]{2,1,0:T(8,128)S(1)} %get-tuple-element.50.o1_ref, f32[4,16,256]{2,1,0:T(8,128)S(1)} %get-tuple-element.51.o2_ref, ...), custom_call_target="tpu_custom_call", output_to_operand_aliasing={{}: (0, {})} | custom-call | flops 1073741824 | bytes 11680768 | tf_op jit(solution)/shard_map/pallas_call | solution.py:435
  (98 shorter events, 9.3 us)
Async XLA Ops:
  0.0 11.2 %copy-start.15 = (bf16[512,256]{1,0:T(8,128)(2,1)S(1)}, bf16[512,256]{1,0:T(8,128)(2,1)}, u32[]{:S(2)}) copy-start(bf16[512,256]{1,0:T(8,128)(2,1)} %constant.51.clone.t12l) | copy-start | bytes 786436
  0.0 11.2 %copy-start.17 = (bf16[512,256]{1,0:T(8,128)(2,1)S(1)}, bf16[512,256]{1,0:T(8,128)(2,1)}, u32[]{:S(2)}) copy-start(bf16[512,256]{1,0:T(8,128)(2,1)} %constant.50.clone.t12h) | copy-start | bytes 786436
  0.0 11.2 %copy-start.19 = (bf16[128,1024]{1,0:T(8,128)(2,1)S(1)}, bf16[128,1024]{1,0:T(8,128)(2,1)}, u32[]{:S(2)}) copy-start(bf16[128,1024]{1,0:T(8,128)(2,1)} %constant.68.clone.rims) | copy-start | bytes 786436
  0.0 11.2 %copy-start.21 = (bf16[256,256]{1,0:T(8,128)(2,1)S(1)}, bf16[256,256]{1,0:T(8,128)(2,1)}, u32[]{:S(2)}) copy-start(bf16[256,256]{1,0:T(8,128)(2,1)} %constant.47.clone.txl) | copy-start | bytes 393220
  0.0 11.2 %copy-start.22 = (bf16[256,256]{1,0:T(8,128)(2,1)S(1)}, bf16[256,256]{1,0:T(8,128)(2,1)}, u32[]{:S(2)}) copy-start(bf16[256,256]{1,0:T(8,128)(2,1)} %constant.46.clone.txh) | copy-start | bytes 393220
  2.7 27.5 %collective-permute-start = (f32[4,2,16,1024]{3,2,1,0:T(8,128)}, f32[4,2,16,1024]{3,2,1,0:T(8,128)S(1)}, u32[]{:S(2)}, u32[]{:S(2)}) collective-permute-start(f32[4,2,16,1024]{3,2,1,0:T(8,128)} %get-tuple-element.35), channel_id=1, source_target_pairs={{0,8},{8,16},{16,24},{24,32},{32,40},{40,48},{48,56},{56,64},{64,7... | collective-permute-start | bytes 1572872 | tf_op jit(solution)/shard_map/ppermute | solution.py:449
  4.3 25.9 %collective-permute-start.1 = (f32[4,2,16,1024]{3,2,1,0:T(8,128)}, f32[4,2,16,1024]{3,2,1,0:T(8,128)S(1)}, u32[]{:S(2)}, u32[]{:S(2)}) collective-permute-start(f32[4,2,16,1024]{3,2,1,0:T(8,128)} %get-tuple-element.36), channel_id=1, source_target_pairs={{0,248},{8,0},{16,8},{24,16},{32,24},{40,32},{48,40},{56,48},{64,5... | collective-permute-start | bytes 1572872 | tf_op jit(solution)/shard_map/ppermute | solution.py:449
  11.2 11.5 %copy-start.26 = (bf16[192,256]{1,0:T(8,128)(2,1)S(1)}, bf16[192,256]{1,0:T(8,128)(2,1)}, u32[]{:S(2)}) copy-start(bf16[192,256]{1,0:T(8,128)(2,1)} %constant.55.clone.zol) | copy-start | bytes 294916
  11.2 11.5 %copy-start.27 = (bf16[192,256]{1,0:T(8,128)(2,1)S(1)}, bf16[192,256]{1,0:T(8,128)(2,1)}, u32[]{:S(2)}) copy-start(bf16[192,256]{1,0:T(8,128)(2,1)} %constant.54.clone.zoh) | copy-start | bytes 294916
  11.2 11.4 %copy-start.30 = (bf16[112,128]{1,0:T(8,128)(2,1)S(1)}, bf16[112,128]{1,0:T(8,128)(2,1)}, u32[]{:S(2)}) copy-start(bf16[112,128]{1,0:T(8,128)(2,1)} %constant.57.clone.c1l) | copy-start | bytes 86020
  11.2 11.4 %copy-start.31 = (bf16[112,128]{1,0:T(8,128)(2,1)S(1)}, bf16[112,128]{1,0:T(8,128)(2,1)}, u32[]{:S(2)}) copy-start(bf16[112,128]{1,0:T(8,128)(2,1)} %constant.56.clone.c1h) | copy-start | bytes 86020
  11.3 11.4 %copy-start.34 = (bf16[64,64]{1,0:T(8,128)(2,1)S(1)}, bf16[64,64]{1,0:T(8,128)(2,1)}, u32[]{:S(2)}) copy-start(bf16[64,64]{1,0:T(8,128)(2,1)} %constant.59.clone.c2l) | copy-start | bytes 24580
  11.3 11.4 %copy-start.35 = (bf16[64,64]{1,0:T(8,128)(2,1)S(1)}, bf16[64,64]{1,0:T(8,128)(2,1)}, u32[]{:S(2)}) copy-start(bf16[64,64]{1,0:T(8,128)(2,1)} %constant.58.clone.c2h) | copy-start | bytes 24580
  19.4 8.4 %collective-permute-start.2 = (f32[4,16,512]{2,1,0:T(8,128)S(1)}, f32[4,16,512]{2,1,0:T(8,128)S(1)}, u32[]{:S(2)}, u32[]{:S(2)}) collective-permute-start(f32[4,16,512]{2,1,0:T(8,128)S(1)} %get-tuple-element.41), channel_id=1, source_target_pairs={{0,2},{1,3},{2,4},{3,5},{4,6},{5,7},{6,0},{7,1},{8,10},{9,11},{10,... | collective-permute-start | bytes 393224 | tf_op jit(solution)/shard_map/ppermute | solution.py:449
  20.9 23.5 %collective-permute-start.6 = (f32[4,64,512]{2,1,0:T(8,128)S(1)}, f32[4,64,512]{2,1,0:T(8,128)S(1)}, u32[]{:S(2)}, u32[]{:S(2)}) collective-permute-start(f32[4,64,512]{2,1,0:T(8,128)S(1)} %get-tuple-element.48), channel_id=1, source_target_pairs={{0,1},{1,2},{2,3},{3,4},{4,5},{5,6},{6,7},{7,0},{8,9},{9,10},{10,1... | collective-permute-start | bytes 1572872 | tf_op jit(solution)/shard_map/ppermute | solution.py:449
  20.9 23.5 %collective-permute-start.7 = (f32[4,64,512]{2,1,0:T(8,128)S(1)}, f32[4,64,512]{2,1,0:T(8,128)S(1)}, u32[]{:S(2)}, u32[]{:S(2)}) collective-permute-start(f32[4,64,512]{2,1,0:T(8,128)S(1)} %get-tuple-element.49), channel_id=1, source_target_pairs={{0,7},{1,0},{2,1},{3,2},{4,3},{5,4},{6,5},{7,6},{8,15},{9,8},{10,9... | collective-permute-start | bytes 1572872 | tf_op jit(solution)/shard_map/ppermute | solution.py:449
  28.5 13.5 %collective-permute-start.3 = (f32[4,16,512]{2,1,0:T(8,128)}, f32[4,16,512]{2,1,0:T(8,128)S(1)}, u32[]{:S(2)}, u32[]{:S(2)}) collective-permute-start(f32[4,16,512]{2,1,0:T(8,128)} %shard_map.230), channel_id=1, source_target_pairs={{0,6},{1,7},{2,0},{3,1},{4,2},{5,3},{6,4},{7,5},{8,14},{9,15},{10,... | collective-permute-start | bytes 393224 | tf_op jit(solution)/shard_map/ppermute | solution.py:449
  42.7 16.0 %collective-permute-start.4 = (f32[4,8,2,16,128]{4,3,2,1,0:T(8,128)}, f32[4,8,2,16,128]{4,3,2,1,0:T(8,128)S(1)}, u32[]{:S(2)}, u32[]{:S(2)}) collective-permute-start(f32[4,8,2,16,128]{4,3,2,1,0:T(8,128)} %get-tuple-element.42), channel_id=1, source_target_pairs={{0,1},{1,2},{2,3},{3,4},{4,5},{5,6},{6,7},{7,0},{8,9},{9,10},{10,1... | collective-permute-start | bytes 1572872 | tf_op jit(solution)/shard_map/ppermute | solution.py:449
  42.7 21.8 %collective-permute-start.5 = (f32[4,8,2,16,128]{4,3,2,1,0:T(8,128)}, f32[4,8,2,16,128]{4,3,2,1,0:T(8,128)S(1)}, u32[]{:S(2)}, u32[]{:S(2)}) collective-permute-start(f32[4,8,2,16,128]{4,3,2,1,0:T(8,128)} %get-tuple-element.43), channel_id=1, source_target_pairs={{0,7},{1,0},{2,1},{3,2},{4,3},{5,4},{6,5},{7,6},{8,15},{9,8},{10,9... | collective-permute-start | bytes 1572872 | tf_op jit(solution)/shard_map/ppermute | solution.py:449
  51.7 12.8 %copy-start.37 = (f32[4,8,256,128]{3,2,1,0:T(8,128)S(1)}, f32[4,8,256,128]{3,2,1,0:T(8,128)}, u32[]{:S(2)}) copy-start(f32[4,8,256,128]{3,2,1,0:T(8,128)} %copy-done.36) | copy-start | bytes 12582916
  53.3 14.5 %collective-permute-start.8 = (f32[4,32,512]{2,1,0:T(8,128)S(1)}, f32[4,32,512]{2,1,0:T(8,128)S(1)}, u32[]{:S(2)}, u32[]{:S(2)}) collective-permute-start(f32[4,32,512]{2,1,0:T(8,128)S(1)} %get-tuple-element.52), channel_id=1, source_target_pairs={{0,8},{8,16},{16,24},{24,32},{32,40},{40,48},{48,56},{56,64},{64,7... | collective-permute-start | bytes 786440 | tf_op jit(solution)/shard_map/ppermute | solution.py:449
  53.4 14.5 %collective-permute-start.9 = (f32[4,32,512]{2,1,0:T(8,128)S(1)}, f32[4,32,512]{2,1,0:T(8,128)S(1)}, u32[]{:S(2)}, u32[]{:S(2)}) collective-permute-start(f32[4,32,512]{2,1,0:T(8,128)S(1)} %get-tuple-element.53), channel_id=1, source_target_pairs={{0,248},{8,0},{16,8},{24,16},{32,24},{40,32},{48,40},{56,48},{64,5... | collective-permute-start | bytes 786440 | tf_op jit(solution)/shard_map/ppermute | solution.py:449
  58.7 9.1 %collective-permute-start.10 = (f32[4,8,256]{2,1,0:T(8,128)S(1)}, f32[4,8,256]{2,1,0:T(8,128)S(1)}, u32[]{:S(2)}, u32[]{:S(2)}) collective-permute-start(f32[4,8,256]{2,1,0:T(8,128)S(1)} %get-tuple-element.55), channel_id=1, source_target_pairs={{0,16},{8,24},{16,32},{24,40},{32,48},{40,56},{48,64},{56,72},{64,... | collective-permute-start | bytes 98312 | tf_op jit(solution)/shard_map/ppermute | solution.py:449
  58.8 9.0 %collective-permute-start.11 = (f32[4,8,256]{2,1,0:T(8,128)S(1)}, f32[4,8,256]{2,1,0:T(8,128)S(1)}, u32[]{:S(2)}, u32[]{:S(2)}) collective-permute-start(f32[4,8,256]{2,1,0:T(8,128)S(1)} %get-tuple-element.56), channel_id=1, source_target_pairs={{0,240},{8,248},{16,0},{24,8},{32,16},{40,24},{48,32},{56,40},{64,... | collective-permute-start | bytes 98312 | tf_op jit(solution)/shard_map/ppermute | solution.py:449
  (32 other events, 89.1 us)

commit v4 on v3

--- a/solution.py
+++ b/solution.py
@@ -99,8 +99,7 @@
     def planes(send):
         return np.einsum("pz,ab->paBz".replace("B", "b"), send, eye(ROWS)).reshape(-1, ROWS * ROWS)
 
-    out["zsend"] = stack(*[planes(send[s]) for send in (send1, send2, send22) for s in sides])
-    out["zown"] = stack(np.kron(eye(ROWS), second[0]), np.kron(eye(ROWS), third[0]))
+    zsend = [planes(send[s]) for send in (send1, send2, send22) for s in sides]
 
     def back(give):
         return np.einsum("zp,ab->azpb", give, eye(ROWS)).reshape(ROWS * give.shape[0], -1)
@@ -108,14 +107,16 @@
     zgive1 = np.concatenate([back(give1[s]) for s in sides], 1)
     zgive2a = np.concatenate([back(give2a[s]) for s in sides], 1)
     zgive2b = np.concatenate([back(give2b[s]) for s in sides] + [back(give22[s]) for s in sides], 1)
-    out["ychain1"] = stack(np.kron(second[0], eye(8)), *[np.kron(send1[s], eye(8)) for s in sides])
-    out["ychain2"] = stack(
+    ychain1 = stack(np.kron(second[0], eye(8)), *[np.kron(send1[s], eye(8)) for s in sides])
+    ychain2 = stack(
         np.kron(third[0], eye(4)),
         *[np.kron(send2d[s], eye(4)) for s in sides],
         *[np.kron(send22[s], eye(4)) for s in sides],
     )
-    out["chain1"] = stack(out["ychain1"] @ zgive1, out["ychain2"] @ zgive2a)
-    out["chain2"] = out["ychain2"] @ zgive2b
+    own1, own2 = np.kron(eye(ROWS), second[0]), np.kron(eye(ROWS), third[0])
+    out["zsend"] = stack(*zsend, ychain2 @ own2, ychain1 @ own1)
+    out["chain1"] = stack(ychain1 @ zgive1, ychain2 @ zgive2a)
+    out["chain2"] = ychain2 @ zgive2b
     out["ygive1"] = np.concatenate([np.kron(give1[s], eye(8)) for s in sides], 1)
     out["ygive2"] = np.concatenate(
         [np.kron(give2[s], eye(4)) for s in sides] + [np.kron(give22[s], eye(4)) for s in sides], 1
@@ -195,24 +196,27 @@
         store(j, right([part[:, lanes] for part in parts], table) + dot(rims, rims_ref[:, lanes]))
 
 
-def edge_kernel(x_ref, to_right_ref, to_left_ref, rows_ref, sems):
+def edge_kernel(x_ref, to_right_ref, to_left_ref, head_ref, rows_ref, sems, head_sem):
     comps = x_ref.shape[0]
     copies = []
     for c in range(comps):
         copies.append(pltpu.make_async_copy(x_ref.at[c, pl.ds(0, 3)], rows_ref.at[c, pl.ds(0, 3)], sems.at[c, 0]))
         copies.append(pltpu.make_async_copy(x_ref.at[c, pl.ds(12, 4)], rows_ref.at[c, pl.ds(3, 4)], sems.at[c, 1]))
+    head = pltpu.make_async_copy(x_ref.at[0], head_ref, head_sem)
     for copy in copies:
         copy.start()
+    head.start()
     for c in range(comps):
         copies[2 * c].wait()
         to_left_ref[c, 0], to_left_ref[c, 1] = give_left([rows_ref[c, k] for k in range(3)])
         copies[2 * c + 1].wait()
         to_right_ref[c, 0], to_right_ref[c, 1] = give_right([rows_ref[c, k] for k in range(3, 7)])
+    head.wait()
 
 
 def lift_kernel(
-    x_ref, txh, txl, rims, zsh, zsl, t12h, t12l,
-    u_ref, high_ref, low_ref, r1_ref, l1_ref, r2_ref, l2_ref, cells_ref, far_ref, sems,
+    x_ref, head_ref, txh, txl, rims, zsh, zsl, t12h, t12l,
+    u_ref, first_ref, second_ref, r1_ref, l1_ref, r2_ref, l2_ref, cells_ref, high_ref, low_ref, far_ref, sems,
 ):
     comps, _, nx = x_ref.shape
     blocks, quarter = nx // 256, nx // 4
@@ -220,57 +224,40 @@
     def copy(c):
         return pltpu.make_async_copy(x_ref.at[c], cells_ref.at[c], sems.at[c])
 
-    copy(0).start()
-    copy(1).start()
-
-    def step(c, _):
-        copy(c).wait()
-
-        @pl.when(c + 2 < comps)
-        def _():
-            copy(c + 2).start()
-
+    for c in range(1, comps):
+        copy(c).start()
+
+    def part(c, cells):
         def store(j, value):
             u_ref[c, j] = value[:, :128]
             u_ref[c, blocks + j] = value[:, 128:]
             high, low = split(value[:, :128])
-            high_ref[c, :, 128 * j : 128 * j + 128] = high
-            low_ref[c, :, 128 * j : 128 * j + 128] = low
-
-        lift_x(cells_ref[c], both(txh, txl), rims, store)
-        rows = left(both(zsh, zsl), (high_ref[c], low_ref[c]))
+            high_ref[:, 128 * j : 128 * j + 128] = high
+            low_ref[:, 128 * j : 128 * j + 128] = low
+
+        lift_x(cells, both(txh, txl), rims, store)
+        rows = left(both(zsh, zsl), both(high_ref, low_ref))
         r1_ref[c, :48] = rows[:48]
         l1_ref[c, :48] = rows[48:96]
-        far_ref[c] = rows[96:]
+        far_ref[c] = rows[96:288]
+        first_ref[c] = rows[288:]
+
+    def step(c, _):
+        copy(c).wait()
+        part(c, cells_ref[c])
         return 0
 
-    lax.fori_loop(0, comps, step, 0)
-    far = right(split(far_ref[...].reshape(128 * comps, nx // 2)), both(t12h, t12l))
+    part(0, head_ref[...])
+    lax.fori_loop(1, comps, step, 0)
+    far = right(split(far_ref[...].reshape(192 * comps, nx // 2)), both(t12h, t12l))
     for c in range(comps):
         for k, (ref, ref2) in enumerate(((r1_ref, r2_ref), (l1_ref, l2_ref))):
             for p in range(2):
                 lanes = slice(quarter * p, quarter * p + quarter)
-                at = 128 * c + 32 * k + 16 * p
+                at = 192 * c + 32 * k + 16 * p
                 ref[c, 48:, lanes] = far[at : at + 16]
                 ref2[c, :, lanes] = far[at + 64 : at + 80]
-
-
-def own_kernel(
-    high_ref, low_ref, zoh, zol, t12h, t12l, c1h, c1l, c2h, c2l, first_ref, second_ref, token_ref, far_ref,
-):
-    comps, _, half = high_ref.shape
-    token_ref[...] = jnp.zeros_like(token_ref)
-
-    def step(c, _):
-        rows = left(both(zoh, zol), (high_ref[c], low_ref[c]))
-        first_ref[c] = left(both(c1h, c1l), split(rows[:128]))
-        far_ref[c] = rows[128:]
-        return 0
-
-    lax.fori_loop(0, comps, step, 0)
-    far = right(split(far_ref[...].reshape(64 * comps, half)), both(t12h, t12l))
-    for c in range(comps):
-        second_ref[c] = left(both(c2h, c2l), split(far[64 * c : 64 * c + 64]))
+        second_ref[c] = far[192 * c + 128 : 192 * c + 192]
 
 
 def chain_kernel(
@@ -308,7 +295,7 @@
         away_ref[c] = second[48:]
 
 
-def along_y_kernel(_, u_ref, l_ref, r_ref, txh, txl, rims, b_ref, to_r_ref, to_l_ref, halo_ref):
+def along_y_kernel(_, _2, u_ref, l_ref, r_ref, txh, txl, rims, b_ref, to_r_ref, to_l_ref, halo_ref):
     comps, lanes = u_ref.shape[:2]
     blocks = lanes // 2
 
@@ -336,21 +323,6 @@
         return 0
 
     lax.fori_loop(0, comps * lanes, step, 0)
-
-
-def after(values, earlier):
-    count = len(values)
-
-    def body(*refs):
-        pass
-
-    return pl.pallas_call(
-        body,
-        in_specs=[pl.BlockSpec(memory_space=pl.ANY)] * (count + len(earlier)),
-        out_specs=[pl.BlockSpec(memory_space=pl.ANY)] * count,
-        out_shape=[jax.ShapeDtypeStruct(v.shape, v.dtype) for v in values],
-        input_output_aliases={n: n for n in range(count)},
-    )(*values, *earlier)
 
 
 def away_kernel(_, away_ref, to_r2_ref, to_l2_ref):
@@ -465,11 +437,11 @@
         return pltpu.SemaphoreType.DMA(shape)
 
     edge = ((comps, 2, ROWS, nx), F32)
-    y_right, y_left = call(
+    y_right, y_left, head = call(
         edge_kernel,
         [field],
-        [edge] * 2,
-        [pltpu.VMEM((comps, 7, ROWS, nx), F32), dma(comps, 2)],
+        [edge] * 2 + [((ROWS, ROWS, nx), F32)],
+        [pltpu.VMEM((comps, 7, ROWS, nx), F32), dma(comps, 2), pltpu.SemaphoreType.DMA],
         hbm_in=(0,),
     )
     from_left0 = move(y_right, "gy", 1)
@@ -478,38 +450,33 @@
     near = ((comps, 64, half), F32)
     far = ((comps, 16, half), F32)
     cells = ((comps, lanes, ROWS * ROWS, 128), F32)
-    u, high, low, z_right, z_left, z_right2, z_left2 = call(
+    u, first, second, z_right, z_left, z_right2, z_left2 = call(
         lift_kernel,
-        [flat] + consts("tx", "rims", "zsend", "tx12"),
-        [cells] + [((comps, ROWS * ROWS, half), BF16)] * 2 + [near] * 2 + [far] * 2,
-        [pltpu.VMEM((comps, ROWS * ROWS, nx), F32), pltpu.VMEM((comps, 128, half), F32), dma(comps)],
+        [flat, head.reshape(ROWS * ROWS, nx)] + consts("tx", "rims", "zsend", "tx12"),
+        [cells, ((comps, 112, half), F32), ((comps, 64, quarter), F32)] + [near] * 2 + [far] * 2,
+        [
+            pltpu.VMEM((comps, ROWS * ROWS, nx), F32),
+            pltpu.VMEM((ROWS * ROWS, half), BF16),
+            pltpu.VMEM((ROWS * ROWS, half), BF16),
+            pltpu.VMEM((comps, 192, half), F32),
+            dma(comps),
+        ],
         flops=1 << 33,
         hbm_in=(0,),
     )
+    z_from_left2 = move(z_right2, "gz", 2)
     z_from_left = move(z_right, "gz", 1)
     z_from_right = move(z_left, "gz", -1)
-    z_from_left2 = move(z_right2, "gz", 2)
-
-    first, second, token = call(
-        own_kernel,
-        [high, low] + consts("zown", "tx12", "ychain1", "ychain2"),
-        [((comps, 112, half), F32), ((comps, 64, quarter), F32)] + [((8, 128), F32)],
-        [pltpu.VMEM((comps, 64, half), F32)],
-        flops=1 << 32,
-    )
-
-    (z_left2,) = after([z_left2], [token, z_from_left2])
     z_from_right2 = move(z_left2, "gz", -2)
 
     planes = ((comps, lanes, 2, ROWS, 128), F32)
     b, z0_right, z0_left = call(
         along_y_kernel,
-        [token, u, from_left0, from_right0] + consts("tx", "rims"),
+        [z_from_left2, z_from_right2, u, from_left0, from_right0] + consts("tx", "rims"),
         [cells] + [planes] * 2,
         [pltpu.VMEM((lanes, 64 * comps, 128), F32)],
         flops=1 << 32,
     )
-    z0_right, z0_left = after([z0_right, z0_left], [z_from_right2])
     z0_from_left = move(z0_right, "gz", 1)
     z0_from_right = move(z0_left, "gz", -1)
 

time: 70.5 us -> 48.2 us (0.68)
  the two profiles are of different devices: /device:TPU:2 before, /device:TPU:1 now
where the time goes in v4:
time: 48.2 us; the launch traced here: 48.1 us
  starting transfers between devices  26.4 us (55%)
  Pallas kernels  18.1 us (38%)
  waiting for transfers between devices  3.18 us (7%)
    ppermute x12, starting transfers between devices, move(): lax.ppermute(value, axis, [(i, (i + step) % count) for i in range(count)])  26.4 us
    pallas_call x7, Pallas kernels, call(): pl.pallas_call(body, in_specs=[spec(n, hbm_in) for n in range(len(ins))],...  18.1 us
    ppermute x12, waiting for transfers between devices, move(): lax.ppermute(value, axis, [(i, (i + step) % count) for i in range(count)])  3.18 us
  transfers between devices with their start and end apart: 12, of which 2 were waited for; matrix products, arithmetic and copies ran while one was open for 0% of the time, Pallas kernels for 29%

profile of v4, /device:TPU:1, one launch (start us, length us, event | category | flops | bytes accessed | tf_op | source)
XLA Modules:
  0.0 48.1 jit_solution(13773258166728765711)
XLA Ops:
  0.0 0.0 copy-start.7
  0.0 0.0 copy-start.9
  0.0 0.0 copy-start.10
  0.1 2.0 %shard_map.172 = (f32[4,2,16,1024]{3,2,1,0:T(8,128)S(1)}, f32[4,2,16,1024]{3,2,1,0:T(8,128)S(1)}, f32[16,16,1024]{2,1,0:T(8,128)S(1)}) custom-call(f32[4,16,16,1024]{3,2,1,0:T(8,128)} %x_ref.1), custom_call_target="tpu_custom_call" | custom-call | bytes 6291456 | tf_op jit(solution)/shard_map/pallas_call | solution.py:407
  2.1 2.2 %collective-permute-start.2 = (f32[4,2,16,1024]{3,2,1,0:T(8,128)S(1)}, f32[4,2,16,1024]{3,2,1,0:T(8,128)S(1)}, u32[]{:S(2)}, u32[]{:S(2)}) collective-permute-start(f32[4,2,16,1024]{3,2,1,0:T(8,128)S(1)} %get-tuple-element.31), channel_id=1, source_target_pairs={{0,8},{8,16},{16,24},{24,32},{32,40},{40,48},{48,56},{56,64},{64,7... | collective-permute-start | bytes 1572872 | tf_op jit(solution)/shard_map/ppermute | solution.py:421
  4.3 6.8 %collective-permute-start.3 = (f32[4,2,16,1024]{3,2,1,0:T(8,128)S(1)}, f32[4,2,16,1024]{3,2,1,0:T(8,128)S(1)}, u32[]{:S(2)}, u32[]{:S(2)}) collective-permute-start(f32[4,2,16,1024]{3,2,1,0:T(8,128)S(1)} %get-tuple-element.32), channel_id=1, source_target_pairs={{0,248},{8,0},{16,8},{24,16},{32,24},{40,32},{48,40},{56,48},{64,5... | collective-permute-start | bytes 1572872 | tf_op jit(solution)/shard_map/ppermute | solution.py:421
  11.2 5.8 %shard_map.173 = (f32[4,8,256,128]{3,2,1,0:T(8,128)S(1)}, f32[4,112,512]{2,1,0:T(8,128)S(1)}, f32[4,64,256]{2,1,0:T(8,128)S(1)}, f32[4,64,512]{2,1,0:T(8,128)S(1...) custom-call(f32[4,256,1024]{2,1,0:T(8,128)} %bitcast.4, ...), custom_call_target="tpu_custom_call" | custom-call | flops 8589934592 | bytes 13385728 | tf_op jit(solution)/shard_map/pallas_call | solution.py:407
  17.0 1.3 %collective-permute-start = (f32[4,16,512]{2,1,0:T(8,128)S(1)}, f32[4,16,512]{2,1,0:T(8,128)S(1)}, u32[]{:S(2)}, u32[]{:S(2)}) collective-permute-start(f32[4,16,512]{2,1,0:T(8,128)S(1)} %get-tuple-element.28), channel_id=1, source_target_pairs={{0,2},{1,3},{2,4},{3,5},{4,6},{5,7},{6,0},{7,1},{8,10},{9,11},{10,... | collective-permute-start | bytes 393224 | tf_op jit(solution)/shard_map/ppermute | solution.py:421
  18.3 1.5 %collective-permute-start.1 = (f32[4,16,512]{2,1,0:T(8,128)S(1)}, f32[4,16,512]{2,1,0:T(8,128)S(1)}, u32[]{:S(2)}, u32[]{:S(2)}) collective-permute-start(f32[4,16,512]{2,1,0:T(8,128)S(1)} %get-tuple-element.29), channel_id=1, source_target_pairs={{0,6},{1,7},{2,0},{3,1},{4,2},{5,3},{6,4},{7,5},{8,14},{9,15},{10,... | collective-permute-start | bytes 393224 | tf_op jit(solution)/shard_map/ppermute | solution.py:421
  19.7 1.4 %collective-permute-start.6 = (f32[4,64,512]{2,1,0:T(8,128)S(1)}, f32[4,64,512]{2,1,0:T(8,128)S(1)}, u32[]{:S(2)}, u32[]{:S(2)}) collective-permute-start(f32[4,64,512]{2,1,0:T(8,128)S(1)} %get-tuple-element.40), channel_id=1, source_target_pairs={{0,1},{1,2},{2,3},{3,4},{4,5},{5,6},{6,7},{7,0},{8,9},{9,10},{10,1... | collective-permute-start | bytes 1572872 | tf_op jit(solution)/shard_map/ppermute | solution.py:421
  21.1 1.2 %collective-permute-done._.l2_ref = f32[4,16,512]{2,1,0:T(8,128)S(1)} collective-permute-done((f32[4,16,512]{2,1,0:T(8,128)S(1)}, f32[4,16,512]{2,1,0:T(8,128)S(1)}, u32[]{:S(2)}, u32[]{:S(2)}) %collective-permute-start) | collective-permute-done | bytes 131104 | tf_op jit(solution)/shard_map/ppermute | solution.py:421
  22.4 1.8 %collective-permute-start.7 = (f32[4,64,512]{2,1,0:T(8,128)S(1)}, f32[4,64,512]{2,1,0:T(8,128)S(1)}, u32[]{:S(2)}, u32[]{:S(2)}) collective-permute-start(f32[4,64,512]{2,1,0:T(8,128)S(1)} %get-tuple-element.41), channel_id=1, source_target_pairs={{0,7},{1,0},{2,1},{3,2},{4,3},{5,4},{6,5},{7,6},{8,15},{9,8},{10,9... | collective-permute-start | bytes 1572872 | tf_op jit(solution)/shard_map/ppermute | solution.py:421
  24.2 0.0 copy-start.13
  24.2 0.0 copy-start.14
  24.2 3.4 %shard_map.174 = (f32[4,8,256,128]{3,2,1,0:T(8,128)S(1)}, f32[4,8,2,16,128]{4,3,2,1,0:T(8,128)S(1)}, f32[4,8,2,16,128]{4,3,2,1,0:T(8,128)S(1)}) custom-call(f32[4,16,512]{2,1,0:T(8,128)S(1)} %collective-permute-done._.l2_ref, f32[4,16,512]{2,1,0:T(8,128)S(1)} %collective-permute-done.1._2.r2_ref, f32[4,8,256,128]{3,2,1,0:T(8,128)S(1)} %get-tuple-element.30.u_ref, ...), custom_call_target="tpu_custom_call" | custom-call | flops 4294967296 | bytes 11272192 | tf_op jit(solution)/shard_map/pallas_call | solution.py:407
  27.7 1.4 %collective-permute-start.4 = (f32[4,8,2,16,128]{4,3,2,1,0:T(8,128)S(1)}, f32[4,8,2,16,128]{4,3,2,1,0:T(8,128)S(1)}, u32[]{:S(2)}, u32[]{:S(2)}) collective-permute-start(f32[4,8,2,16,128]{4,3,2,1,0:T(8,128)S(1)} %get-tuple-element.34), channel_id=1, source_target_pairs={{0,1},{1,2},{2,3},{3,4},{4,5},{5,6},{6,7},{7,0},{8,9},{9,10},{10,1... | collective-permute-start | bytes 1572872 | tf_op jit(solution)/shard_map/ppermute | solution.py:421
  29.0 1.9 %collective-permute-done.7.r1_ref = f32[4,64,512]{2,1,0:T(8,128)S(1)} collective-permute-done((f32[4,64,512]{2,1,0:T(8,128)S(1)}, f32[4,64,512]{2,1,0:T(8,128)S(1)}, u32[]{:S(2)}, u32[]{:S(2)}) %collective-permute-start.7) | collective-permute-done | bytes 524320 | tf_op jit(solution)/shard_map/ppermute | solution.py:421
  31.0 1.6 %shard_map.176 = (f32[4,64,512]{2,1,0:T(8,128)S(1)}, f32[4,16,256]{2,1,0:T(8,128)S(1)}, f32[4,32,512]{2,1,0:T(8,128)S(1)}, f32[4,32,512]{2,1,0:T(8,128)S(1)}, f32[4,16,256]{2,1,0:T(8,128)S(1)}) custom-call(f32[4,112,512]{2,1,0:T(8,128)S(1)} %get-tuple-element.38.first_ref, f32[4,64,256]{2,1,0:T(8,128)S(1)} %get-tuple-element.39.second_ref, ...), custom_call_target="tpu_custom_call" | custom-call | flops 2147483648 | bytes 4294656 | tf_op jit(solution)/shard_map/pallas_call | solution.py:407
  32.6 0.1 collective-permute-start.8
  32.7 4.8 %collective-permute-start.9 = (f32[4,32,512]{2,1,0:T(8,128)S(1)}, f32[4,32,512]{2,1,0:T(8,128)S(1)}, u32[]{:S(2)}, u32[]{:S(2)}) collective-permute-start(f32[4,32,512]{2,1,0:T(8,128)S(1)} %get-tuple-element.45), channel_id=1, source_target_pairs={{0,248},{8,0},{16,8},{24,16},{32,24},{40,32},{48,40},{56,48},{64,5... | collective-permute-start | bytes 786440 | tf_op jit(solution)/shard_map/ppermute | solution.py:421
  37.5 0.1 collective-permute-start.10
  37.6 5.1 %collective-permute-start.11 = (f32[4,8,256]{2,1,0:T(8,128)S(1)}, f32[4,8,256]{2,1,0:T(8,128)S(1)}, u32[]{:S(2)}, u32[]{:S(2)}) collective-permute-start(f32[4,8,256]{2,1,0:T(8,128)S(1)} %get-tuple-element.48), channel_id=1, source_target_pairs={{0,240},{8,248},{16,0},{24,8},{32,16},{40,24},{48,32},{56,40},{64,... | collective-permute-start | bytes 98312 | tf_op jit(solution)/shard_map/ppermute | solution.py:421
  42.7 3.3 %shard_map.175 = (f32[4,256,1024]{2,1,0:T(8,128)}, f32[4,4,128,128]{3,2,1,0:T(8,128)S(1)}) custom-call(f32[4,8,256,128]{3,2,1,0:T(8,128)S(1)} %get-tuple-element.33.b_ref, f32[4,8,2,16,128]{4,3,2,1,0:T(8,128)S(1)} %collective-permute-done.4.l_ref._, f32[4,8,2,16,128]{4,3,2,1,0:T(8,128)S(1)} %collective-permute-done.5.r_ref), custom_call_target="tpu_custom_call" | custom-call | flops 4294967296 | bytes 10485760 | tf_op jit(solution)/shard_map/pallas_call | solution.py:407
  46.1 2.0 %shard_map.178 = f32[4,256,1024]{2,1,0:T(8,128)} custom-call(f32[4,256,1024]{2,1,0:T(8,128)} %get-tuple-element.36._, f32[4,4,128,128]{3,2,1,0:T(8,128)S(1)} %get-tuple-element.37.even_ref, f32[4,64,512]{2,1,0:T(8,128)S(1)} %get-tuple-element.42.o1_ref, f32[4,16,256]{2,1,0:T(8,128)S(1)} %get-tuple-element.43.o2_ref, ...), custom_call_target="tpu_custom_call", output_to_operand_aliasing={{}: (0, {})} | custom-call | flops 1073741824 | bytes 11680768 | tf_op jit(solution)/shard_map/pallas_call | solution.py:407
  (41 shorter events, 0.1 us)
Async XLA Ops:
  0.0 11.1 %copy-start.11 = (bf16[256,256]{1,0:T(8,128)(2,1)S(1)}, bf16[256,256]{1,0:T(8,128)(2,1)}, u32[]{:S(2)}) copy-start(bf16[256,256]{1,0:T(8,128)(2,1)} %constant.34.clone.txh) | copy-start | bytes 393220
  0.0 11.1 %copy-start.12 = (bf16[256,256]{1,0:T(8,128)(2,1)S(1)}, bf16[256,256]{1,0:T(8,128)(2,1)}, u32[]{:S(2)}) copy-start(bf16[256,256]{1,0:T(8,128)(2,1)} %constant.35.clone.txl) | copy-start | bytes 393220
  0.0 11.1 %copy-start.6 = (bf16[512,256]{1,0:T(8,128)(2,1)S(1)}, bf16[512,256]{1,0:T(8,128)(2,1)}, u32[]{:S(2)}) copy-start(bf16[512,256]{1,0:T(8,128)(2,1)} %constant.38.clone.t12h) | copy-start | bytes 786436
  0.0 11.1 %copy-start.7 = (bf16[512,256]{1,0:T(8,128)(2,1)S(1)}, bf16[512,256]{1,0:T(8,128)(2,1)}, u32[]{:S(2)}) copy-start(bf16[512,256]{1,0:T(8,128)(2,1)} %constant.39.clone.t12l) | copy-start | bytes 786436
  0.0 11.1 %copy-start.9 = (bf16[400,256]{1,0:T(8,128)(2,1)S(1)}, bf16[400,256]{1,0:T(8,128)(2,1)}, u32[]{:S(2)}) copy-start(bf16[400,256]{1,0:T(8,128)(2,1)} %constant.40.clone.zsh) | copy-start | bytes 614404
  0.0 11.1 %copy-start.10 = (bf16[400,256]{1,0:T(8,128)(2,1)S(1)}, bf16[400,256]{1,0:T(8,128)(2,1)}, u32[]{:S(2)}) copy-start(bf16[400,256]{1,0:T(8,128)(2,1)} %constant.41.clone.zsl) | copy-start | bytes 614404
  0.0 11.1 %copy-start.8 = (bf16[128,1024]{1,0:T(8,128)(2,1)S(1)}, bf16[128,1024]{1,0:T(8,128)(2,1)}, u32[]{:S(2)}) copy-start(bf16[128,1024]{1,0:T(8,128)(2,1)} %constant.50.clone.rims) | copy-start | bytes 786436
  2.1 22.1 %collective-permute-start.2 = (f32[4,2,16,1024]{3,2,1,0:T(8,128)S(1)}, f32[4,2,16,1024]{3,2,1,0:T(8,128)S(1)}, u32[]{:S(2)}, u32[]{:S(2)}) collective-permute-start(f32[4,2,16,1024]{3,2,1,0:T(8,128)S(1)} %get-tuple-element.31), channel_id=1, source_target_pairs={{0,8},{8,16},{16,24},{24,32},{32,40},{40,48},{48,56},{56,64},{64,7... | collective-permute-start | bytes 1572872 | tf_op jit(solution)/shard_map/ppermute | solution.py:421
  4.3 19.9 %collective-permute-start.3 = (f32[4,2,16,1024]{3,2,1,0:T(8,128)S(1)}, f32[4,2,16,1024]{3,2,1,0:T(8,128)S(1)}, u32[]{:S(2)}, u32[]{:S(2)}) collective-permute-start(f32[4,2,16,1024]{3,2,1,0:T(8,128)S(1)} %get-tuple-element.32), channel_id=1, source_target_pairs={{0,248},{8,0},{16,8},{24,16},{32,24},{40,32},{48,40},{56,48},{64,5... | collective-permute-start | bytes 1572872 | tf_op jit(solution)/shard_map/ppermute | solution.py:421
  17.0 5.4 %collective-permute-start = (f32[4,16,512]{2,1,0:T(8,128)S(1)}, f32[4,16,512]{2,1,0:T(8,128)S(1)}, u32[]{:S(2)}, u32[]{:S(2)}) collective-permute-start(f32[4,16,512]{2,1,0:T(8,128)S(1)} %get-tuple-element.28), channel_id=1, source_target_pairs={{0,2},{1,3},{2,4},{3,5},{4,6},{5,7},{6,0},{7,1},{8,10},{9,11},{10,... | collective-permute-start | bytes 393224 | tf_op jit(solution)/shard_map/ppermute | solution.py:421
  18.3 5.9 %collective-permute-start.1 = (f32[4,16,512]{2,1,0:T(8,128)S(1)}, f32[4,16,512]{2,1,0:T(8,128)S(1)}, u32[]{:S(2)}, u32[]{:S(2)}) collective-permute-start(f32[4,16,512]{2,1,0:T(8,128)S(1)} %get-tuple-element.29), channel_id=1, source_target_pairs={{0,6},{1,7},{2,0},{3,1},{4,2},{5,3},{6,4},{7,5},{8,14},{9,15},{10,... | collective-permute-start | bytes 393224 | tf_op jit(solution)/shard_map/ppermute | solution.py:421
  19.7 9.3 %collective-permute-start.6 = (f32[4,64,512]{2,1,0:T(8,128)S(1)}, f32[4,64,512]{2,1,0:T(8,128)S(1)}, u32[]{:S(2)}, u32[]{:S(2)}) collective-permute-start(f32[4,64,512]{2,1,0:T(8,128)S(1)} %get-tuple-element.40), channel_id=1, source_target_pairs={{0,1},{1,2},{2,3},{3,4},{4,5},{5,6},{6,7},{7,0},{8,9},{9,10},{10,1... | collective-permute-start | bytes 1572872 | tf_op jit(solution)/shard_map/ppermute | solution.py:421
  22.4 8.6 %collective-permute-start.7 = (f32[4,64,512]{2,1,0:T(8,128)S(1)}, f32[4,64,512]{2,1,0:T(8,128)S(1)}, u32[]{:S(2)}, u32[]{:S(2)}) collective-permute-start(f32[4,64,512]{2,1,0:T(8,128)S(1)} %get-tuple-element.41), channel_id=1, source_target_pairs={{0,7},{1,0},{2,1},{3,2},{4,3},{5,4},{6,5},{7,6},{8,15},{9,8},{10,9... | collective-permute-start | bytes 1572872 | tf_op jit(solution)/shard_map/ppermute | solution.py:421
  24.2 6.8 %copy-start.13 = (bf16[176,96]{1,0:T(8,128)(2,1)S(1)}, bf16[176,96]{1,0:T(8,128)(2,1)}, u32[]{:S(2)}) copy-start(bf16[176,96]{1,0:T(8,128)(2,1)} %constant.42.clone.g1h) | copy-start | bytes 101380
  24.2 6.8 %copy-start.14 = (bf16[176,96]{1,0:T(8,128)(2,1)S(1)}, bf16[176,96]{1,0:T(8,128)(2,1)}, u32[]{:S(2)}) copy-start(bf16[176,96]{1,0:T(8,128)(2,1)} %constant.43.clone.g1l) | copy-start | bytes 101380
  24.2 6.8 %copy-start.15 = (bf16[64,128]{1,0:T(8,128)(2,1)S(1)}, bf16[64,128]{1,0:T(8,128)(2,1)}, u32[]{:S(2)}) copy-start(bf16[64,128]{1,0:T(8,128)(2,1)} %constant.44.clone.g2h) | copy-start | bytes 49156
  24.2 6.7 %copy-start.16 = (bf16[64,128]{1,0:T(8,128)(2,1)S(1)}, bf16[64,128]{1,0:T(8,128)(2,1)}, u32[]{:S(2)}) copy-start(bf16[64,128]{1,0:T(8,128)(2,1)} %constant.45.clone.g2l) | copy-start | bytes 49156
  27.7 9.8 %collective-permute-start.4 = (f32[4,8,2,16,128]{4,3,2,1,0:T(8,128)S(1)}, f32[4,8,2,16,128]{4,3,2,1,0:T(8,128)S(1)}, u32[]{:S(2)}, u32[]{:S(2)}) collective-permute-start(f32[4,8,2,16,128]{4,3,2,1,0:T(8,128)S(1)} %get-tuple-element.34), channel_id=1, source_target_pairs={{0,1},{1,2},{2,3},{3,4},{4,5},{5,6},{6,7},{7,0},{8,9},{9,10},{10,1... | collective-permute-start | bytes 1572872 | tf_op jit(solution)/shard_map/ppermute | solution.py:421
  29.0 13.6 %collective-permute-start.5 = (f32[4,8,2,16,128]{4,3,2,1,0:T(8,128)S(1)}, f32[4,8,2,16,128]{4,3,2,1,0:T(8,128)S(1)}, u32[]{:S(2)}, u32[]{:S(2)}) collective-permute-start(f32[4,8,2,16,128]{4,3,2,1,0:T(8,128)S(1)} %get-tuple-element.35), channel_id=1, source_target_pairs={{0,7},{1,0},{2,1},{3,2},{4,3},{5,4},{6,5},{7,6},{8,15},{9,8},{10,9... | collective-permute-start | bytes 1572872 | tf_op jit(solution)/shard_map/ppermute | solution.py:421
  32.6 13.4 %collective-permute-start.8 = (f32[4,32,512]{2,1,0:T(8,128)S(1)}, f32[4,32,512]{2,1,0:T(8,128)S(1)}, u32[]{:S(2)}, u32[]{:S(2)}) collective-permute-start(f32[4,32,512]{2,1,0:T(8,128)S(1)} %get-tuple-element.44), channel_id=1, source_target_pairs={{0,8},{8,16},{16,24},{24,32},{32,40},{40,48},{48,56},{56,64},{64,7... | collective-permute-start | bytes 786440 | tf_op jit(solution)/shard_map/ppermute | solution.py:421
  32.7 13.3 %collective-permute-start.9 = (f32[4,32,512]{2,1,0:T(8,128)S(1)}, f32[4,32,512]{2,1,0:T(8,128)S(1)}, u32[]{:S(2)}, u32[]{:S(2)}) collective-permute-start(f32[4,32,512]{2,1,0:T(8,128)S(1)} %get-tuple-element.45), channel_id=1, source_target_pairs={{0,248},{8,0},{16,8},{24,16},{32,24},{40,32},{48,40},{56,48},{64,5... | collective-permute-start | bytes 786440 | tf_op jit(solution)/shard_map/ppermute | solution.py:421
  37.5 8.6 %collective-permute-start.10 = (f32[4,8,256]{2,1,0:T(8,128)S(1)}, f32[4,8,256]{2,1,0:T(8,128)S(1)}, u32[]{:S(2)}, u32[]{:S(2)}) collective-permute-start(f32[4,8,256]{2,1,0:T(8,128)S(1)} %get-tuple-element.47), channel_id=1, source_target_pairs={{0,16},{8,24},{16,32},{24,40},{32,48},{40,56},{48,64},{56,72},{64,... | collective-permute-start | bytes 98312 | tf_op jit(solution)/shard_map/ppermute | solution.py:421
  37.6 8.5 %collective-permute-start.11 = (f32[4,8,256]{2,1,0:T(8,128)S(1)}, f32[4,8,256]{2,1,0:T(8,128)S(1)}, u32[]{:S(2)}, u32[]{:S(2)}) collective-permute-start(f32[4,8,256]{2,1,0:T(8,128)S(1)} %get-tuple-element.48), channel_id=1, source_target_pairs={{0,240},{8,248},{16,0},{24,8},{32,16},{40,24},{48,32},{56,40},{64,... | collective-permute-start | bytes 98312 | tf_op jit(solution)/shard_map/ppermute | solution.py:421
  42.7 3.4 %copy-start.3 = (bf16[64,48]{1,0:T(8,128)(2,1)S(1)}, bf16[64,48]{1,0:T(8,128)(2,1)}, u32[]{:S(2)}) copy-start(bf16[64,48]{1,0:T(8,128)(2,1)} %constant.47.clone.g1l) | copy-start | bytes 18436
  (5 other events, 17.1 us)

commit v5 on v4

--- a/solution.py
+++ b/solution.py
@@ -248,7 +248,7 @@
         return 0
 
     part(0, head_ref[...])
-    lax.fori_loop(1, comps, step, 0)
+    lax.fori_loop(1, comps, step, 0, unroll=True)
     far = right(split(far_ref[...].reshape(192 * comps, nx // 2)), both(t12h, t12l))
     for c in range(comps):
         for k, (ref, ref2) in enumerate(((r1_ref, r2_ref), (l1_ref, l2_ref))):
@@ -263,7 +263,7 @@
 def chain_kernel(
     first_ref, second_ref, l1_ref, r1_ref, l2_ref, r2_ref,
     g1h, g1l, g2h, g2l, t12h, t12l,
-    o1_ref, o2_ref, to_r_ref, to_l_ref, away_ref, far_ref,
+    o1_ref, o2_ref, to_r_ref, to_l_ref, to_r2_ref, to_l2_ref, far_ref,
 ):
     comps, _, half = first_ref.shape
     quarter = half // 2
@@ -292,11 +292,28 @@
         for k, ref in enumerate((to_r_ref, to_l_ref)):
             ref[c, 24:, :quarter] = second[16 + 16 * k : 24 + 16 * k]
             ref[c, 24:, quarter:] = second[24 + 16 * k : 32 + 16 * k]
-        away_ref[c] = second[48:]
-
-
-def along_y_kernel(_, _2, u_ref, l_ref, r_ref, txh, txl, rims, b_ref, to_r_ref, to_l_ref, halo_ref):
+        to_r2_ref[c] = second[48:56]
+        to_l2_ref[c] = second[56:]
+
+
+def along_y_kernel(u_ref, b_ref):
     comps, lanes = u_ref.shape[:2]
+
+    def step(n, _):
+        c, k = n // lanes, n % lanes
+        u, b = u_ref.at[c, k], b_ref.at[c, k]
+        nothing = [jnp.zeros((8, 128), F32)] * 2
+        for part in range(2):
+            cells = [u[16 * y + 8 * part : 16 * y + 8 * part + 8] for y in range(ROWS)]
+            for y, value in enumerate(lift_line(cells, nothing, nothing)):
+                b[pl.ds(128 * part + y, 8, stride=ROWS)] = value
+        return 0
+
+    lax.fori_loop(0, comps * lanes, step, 0, unroll=2)
+
+
+def rim_kernel(_, _2, own_ref, l_ref, r_ref, txh, txl, rims, b_ref, to_r_ref, to_l_ref, halo_ref, added_ref):
+    comps, lanes = own_ref.shape[:2]
     blocks = lanes // 2
 
     def store(j, value):
@@ -305,29 +322,35 @@
 
     rows = [ref[c, p] for c in range(comps) for ref in (l_ref, r_ref) for p in range(2)]
     lift_x(jnp.concatenate(rows, 0), both(txh, txl), rims, store)
+    added_ref[...] = jnp.zeros_like(added_ref)
+    units = np.eye(4)
+    weights = np.array([lift_line([0.0] * ROWS, list(unit[:2]), list(unit[2:])) for unit in units])
 
     def step(n, _):
         c, k = n // lanes, n % lanes
-        u, b, halo = u_ref.at[c, k], b_ref.at[c, k], halo_ref.at[k]
+        b, halo, added = b_ref.at[c, k], halo_ref.at[k], added_ref.at[n % 2]
         for part in range(2):
-            cells = [u[16 * y + 8 * part : 16 * y + 8 * part + 8] for y in range(ROWS)]
             around = [halo[pl.ds(pl.multiple_of(64 * c + 16 * p + 8 * part, 8), 8)] for p in range(4)]
-            for y, value in enumerate(lift_line(cells, around[:2], around[2:])):
-                b[pl.ds(128 * part + y, 8, stride=ROWS)] = value
+            for y in range(ROWS):
+                terms = [float(weights[p, y]) * around[p] for p in range(4) if weights[p, y] != 0.0]
+                if terms:
+                    added[pl.ds(128 * part + y, 8, stride=ROWS)] = sum(terms[1:], terms[0])
+        for z in range(ROWS):
+            at = slice(16 * z, 16 * z + 16)
+            b[at] = own_ref[c, k, at] + added[at]
 
         def plane(z):
-            return b[16 * z : 16 * z + 16]
+            return own_ref[c, k, 16 * z : 16 * z + 16] + added[16 * z : 16 * z + 16]
 
         to_r_ref[c, k, 0], to_r_ref[c, k, 1] = give_right([plane(z) for z in range(12, 16)])
         to_l_ref[c, k, 0], to_l_ref[c, k, 1] = give_left([plane(z) for z in range(3)])
         return 0
 
-    lax.fori_loop(0, comps * lanes, step, 0)
-
-
-def away_kernel(_, away_ref, to_r2_ref, to_l2_ref):
-    to_r2_ref[...] = away_ref[:, :8]
-    to_l2_ref[...] = away_ref[:, 8:]
+    lax.fori_loop(0, comps * lanes, step, 0, unroll=2)
+
+
+def hand_on_kernel(_, value_ref, out_ref):
+    out_ref[...] = value_ref[...]
 
 
 def along_z_kernel(b_ref, l_ref, r_ref, out_ref, even_ref, done_ref, sems):
@@ -351,11 +374,11 @@
         @pl.when(k < lanes // 2)
         def _():
             for y in range(ROWS // 2):
-                even_ref[c, k, 16 * y : 16 * y + 16] = done[32 * y : 32 * y + 16]
+                even_ref[c, k, y] = done[32 * y : 32 * y + 16]
 
         return 0
 
-    lax.fori_loop(0, comps * lanes, step, 0)
+    lax.fori_loop(0, comps * lanes, step, 0, unroll=2)
     for c in range(comps):
         for k in range(lanes):
             copy(c, k).wait()
@@ -382,18 +405,14 @@
     for c in range(comps):
         for k in range(lanes):
             at = slice(128 * k, 128 * k + 128)
-            done = done_ref.at[c, k]
-            done[...] = even_ref[c, k]
             for y in range(8):
-                done[pl.ds(16 * y, 8, stride=2)] = window[64 * c + 8 * y : 64 * c + 8 * y + 8, at]
+                done_ref[c, k, y] = even_ref[c, k, y]
+                done_ref[c, k, y, pl.ds(0, 8, stride=2)] = window[64 * c + 8 * y : 64 * c + 8 * y + 8, at]
             if 128 * k < quarter:
                 for y in range(4):
-                    done[pl.ds(32 * y, 4, stride=4)] = deepest[c][4 * y : 4 * y + 4, at]
-            for y in range(8):
-                copies.append(
-                    pltpu.make_async_copy(done.at[pl.ds(16 * y, 16)], out_ref.at[c, pl.ds(32 * y, 16), at], sems.at[c])
-                )
-                copies[-1].start()
+                    done_ref[c, k, 2 * y, pl.ds(0, 4, stride=4)] = deepest[c][4 * y : 4 * y + 4, at]
+            copies.append(pltpu.make_async_copy(done_ref.at[c, k], out_ref.at[c, :, 0, :, at], sems.at[c]))
+            copies[-1].start()
     for copy in copies:
         copy.wait()
 
@@ -470,46 +489,49 @@
     z_from_right2 = move(z_left2, "gz", -2)
 
     planes = ((comps, lanes, 2, ROWS, 128), F32)
+    (own,) = call(along_y_kernel, [u], [cells], flops=1 << 31)
     b, z0_right, z0_left = call(
-        along_y_kernel,
-        [z_from_left2, z_from_right2, u, from_left0, from_right0] + consts("tx", "rims"),
+        rim_kernel,
+        [z_from_left2, z_from_right2, own, from_left0, from_right0] + consts("tx", "rims"),
         [cells] + [planes] * 2,
-        [pltpu.VMEM((lanes, 64 * comps, 128), F32)],
-        flops=1 << 32,
+        [pltpu.VMEM((lanes, 64 * comps, 128), F32), pltpu.VMEM((2, ROWS * ROWS, 128), F32)],
+        flops=1 << 31,
     )
     z0_from_left = move(z0_right, "gz", 1)
     z0_from_right = move(z0_left, "gz", -1)
 
-    o1, o2, y1_right, y1_left, away = call(
+    o1, o2, y1_right, y1_left, y2_right, y2_left = call(
         chain_kernel,
         [first, second, z_from_left, z_from_right, z_from_left2, z_from_right2] + consts("chain1", "chain2", "tx12"),
         [((comps, 64, half), F32), ((comps, 16, quarter), F32)]
         + [((comps, 32, half), F32)] * 2
-        + [((comps, 16, quarter), F32)],
+        + [((comps, 8, quarter), F32)] * 2,
         [pltpu.VMEM((comps, 64, half), F32)],
         flops=1 << 31,
     )
     y_from_left = move(y1_right, "gy", 1)
+    y_from_left2 = move(y2_right, "gy", 2)
+    (y1_left,) = call(hand_on_kernel, [z0_from_left, y1_left], [((comps, 32, half), F32)])
+    (y2_left,) = call(hand_on_kernel, [z0_from_right, y2_left], [((comps, 8, quarter), F32)])
     y_from_right = move(y1_left, "gy", -1)
-    y2_right, y2_left = call(away_kernel, [z0_from_left, away], [((comps, 8, quarter), F32)] * 2)
-    y_from_left2 = move(y2_right, "gy", 2)
     y_from_right2 = move(y2_left, "gy", -2)
 
     whole = ((comps, ROWS * ROWS, nx), F32)
     result, even = call(
         along_z_kernel,
         [b, z0_from_left, z0_from_right],
-        [whole, ((comps, lanes // 2, ROWS * ROWS // 2, 128), F32)],
+        [whole, ((comps, lanes // 2, 8, ROWS, 128), F32)],
         [pltpu.VMEM((comps, lanes, ROWS * ROWS, 128), F32), dma(comps)],
         flops=1 << 32,
         hbm_out=(0,),
     )
+    pairs_of_rows = ((comps, 8, 2, ROWS, nx), F32)
     (result,) = call(
         last_kernel,
-        [result, even, o1, o2, y_from_left, y_from_right, y_from_left2, y_from_right2]
+        [result.reshape(pairs_of_rows[0]), even, o1, o2, y_from_left, y_from_right, y_from_left2, y_from_right2]
         + consts("ygive1", "ygive2", "tx1"),
-        [whole],
-        [pltpu.VMEM((comps, lanes // 2, ROWS * ROWS // 2, 128), F32), dma(comps)],
+        [pairs_of_rows],
+        [pltpu.VMEM((comps, lanes // 2, 8, ROWS, 128), F32), dma(comps)],
         flops=1 << 30,
         hbm_in=(0,),
         hbm_out=(0,),

time: 48.2 us -> 46.3 us (0.961)
  the two profiles are of different devices: /device:TPU:1 before, /device:TPU:2 now
where the time goes in v5:
time: 46.3 us; the launch traced here: 46 us
  Pallas kernels  18.3 us (40%)
  starting transfers between devices  16.9 us (37%)
  waiting for transfers between devices  10.5 us (23%)
    pallas_call x9, Pallas kernels, call(): pl.pallas_call(body, in_specs=[spec(n, hbm_in) for n in range(len(ins))],...  18.3 us
    ppermute x12, starting transfers between devices, move(): lax.ppermute(value, axis, [(i, (i + step) % count) for i in range(count)])  16.9 us
    ppermute x12, waiting for transfers between devices, move(): lax.ppermute(value, axis, [(i, (i + step) % count) for i in range(count)])  10.5 us
  transfers between devices with their start and end apart: 12, of which 5 were waited for; matrix products, arithmetic and copies ran while one was open for 0% of the time, Pallas kernels for 31%

profile of v5, /device:TPU:2, one launch (start us, length us, event | category | flops | bytes accessed | tf_op | source)
XLA Modules:
  0.0 46.0 jit_solution(5253109561249178278)
XLA Ops:
  0.0 0.0 copy-start.12
  0.0 0.0 copy-start.9
  0.1 2.0 %shard_map.172 = (f32[4,2,16,1024]{3,2,1,0:T(8,128)S(1)}, f32[4,2,16,1024]{3,2,1,0:T(8,128)S(1)}, f32[16,16,1024]{2,1,0:T(8,128)S(1)}) custom-call(f32[4,16,16,1024]{3,2,1,0:T(8,128)} %x_ref.1), custom_call_target="tpu_custom_call" | custom-call | bytes 6291456 | tf_op jit(solution)/shard_map/pallas_call | solution.py:426
  2.1 1.7 %collective-permute-start.2 = (f32[4,2,16,1024]{3,2,1,0:T(8,128)S(1)}, f32[4,2,16,1024]{3,2,1,0:T(8,128)S(1)}, u32[]{:S(2)}, u32[]{:S(2)}) collective-permute-start(f32[4,2,16,1024]{3,2,1,0:T(8,128)S(1)} %get-tuple-element.30), channel_id=1, source_target_pairs={{0,8},{8,16},{16,24},{24,32},{32,40},{40,48},{48,56},{56,64},{64,7... | collective-permute-start | bytes 1572872 | tf_op jit(solution)/shard_map/ppermute | solution.py:440
  3.8 6.8 %collective-permute-start.3 = (f32[4,2,16,1024]{3,2,1,0:T(8,128)S(1)}, f32[4,2,16,1024]{3,2,1,0:T(8,128)S(1)}, u32[]{:S(2)}, u32[]{:S(2)}) collective-permute-start(f32[4,2,16,1024]{3,2,1,0:T(8,128)S(1)} %get-tuple-element.31), channel_id=1, source_target_pairs={{0,248},{8,0},{16,8},{24,16},{32,24},{40,32},{48,40},{56,48},{64,5... | collective-permute-start | bytes 1572872 | tf_op jit(solution)/shard_map/ppermute | solution.py:440
  10.6 5.5 %shard_map.173 = (f32[4,8,256,128]{3,2,1,0:T(8,128)S(1)}, f32[4,112,512]{2,1,0:T(8,128)S(1)}, f32[4,64,256]{2,1,0:T(8,128)S(1)}, f32[4,64,512]{2,1,0:T(8,128)S(1...) custom-call(f32[4,256,1024]{2,1,0:T(8,128)} %bitcast.5, ...), custom_call_target="tpu_custom_call" | custom-call | flops 8589934592 | bytes 13385728 | tf_op jit(solution)/shard_map/pallas_call | solution.py:426
  16.1 1.6 %collective-permute-start = (f32[4,16,512]{2,1,0:T(8,128)S(1)}, f32[4,16,512]{2,1,0:T(8,128)S(1)}, u32[]{:S(2)}, u32[]{:S(2)}) collective-permute-start(f32[4,16,512]{2,1,0:T(8,128)S(1)} %get-tuple-element.27), channel_id=1, source_target_pairs={{0,2},{1,3},{2,4},{3,5},{4,6},{5,7},{6,0},{7,1},{8,10},{9,11},{10,... | collective-permute-start | bytes 393224 | tf_op jit(solution)/shard_map/ppermute | solution.py:440
  17.6 0.5 %collective-permute-start.1 = (f32[4,16,512]{2,1,0:T(8,128)S(1)}, f32[4,16,512]{2,1,0:T(8,128)S(1)}, u32[]{:S(2)}, u32[]{:S(2)}) collective-permute-start(f32[4,16,512]{2,1,0:T(8,128)S(1)} %get-tuple-element.28), channel_id=1, source_target_pairs={{0,6},{1,7},{2,0},{3,1},{4,2},{5,3},{6,4},{7,5},{8,14},{9,15},{10,... | collective-permute-start | bytes 393224 | tf_op jit(solution)/shard_map/ppermute | solution.py:440
  18.2 2.9 %collective-permute-done._.l2_ref = f32[4,16,512]{2,1,0:T(8,128)S(1)} collective-permute-done((f32[4,16,512]{2,1,0:T(8,128)S(1)}, f32[4,16,512]{2,1,0:T(8,128)S(1)}, u32[]{:S(2)}, u32[]{:S(2)}) %collective-permute-start) | collective-permute-done | bytes 131104 | tf_op jit(solution)/shard_map/ppermute | solution.py:440
  21.1 0.1 collective-permute-start.7
  21.2 2.1 %shard_map.174.own_ref = f32[4,8,256,128]{3,2,1,0:T(8,128)S(1)} custom-call(f32[4,8,256,128]{3,2,1,0:T(8,128)S(1)} %get-tuple-element.29.u_ref), custom_call_target="tpu_custom_call" | custom-call | flops 2147483648 | bytes 8388608 | tf_op jit(solution)/shard_map/pallas_call | solution.py:426
  23.3 2.0 %shard_map.175 = (f32[4,8,256,128]{3,2,1,0:T(8,128)S(1)}, f32[4,8,2,16,128]{4,3,2,1,0:T(8,128)S(1)}, f32[4,8,2,16,128]{4,3,2,1,0:T(8,128)S(1)}) custom-call(f32[4,16,512]{2,1,0:T(8,128)S(1)} %collective-permute-done._.l2_ref, f32[4,16,512]{2,1,0:T(8,128)S(1)} %collective-permute-done.1._2.r2_ref, f32[4,8,256,128]{3,2,1,0:T(8,128)S(1)} %shard_map.174.own_ref, ...), custom_call_target="tpu_custom_call" | custom-call | flops 2147483648 | bytes 11272192 | tf_op jit(solution)/shard_map/pallas_call | solution.py:426
  25.3 0.5 %collective-permute-start.4 = (f32[4,8,2,16,128]{4,3,2,1,0:T(8,128)S(1)}, f32[4,8,2,16,128]{4,3,2,1,0:T(8,128)S(1)}, u32[]{:S(2)}, u32[]{:S(2)}) collective-permute-start(f32[4,8,2,16,128]{4,3,2,1,0:T(8,128)S(1)} %get-tuple-element.33), channel_id=1, source_target_pairs={{0,1},{1,2},{2,3},{3,4},{4,5},{5,6},{6,7},{7,0},{8,9},{9,10},{10,1... | collective-permute-start | bytes 1572872 | tf_op jit(solution)/shard_map/ppermute | solution.py:440
  25.8 1.4 %collective-permute-start.5 = (f32[4,8,2,16,128]{4,3,2,1,0:T(8,128)S(1)}, f32[4,8,2,16,128]{4,3,2,1,0:T(8,128)S(1)}, u32[]{:S(2)}, u32[]{:S(2)}) collective-permute-start(f32[4,8,2,16,128]{4,3,2,1,0:T(8,128)S(1)} %get-tuple-element.34), channel_id=1, source_target_pairs={{0,7},{1,0},{2,1},{3,2},{4,3},{5,4},{6,5},{7,6},{8,15},{9,8},{10,9... | collective-permute-start | bytes 1572872 | tf_op jit(solution)/shard_map/ppermute | solution.py:440
  27.2 0.7 %collective-permute-done.7.r1_ref = f32[4,64,512]{2,1,0:T(8,128)S(1)} collective-permute-done((f32[4,64,512]{2,1,0:T(8,128)S(1)}, f32[4,64,512]{2,1,0:T(8,128)S(1)}, u32[]{:S(2)}, u32[]{:S(2)}) %collective-permute-start.7) | collective-permute-done | bytes 524320 | tf_op jit(solution)/shard_map/ppermute | solution.py:440
  27.9 1.6 %shard_map.177 = (f32[4,64,512]{2,1,0:T(8,128)S(1)}, f32[4,16,256]{2,1,0:T(8,128)S(1)}, f32[4,32,512]{2,1,0:T(8,128)S(1)}, f32[4,32,512]{2,1,0:T(8,128)S(1)}, f3...) custom-call(f32[4,112,512]{2,1,0:T(8,128)S(1)} %get-tuple-element.37.first_ref, ...), custom_call_target="tpu_custom_call" | custom-call | flops 2147483648 | bytes 4294656 | tf_op jit(solution)/shard_map/pallas_call | solution.py:426
  29.5 0.1 collective-permute-start.10
  29.6 0.1 collective-permute-start.8
  29.7 4.3 %collective-permute-done.4.l_ref._ = f32[4,8,2,16,128]{4,3,2,1,0:T(8,128)S(1)} collective-permute-done((f32[4,8,2,16,128]{4,3,2,1,0:T(8,128)S(1)}, f32[4,8,2,16,128]{4,3,2,1,0:T(8,128)S(1)}, u32[]{:S(2)}, u32[]{:S(2)}) %collective-permute-start.4) | collective-permute-done | bytes 524320 | tf_op jit(solution)/shard_map/ppermute | solution.py:440
  34.0 4.2 %collective-permute-start.9 = (f32[4,32,512]{2,1,0:T(8,128)S(1)}, f32[4,32,512]{2,1,0:T(8,128)S(1)}, u32[]{:S(2)}, u32[]{:S(2)}) collective-permute-start(f32[4,32,512]{2,1,0:T(8,128)S(1)} %shard_map.178), channel_id=1, source_target_pairs={{0,248},{8,0},{16,8},{24,16},{32,24},{40,32},{48,40},{56,48},{64,5... | collective-permute-start | bytes 786440 | tf_op jit(solution)/shard_map/ppermute | solution.py:440
  38.3 3.2 %shard_map.176 = (f32[4,256,1024]{2,1,0:T(8,128)}, f32[4,4,8,16,128]{4,3,2,1,0:T(8,128)S(1)}) custom-call(f32[4,8,256,128]{3,2,1,0:T(8,128)S(1)} %get-tuple-element.32.b_ref, f32[4,8,2,16,128]{4,3,2,1,0:T(8,128)S(1)} %collective-permute-done.4.l_ref._, f32[4,8,2,16,128]{4,3,2,1,0:T(8,128)S(1)} %collective-permute-done.5.r_ref._), custom_call_target="tpu_custom_call" | custom-call | flops 4294967296 | bytes 10485760 | tf_op jit(solution)/shard_map/pallas_call | solution.py:426
  41.6 0.6 %collective-permute-done.8.l1_ref = f32[4,32,512]{2,1,0:T(8,128)S(1)} collective-permute-done((f32[4,32,512]{2,1,0:T(8,128)S(1)}, f32[4,32,512]{2,1,0:T(8,128)S(1)}, u32[]{:S(2)}, u32[]{:S(2)}) %collective-permute-start.8) | collective-permute-done | bytes 262176 | tf_op jit(solution)/shard_map/ppermute | solution.py:440
  42.2 1.9 %collective-permute-done.11.r2_ref = f32[4,8,256]{2,1,0:T(8,128)S(1)} collective-permute-done((f32[4,8,256]{2,1,0:T(8,128)S(1)}, f32[4,8,256]{2,1,0:T(8,128)S(1)}, u32[]{:S(2)}, u32[]{:S(2)}) %collective-permute-start.11) | collective-permute-done | bytes 32800 | tf_op jit(solution)/shard_map/ppermute | solution.py:440
  44.1 1.8 %shard_map.180 = f32[4,8,2,16,1024]{4,3,2,1,0:T(8,128)} custom-call(f32[4,8,2,16,1024]{4,3,2,1,0:T(8,128)} %bitcast.6, f32[4,4,8,16,128]{4,3,2,1,0:T(8,128)S(1)} %get-tuple-element.36.even_ref, f32[4,64,512]{2,1,0:T(8,128)S(1)} %get-tuple-element.41.o1_ref, f32[4,16,256]{2,1,0:T(8,128)S(1)} %get-tuple-element.42.o2_ref, ...), custom_call_target="tpu_custom_call", output_to_operand_aliasing={{}: (0, {})} | custom-call | flops 1073741824 | bytes 11680768 | tf_op jit(solution)/shard_map/pallas_call | solution.py:426
  (43 shorter events, 0.1 us)
Async XLA Ops:
  0.0 10.6 %copy-start.8 = (bf16[128,1024]{1,0:T(8,128)(2,1)S(1)}, bf16[128,1024]{1,0:T(8,128)(2,1)}, u32[]{:S(2)}) copy-start(bf16[128,1024]{1,0:T(8,128)(2,1)} %constant.50.clone.rims) | copy-start | bytes 786436
  0.0 10.6 %copy-start.6 = (bf16[512,256]{1,0:T(8,128)(2,1)S(1)}, bf16[512,256]{1,0:T(8,128)(2,1)}, u32[]{:S(2)}) copy-start(bf16[512,256]{1,0:T(8,128)(2,1)} %constant.39.clone.t12l) | copy-start | bytes 786436
  0.0 10.6 %copy-start.7 = (bf16[512,256]{1,0:T(8,128)(2,1)S(1)}, bf16[512,256]{1,0:T(8,128)(2,1)}, u32[]{:S(2)}) copy-start(bf16[512,256]{1,0:T(8,128)(2,1)} %constant.38.clone.t12h) | copy-start | bytes 786436
  0.0 10.6 %copy-start.11 = (bf16[256,256]{1,0:T(8,128)(2,1)S(1)}, bf16[256,256]{1,0:T(8,128)(2,1)}, u32[]{:S(2)}) copy-start(bf16[256,256]{1,0:T(8,128)(2,1)} %constant.35.clone.txl) | copy-start | bytes 393220
  0.0 10.6 %copy-start.12 = (bf16[256,256]{1,0:T(8,128)(2,1)S(1)}, bf16[256,256]{1,0:T(8,128)(2,1)}, u32[]{:S(2)}) copy-start(bf16[256,256]{1,0:T(8,128)(2,1)} %constant.34.clone.txh) | copy-start | bytes 393220
  0.0 10.6 %copy-start.9 = (bf16[400,256]{1,0:T(8,128)(2,1)S(1)}, bf16[400,256]{1,0:T(8,128)(2,1)}, u32[]{:S(2)}) copy-start(bf16[400,256]{1,0:T(8,128)(2,1)} %constant.41.clone.zsl) | copy-start | bytes 614404
  0.0 10.6 %copy-start.10 = (bf16[400,256]{1,0:T(8,128)(2,1)S(1)}, bf16[400,256]{1,0:T(8,128)(2,1)}, u32[]{:S(2)}) copy-start(bf16[400,256]{1,0:T(8,128)(2,1)} %constant.40.clone.zsh) | copy-start | bytes 614404
  2.1 21.2 %collective-permute-start.2 = (f32[4,2,16,1024]{3,2,1,0:T(8,128)S(1)}, f32[4,2,16,1024]{3,2,1,0:T(8,128)S(1)}, u32[]{:S(2)}, u32[]{:S(2)}) collective-permute-start(f32[4,2,16,1024]{3,2,1,0:T(8,128)S(1)} %get-tuple-element.30), channel_id=1, source_target_pairs={{0,8},{8,16},{16,24},{24,32},{32,40},{40,48},{48,56},{56,64},{64,7... | collective-permute-start | bytes 1572872 | tf_op jit(solution)/shard_map/ppermute | solution.py:440
  3.8 19.6 %collective-permute-start.3 = (f32[4,2,16,1024]{3,2,1,0:T(8,128)S(1)}, f32[4,2,16,1024]{3,2,1,0:T(8,128)S(1)}, u32[]{:S(2)}, u32[]{:S(2)}) collective-permute-start(f32[4,2,16,1024]{3,2,1,0:T(8,128)S(1)} %get-tuple-element.31), channel_id=1, source_target_pairs={{0,248},{8,0},{16,8},{24,16},{32,24},{40,32},{48,40},{56,48},{64,5... | collective-permute-start | bytes 1572872 | tf_op jit(solution)/shard_map/ppermute | solution.py:440
  16.1 5.0 %collective-permute-start = (f32[4,16,512]{2,1,0:T(8,128)S(1)}, f32[4,16,512]{2,1,0:T(8,128)S(1)}, u32[]{:S(2)}, u32[]{:S(2)}) collective-permute-start(f32[4,16,512]{2,1,0:T(8,128)S(1)} %get-tuple-element.27), channel_id=1, source_target_pairs={{0,2},{1,3},{2,4},{3,5},{4,6},{5,7},{6,0},{7,1},{8,10},{9,11},{10,... | collective-permute-start | bytes 393224 | tf_op jit(solution)/shard_map/ppermute | solution.py:440
  17.6 5.7 %collective-permute-start.1 = (f32[4,16,512]{2,1,0:T(8,128)S(1)}, f32[4,16,512]{2,1,0:T(8,128)S(1)}, u32[]{:S(2)}, u32[]{:S(2)}) collective-permute-start(f32[4,16,512]{2,1,0:T(8,128)S(1)} %get-tuple-element.28), channel_id=1, source_target_pairs={{0,6},{1,7},{2,0},{3,1},{4,2},{5,3},{6,4},{7,5},{8,14},{9,15},{10,... | collective-permute-start | bytes 393224 | tf_op jit(solution)/shard_map/ppermute | solution.py:440
  18.2 9.0 %collective-permute-start.6 = (f32[4,64,512]{2,1,0:T(8,128)S(1)}, f32[4,64,512]{2,1,0:T(8,128)S(1)}, u32[]{:S(2)}, u32[]{:S(2)}) collective-permute-start(f32[4,64,512]{2,1,0:T(8,128)S(1)} %get-tuple-element.39), channel_id=1, source_target_pairs={{0,1},{1,2},{2,3},{3,4},{4,5},{5,6},{6,7},{7,0},{8,9},{9,10},{10,1... | collective-permute-start | bytes 1572872 | tf_op jit(solution)/shard_map/ppermute | solution.py:440
  21.1 6.8 %collective-permute-start.7 = (f32[4,64,512]{2,1,0:T(8,128)S(1)}, f32[4,64,512]{2,1,0:T(8,128)S(1)}, u32[]{:S(2)}, u32[]{:S(2)}) collective-permute-start(f32[4,64,512]{2,1,0:T(8,128)S(1)} %get-tuple-element.40), channel_id=1, source_target_pairs={{0,7},{1,0},{2,1},{3,2},{4,3},{5,4},{6,5},{7,6},{8,15},{9,8},{10,9... | collective-permute-start | bytes 1572872 | tf_op jit(solution)/shard_map/ppermute | solution.py:440
  25.3 8.7 %collective-permute-start.4 = (f32[4,8,2,16,128]{4,3,2,1,0:T(8,128)S(1)}, f32[4,8,2,16,128]{4,3,2,1,0:T(8,128)S(1)}, u32[]{:S(2)}, u32[]{:S(2)}) collective-permute-start(f32[4,8,2,16,128]{4,3,2,1,0:T(8,128)S(1)} %get-tuple-element.33), channel_id=1, source_target_pairs={{0,1},{1,2},{2,3},{3,4},{4,5},{5,6},{6,7},{7,0},{8,9},{9,10},{10,1... | collective-permute-start | bytes 1572872 | tf_op jit(solution)/shard_map/ppermute | solution.py:440
  25.8 12.5 %collective-permute-start.5 = (f32[4,8,2,16,128]{4,3,2,1,0:T(8,128)S(1)}, f32[4,8,2,16,128]{4,3,2,1,0:T(8,128)S(1)}, u32[]{:S(2)}, u32[]{:S(2)}) collective-permute-start(f32[4,8,2,16,128]{4,3,2,1,0:T(8,128)S(1)} %get-tuple-element.34), channel_id=1, source_target_pairs={{0,7},{1,0},{2,1},{3,2},{4,3},{5,4},{6,5},{7,6},{8,15},{9,8},{10,9... | collective-permute-start | bytes 1572872 | tf_op jit(solution)/shard_map/ppermute | solution.py:440
  29.5 12.1 %collective-permute-start.10 = (f32[4,8,256]{2,1,0:T(8,128)S(1)}, f32[4,8,256]{2,1,0:T(8,128)S(1)}, u32[]{:S(2)}, u32[]{:S(2)}) collective-permute-start(f32[4,8,256]{2,1,0:T(8,128)S(1)} %get-tuple-element.45), channel_id=1, source_target_pairs={{0,16},{8,24},{16,32},{24,40},{32,48},{40,56},{48,64},{56,72},{64,... | collective-permute-start | bytes 98312 | tf_op jit(solution)/shard_map/ppermute | solution.py:440
  29.6 12.6 %collective-permute-start.8 = (f32[4,32,512]{2,1,0:T(8,128)S(1)}, f32[4,32,512]{2,1,0:T(8,128)S(1)}, u32[]{:S(2)}, u32[]{:S(2)}) collective-permute-start(f32[4,32,512]{2,1,0:T(8,128)S(1)} %get-tuple-element.43), channel_id=1, source_target_pairs={{0,8},{8,16},{16,24},{24,32},{32,40},{40,48},{48,56},{56,64},{64,7... | collective-permute-start | bytes 786440 | tf_op jit(solution)/shard_map/ppermute | solution.py:440
  34.0 10.1 %collective-permute-start.9 = (f32[4,32,512]{2,1,0:T(8,128)S(1)}, f32[4,32,512]{2,1,0:T(8,128)S(1)}, u32[]{:S(2)}, u32[]{:S(2)}) collective-permute-start(f32[4,32,512]{2,1,0:T(8,128)S(1)} %shard_map.178), channel_id=1, source_target_pairs={{0,248},{8,0},{16,8},{24,16},{32,24},{40,32},{48,40},{56,48},{64,5... | collective-permute-start | bytes 786440 | tf_op jit(solution)/shard_map/ppermute | solution.py:440
  38.3 5.8 %collective-permute-start.11 = (f32[4,8,256]{2,1,0:T(8,128)S(1)}, f32[4,8,256]{2,1,0:T(8,128)S(1)}, u32[]{:S(2)}, u32[]{:S(2)}) collective-permute-start(f32[4,8,256]{2,1,0:T(8,128)S(1)} %shard_map.179), channel_id=1, source_target_pairs={{0,240},{8,248},{16,0},{24,8},{32,16},{40,24},{48,32},{56,40},{64,... | collective-permute-start | bytes 98312 | tf_op jit(solution)/shard_map/ppermute | solution.py:440
  38.3 5.8 %copy-start = (bf16[512,512]{1,0:T(8,128)(2,1)S(1)}, bf16[512,512]{1,0:T(8,128)(2,1)}, u32[]{:S(2)}) copy-start(bf16[512,512]{1,0:T(8,128)(2,1)} %constant.37.clone.t1l) | copy-start | bytes 1572868
  38.3 5.8 %copy-start.1 = (bf16[512,512]{1,0:T(8,128)(2,1)S(1)}, bf16[512,512]{1,0:T(8,128)(2,1)}, u32[]{:S(2)}) copy-start(bf16[512,512]{1,0:T(8,128)(2,1)} %constant.36.clone.t1h) | copy-start | bytes 1572868
  38.3 5.8 %copy-start.2 = (bf16[64,48]{1,0:T(8,128)(2,1)S(1)}, bf16[64,48]{1,0:T(8,128)(2,1)}, u32[]{:S(2)}) copy-start(bf16[64,48]{1,0:T(8,128)(2,1)} %constant.47.clone.g1l) | copy-start | bytes 18436
  38.3 5.8 %copy-start.3 = (bf16[64,48]{1,0:T(8,128)(2,1)S(1)}, bf16[64,48]{1,0:T(8,128)(2,1)}, u32[]{:S(2)}) copy-start(bf16[64,48]{1,0:T(8,128)(2,1)} %constant.46.clone.g1h) | copy-start | bytes 18436
  38.3 5.8 %copy-start.4 = (bf16[16,48]{1,0:T(8,128)(2,1)S(1)}, bf16[16,48]{1,0:T(8,128)(2,1)}, u32[]{:S(2)}) copy-start(bf16[16,48]{1,0:T(8,128)(2,1)} %constant.49.clone.g2l) | copy-start | bytes 4612
  (5 other events, 24.2 us)

commit v6 on v5

--- a/solution.py
+++ b/solution.py
@@ -278,7 +278,7 @@
         to_l_ref[c, :24] = first[88:]
         return 0
 
-    lax.fori_loop(0, comps, step, 0)
+    lax.fori_loop(0, comps, step, 0, unroll=True)
     far = right(split(far_ref[...].reshape(64 * comps, half)), both(t12h, t12l))
     for c in range(comps):
         deep = []
@@ -309,7 +309,7 @@
                 b[pl.ds(128 * part + y, 8, stride=ROWS)] = value
         return 0
 
-    lax.fori_loop(0, comps * lanes, step, 0, unroll=2)
+    lax.fori_loop(0, comps * lanes, step, 0, unroll=4)
 
 
 def rim_kernel(_, _2, own_ref, l_ref, r_ref, txh, txl, rims, b_ref, to_r_ref, to_l_ref, halo_ref, added_ref):
@@ -346,7 +346,7 @@
         to_l_ref[c, k, 0], to_l_ref[c, k, 1] = give_left([plane(z) for z in range(3)])
         return 0
 
-    lax.fori_loop(0, comps * lanes, step, 0, unroll=2)
+    lax.fori_loop(0, comps * lanes, step, 0, unroll=4)
 
 
 def hand_on_kernel(_, value_ref, out_ref):
@@ -378,7 +378,7 @@
 
         return 0
 
-    lax.fori_loop(0, comps * lanes, step, 0, unroll=2)
+    lax.fori_loop(0, comps * lanes, step, 0, unroll=4)
     for c in range(comps):
         for k in range(lanes):
             copy(c, k).wait()

time: 46.3 us -> 46.2 us (level)
  Pallas kernels: 18.3 us -> 17.4 us
  waiting for transfers between devices: 10.5 us -> 11 us
    pallas_call x9, Pallas kernels: 18.3 us -> 17.4 us  [call(): pl.pallas_call(body, in_specs=[spec(n, hbm_in) for n in range(len(ins))],...]
    ppermute x12, waiting for transfers between devices: 10.5 us -> 11 us  [move(): lax.ppermute(value, axis, [(i, (i + step) % count) for i in range(count)])]
  transfers between devices with their start and end apart: 12 -> 12, of which waited for: 5 -> 4; matrix products, arithmetic and copies ran while one was open for 0% -> 0% of each run, Pallas kernels for 31% -> 29%
where the time goes in v6:
time: 46.2 us; the launch traced here: 45.9 us
  Pallas kernels  17.4 us (38%)
  starting transfers between devices  17 us (37%)
  waiting for transfers between devices  11 us (24%)
    pallas_call x9, Pallas kernels, call(): pl.pallas_call(body, in_specs=[spec(n, hbm_in) for n in range(len(ins))],...  17.4 us
    ppermute x12, starting transfers between devices, move(): lax.ppermute(value, axis, [(i, (i + step) % count) for i in range(count)])  17 us
    ppermute x12, waiting for transfers between devices, move(): lax.ppermute(value, axis, [(i, (i + step) % count) for i in range(count)])  11 us
  transfers between devices with their start and end apart: 12, of which 4 were waited for; matrix products, arithmetic and copies ran while one was open for 0% of the time, Pallas kernels for 29%

profile of v6, /device:TPU:2, one launch (start us, length us, event | category | flops | bytes accessed | tf_op | source)
XLA Modules:
  0.0 45.9 jit_solution(4810508334058933048)
XLA Ops:
  0.0 0.0 copy-start.11
  0.0 0.0 copy-start.12
  0.0 0.0 copy-start.9
  0.1 2.0 %shard_map.172 = (f32[4,2,16,1024]{3,2,1,0:T(8,128)S(1)}, f32[4,2,16,1024]{3,2,1,0:T(8,128)S(1)}, f32[16,16,1024]{2,1,0:T(8,128)S(1)}) custom-call(f32[4,16,16,1024]{3,2,1,0:T(8,128)} %x_ref.1), custom_call_target="tpu_custom_call" | custom-call | bytes 6291456 | tf_op jit(solution)/shard_map/pallas_call | solution.py:426
  2.1 1.7 %collective-permute-start.2 = (f32[4,2,16,1024]{3,2,1,0:T(8,128)S(1)}, f32[4,2,16,1024]{3,2,1,0:T(8,128)S(1)}, u32[]{:S(2)}, u32[]{:S(2)}) collective-permute-start(f32[4,2,16,1024]{3,2,1,0:T(8,128)S(1)} %get-tuple-element.30), channel_id=1, source_target_pairs={{0,8},{8,16},{16,24},{24,32},{32,40},{40,48},{48,56},{56,64},{64,7... | collective-permute-start | bytes 1572872 | tf_op jit(solution)/shard_map/ppermute | solution.py:440
  3.8 6.8 %collective-permute-start.3 = (f32[4,2,16,1024]{3,2,1,0:T(8,128)S(1)}, f32[4,2,16,1024]{3,2,1,0:T(8,128)S(1)}, u32[]{:S(2)}, u32[]{:S(2)}) collective-permute-start(f32[4,2,16,1024]{3,2,1,0:T(8,128)S(1)} %get-tuple-element.31), channel_id=1, source_target_pairs={{0,248},{8,0},{16,8},{24,16},{32,24},{40,32},{48,40},{56,48},{64,5... | collective-permute-start | bytes 1572872 | tf_op jit(solution)/shard_map/ppermute | solution.py:440
  10.6 5.5 %shard_map.173 = (f32[4,8,256,128]{3,2,1,0:T(8,128)S(1)}, f32[4,112,512]{2,1,0:T(8,128)S(1)}, f32[4,64,256]{2,1,0:T(8,128)S(1)}, f32[4,64,512]{2,1,0:T(8,128)S(1...) custom-call(f32[4,256,1024]{2,1,0:T(8,128)} %bitcast.5, ...), custom_call_target="tpu_custom_call" | custom-call | flops 8589934592 | bytes 13385728 | tf_op jit(solution)/shard_map/pallas_call | solution.py:426
  16.1 1.6 %collective-permute-start = (f32[4,16,512]{2,1,0:T(8,128)S(1)}, f32[4,16,512]{2,1,0:T(8,128)S(1)}, u32[]{:S(2)}, u32[]{:S(2)}) collective-permute-start(f32[4,16,512]{2,1,0:T(8,128)S(1)} %get-tuple-element.27), channel_id=1, source_target_pairs={{0,2},{1,3},{2,4},{3,5},{4,6},{5,7},{6,0},{7,1},{8,10},{9,11},{10,... | collective-permute-start | bytes 393224 | tf_op jit(solution)/shard_map/ppermute | solution.py:440
  17.6 0.5 %collective-permute-start.1 = (f32[4,16,512]{2,1,0:T(8,128)S(1)}, f32[4,16,512]{2,1,0:T(8,128)S(1)}, u32[]{:S(2)}, u32[]{:S(2)}) collective-permute-start(f32[4,16,512]{2,1,0:T(8,128)S(1)} %get-tuple-element.28), channel_id=1, source_target_pairs={{0,6},{1,7},{2,0},{3,1},{4,2},{5,3},{6,4},{7,5},{8,14},{9,15},{10,... | collective-permute-start | bytes 393224 | tf_op jit(solution)/shard_map/ppermute | solution.py:440
  18.2 2.9 %collective-permute-done._.l2_ref = f32[4,16,512]{2,1,0:T(8,128)S(1)} collective-permute-done((f32[4,16,512]{2,1,0:T(8,128)S(1)}, f32[4,16,512]{2,1,0:T(8,128)S(1)}, u32[]{:S(2)}, u32[]{:S(2)}) %collective-permute-start) | collective-permute-done | bytes 131104 | tf_op jit(solution)/shard_map/ppermute | solution.py:440
  21.1 0.1 collective-permute-start.7
  21.2 1.9 %shard_map.174.own_ref = f32[4,8,256,128]{3,2,1,0:T(8,128)S(1)} custom-call(f32[4,8,256,128]{3,2,1,0:T(8,128)S(1)} %get-tuple-element.29.u_ref), custom_call_target="tpu_custom_call" | custom-call | flops 2147483648 | bytes 8388608 | tf_op jit(solution)/shard_map/pallas_call | solution.py:426
  23.2 1.9 %shard_map.175 = (f32[4,8,256,128]{3,2,1,0:T(8,128)S(1)}, f32[4,8,2,16,128]{4,3,2,1,0:T(8,128)S(1)}, f32[4,8,2,16,128]{4,3,2,1,0:T(8,128)S(1)}) custom-call(f32[4,16,512]{2,1,0:T(8,128)S(1)} %collective-permute-done._.l2_ref, f32[4,16,512]{2,1,0:T(8,128)S(1)} %collective-permute-done.1._2.r2_ref, f32[4,8,256,128]{3,2,1,0:T(8,128)S(1)} %shard_map.174.own_ref, ...), custom_call_target="tpu_custom_call" | custom-call | flops 2147483648 | bytes 11272192 | tf_op jit(solution)/shard_map/pallas_call | solution.py:426
  25.1 0.5 %collective-permute-start.4 = (f32[4,8,2,16,128]{4,3,2,1,0:T(8,128)S(1)}, f32[4,8,2,16,128]{4,3,2,1,0:T(8,128)S(1)}, u32[]{:S(2)}, u32[]{:S(2)}) collective-permute-start(f32[4,8,2,16,128]{4,3,2,1,0:T(8,128)S(1)} %get-tuple-element.33), channel_id=1, source_target_pairs={{0,1},{1,2},{2,3},{3,4},{4,5},{5,6},{6,7},{7,0},{8,9},{9,10},{10,1... | collective-permute-start | bytes 1572872 | tf_op jit(solution)/shard_map/ppermute | solution.py:440
  25.5 1.4 %collective-permute-start.5 = (f32[4,8,2,16,128]{4,3,2,1,0:T(8,128)S(1)}, f32[4,8,2,16,128]{4,3,2,1,0:T(8,128)S(1)}, u32[]{:S(2)}, u32[]{:S(2)}) collective-permute-start(f32[4,8,2,16,128]{4,3,2,1,0:T(8,128)S(1)} %get-tuple-element.34), channel_id=1, source_target_pairs={{0,7},{1,0},{2,1},{3,2},{4,3},{5,4},{6,5},{7,6},{8,15},{9,8},{10,9... | collective-permute-start | bytes 1572872 | tf_op jit(solution)/shard_map/ppermute | solution.py:440
  26.9 1.0 %collective-permute-done.7.r1_ref = f32[4,64,512]{2,1,0:T(8,128)S(1)} collective-permute-done((f32[4,64,512]{2,1,0:T(8,128)S(1)}, f32[4,64,512]{2,1,0:T(8,128)S(1)}, u32[]{:S(2)}, u32[]{:S(2)}) %collective-permute-start.7) | collective-permute-done | bytes 524320 | tf_op jit(solution)/shard_map/ppermute | solution.py:440
  27.9 1.1 %shard_map.177 = (f32[4,64,512]{2,1,0:T(8,128)S(1)}, f32[4,16,256]{2,1,0:T(8,128)S(1)}, f32[4,32,512]{2,1,0:T(8,128)S(1)}, f32[4,32,512]{2,1,0:T(8,128)S(1)}, f3...) custom-call(f32[4,112,512]{2,1,0:T(8,128)S(1)} %get-tuple-element.37.first_ref, ...), custom_call_target="tpu_custom_call" | custom-call | flops 2147483648 | bytes 4294656 | tf_op jit(solution)/shard_map/pallas_call | solution.py:426
  29.0 0.1 collective-permute-start.10
  29.1 0.1 collective-permute-start.8
  29.2 4.6 %collective-permute-done.4.l_ref._ = f32[4,8,2,16,128]{4,3,2,1,0:T(8,128)S(1)} collective-permute-done((f32[4,8,2,16,128]{4,3,2,1,0:T(8,128)S(1)}, f32[4,8,2,16,128]{4,3,2,1,0:T(8,128)S(1)}, u32[]{:S(2)}, u32[]{:S(2)}) %collective-permute-start.4) | collective-permute-done | bytes 524320 | tf_op jit(solution)/shard_map/ppermute | solution.py:440
  33.8 4.4 %collective-permute-start.9 = (f32[4,32,512]{2,1,0:T(8,128)S(1)}, f32[4,32,512]{2,1,0:T(8,128)S(1)}, u32[]{:S(2)}, u32[]{:S(2)}) collective-permute-start(f32[4,32,512]{2,1,0:T(8,128)S(1)} %shard_map.178), channel_id=1, source_target_pairs={{0,248},{8,0},{16,8},{24,16},{32,24},{40,32},{48,40},{56,48},{64,5... | collective-permute-start | bytes 786440 | tf_op jit(solution)/shard_map/ppermute | solution.py:440
  38.2 3.2 %shard_map.176 = (f32[4,256,1024]{2,1,0:T(8,128)}, f32[4,4,8,16,128]{4,3,2,1,0:T(8,128)S(1)}) custom-call(f32[4,8,256,128]{3,2,1,0:T(8,128)S(1)} %get-tuple-element.32.b_ref, f32[4,8,2,16,128]{4,3,2,1,0:T(8,128)S(1)} %collective-permute-done.4.l_ref._, f32[4,8,2,16,128]{4,3,2,1,0:T(8,128)S(1)} %collective-permute-done.5.r_ref._), custom_call_target="tpu_custom_call" | custom-call | flops 4294967296 | bytes 10485760 | tf_op jit(solution)/shard_map/pallas_call | solution.py:426
  41.5 2.5 %collective-permute-done.11.r2_ref = f32[4,8,256]{2,1,0:T(8,128)S(1)} collective-permute-done((f32[4,8,256]{2,1,0:T(8,128)S(1)}, f32[4,8,256]{2,1,0:T(8,128)S(1)}, u32[]{:S(2)}, u32[]{:S(2)}) %collective-permute-start.11) | collective-permute-done | bytes 32800 | tf_op jit(solution)/shard_map/ppermute | solution.py:440
  44.0 1.8 %shard_map.180 = f32[4,8,2,16,1024]{4,3,2,1,0:T(8,128)} custom-call(f32[4,8,2,16,1024]{4,3,2,1,0:T(8,128)} %bitcast.6, f32[4,4,8,16,128]{4,3,2,1,0:T(8,128)S(1)} %get-tuple-element.36.even_ref, f32[4,64,512]{2,1,0:T(8,128)S(1)} %get-tuple-element.41.o1_ref, f32[4,16,256]{2,1,0:T(8,128)S(1)} %get-tuple-element.42.o2_ref, ...), custom_call_target="tpu_custom_call", output_to_operand_aliasing={{}: (0, {})} | custom-call | flops 1073741824 | bytes 11680768 | tf_op jit(solution)/shard_map/pallas_call | solution.py:426
  (43 shorter events, 0.1 us)
Async XLA Ops:
  0.0 10.6 %copy-start.8 = (bf16[128,1024]{1,0:T(8,128)(2,1)S(1)}, bf16[128,1024]{1,0:T(8,128)(2,1)}, u32[]{:S(2)}) copy-start(bf16[128,1024]{1,0:T(8,128)(2,1)} %constant.50.clone.rims) | copy-start | bytes 786436
  0.0 10.6 %copy-start.6 = (bf16[512,256]{1,0:T(8,128)(2,1)S(1)}, bf16[512,256]{1,0:T(8,128)(2,1)}, u32[]{:S(2)}) copy-start(bf16[512,256]{1,0:T(8,128)(2,1)} %constant.39.clone.t12l) | copy-start | bytes 786436
  0.0 10.6 %copy-start.7 = (bf16[512,256]{1,0:T(8,128)(2,1)S(1)}, bf16[512,256]{1,0:T(8,128)(2,1)}, u32[]{:S(2)}) copy-start(bf16[512,256]{1,0:T(8,128)(2,1)} %constant.38.clone.t12h) | copy-start | bytes 786436
  0.0 10.6 %copy-start.11 = (bf16[256,256]{1,0:T(8,128)(2,1)S(1)}, bf16[256,256]{1,0:T(8,128)(2,1)}, u32[]{:S(2)}) copy-start(bf16[256,256]{1,0:T(8,128)(2,1)} %constant.35.clone.txl) | copy-start | bytes 393220
  0.0 10.6 %copy-start.12 = (bf16[256,256]{1,0:T(8,128)(2,1)S(1)}, bf16[256,256]{1,0:T(8,128)(2,1)}, u32[]{:S(2)}) copy-start(bf16[256,256]{1,0:T(8,128)(2,1)} %constant.34.clone.txh) | copy-start | bytes 393220
  0.0 10.6 %copy-start.9 = (bf16[400,256]{1,0:T(8,128)(2,1)S(1)}, bf16[400,256]{1,0:T(8,128)(2,1)}, u32[]{:S(2)}) copy-start(bf16[400,256]{1,0:T(8,128)(2,1)} %constant.41.clone.zsl) | copy-start | bytes 614404
  0.0 10.6 %copy-start.10 = (bf16[400,256]{1,0:T(8,128)(2,1)S(1)}, bf16[400,256]{1,0:T(8,128)(2,1)}, u32[]{:S(2)}) copy-start(bf16[400,256]{1,0:T(8,128)(2,1)} %constant.40.clone.zsh) | copy-start | bytes 614404
  2.1 21.1 %collective-permute-start.2 = (f32[4,2,16,1024]{3,2,1,0:T(8,128)S(1)}, f32[4,2,16,1024]{3,2,1,0:T(8,128)S(1)}, u32[]{:S(2)}, u32[]{:S(2)}) collective-permute-start(f32[4,2,16,1024]{3,2,1,0:T(8,128)S(1)} %get-tuple-element.30), channel_id=1, source_target_pairs={{0,8},{8,16},{16,24},{24,32},{32,40},{40,48},{48,56},{56,64},{64,7... | collective-permute-start | bytes 1572872 | tf_op jit(solution)/shard_map/ppermute | solution.py:440
  3.8 19.4 %collective-permute-start.3 = (f32[4,2,16,1024]{3,2,1,0:T(8,128)S(1)}, f32[4,2,16,1024]{3,2,1,0:T(8,128)S(1)}, u32[]{:S(2)}, u32[]{:S(2)}) collective-permute-start(f32[4,2,16,1024]{3,2,1,0:T(8,128)S(1)} %get-tuple-element.31), channel_id=1, source_target_pairs={{0,248},{8,0},{16,8},{24,16},{32,24},{40,32},{48,40},{56,48},{64,5... | collective-permute-start | bytes 1572872 | tf_op jit(solution)/shard_map/ppermute | solution.py:440
  16.1 5.0 %collective-permute-start = (f32[4,16,512]{2,1,0:T(8,128)S(1)}, f32[4,16,512]{2,1,0:T(8,128)S(1)}, u32[]{:S(2)}, u32[]{:S(2)}) collective-permute-start(f32[4,16,512]{2,1,0:T(8,128)S(1)} %get-tuple-element.27), channel_id=1, source_target_pairs={{0,2},{1,3},{2,4},{3,5},{4,6},{5,7},{6,0},{7,1},{8,10},{9,11},{10,... | collective-permute-start | bytes 393224 | tf_op jit(solution)/shard_map/ppermute | solution.py:440
  17.6 5.5 %collective-permute-start.1 = (f32[4,16,512]{2,1,0:T(8,128)S(1)}, f32[4,16,512]{2,1,0:T(8,128)S(1)}, u32[]{:S(2)}, u32[]{:S(2)}) collective-permute-start(f32[4,16,512]{2,1,0:T(8,128)S(1)} %get-tuple-element.28), channel_id=1, source_target_pairs={{0,6},{1,7},{2,0},{3,1},{4,2},{5,3},{6,4},{7,5},{8,14},{9,15},{10,... | collective-permute-start | bytes 393224 | tf_op jit(solution)/shard_map/ppermute | solution.py:440
  18.2 8.7 %collective-permute-start.6 = (f32[4,64,512]{2,1,0:T(8,128)S(1)}, f32[4,64,512]{2,1,0:T(8,128)S(1)}, u32[]{:S(2)}, u32[]{:S(2)}) collective-permute-start(f32[4,64,512]{2,1,0:T(8,128)S(1)} %get-tuple-element.39), channel_id=1, source_target_pairs={{0,1},{1,2},{2,3},{3,4},{4,5},{5,6},{6,7},{7,0},{8,9},{9,10},{10,1... | collective-permute-start | bytes 1572872 | tf_op jit(solution)/shard_map/ppermute | solution.py:440
  21.1 6.8 %collective-permute-start.7 = (f32[4,64,512]{2,1,0:T(8,128)S(1)}, f32[4,64,512]{2,1,0:T(8,128)S(1)}, u32[]{:S(2)}, u32[]{:S(2)}) collective-permute-start(f32[4,64,512]{2,1,0:T(8,128)S(1)} %get-tuple-element.40), channel_id=1, source_target_pairs={{0,7},{1,0},{2,1},{3,2},{4,3},{5,4},{6,5},{7,6},{8,15},{9,8},{10,9... | collective-permute-start | bytes 1572872 | tf_op jit(solution)/shard_map/ppermute | solution.py:440
  25.1 8.7 %collective-permute-start.4 = (f32[4,8,2,16,128]{4,3,2,1,0:T(8,128)S(1)}, f32[4,8,2,16,128]{4,3,2,1,0:T(8,128)S(1)}, u32[]{:S(2)}, u32[]{:S(2)}) collective-permute-start(f32[4,8,2,16,128]{4,3,2,1,0:T(8,128)S(1)} %get-tuple-element.33), channel_id=1, source_target_pairs={{0,1},{1,2},{2,3},{3,4},{4,5},{5,6},{6,7},{7,0},{8,9},{9,10},{10,1... | collective-permute-start | bytes 1572872 | tf_op jit(solution)/shard_map/ppermute | solution.py:440
  25.5 12.6 %collective-permute-start.5 = (f32[4,8,2,16,128]{4,3,2,1,0:T(8,128)S(1)}, f32[4,8,2,16,128]{4,3,2,1,0:T(8,128)S(1)}, u32[]{:S(2)}, u32[]{:S(2)}) collective-permute-start(f32[4,8,2,16,128]{4,3,2,1,0:T(8,128)S(1)} %get-tuple-element.34), channel_id=1, source_target_pairs={{0,7},{1,0},{2,1},{3,2},{4,3},{5,4},{6,5},{7,6},{8,15},{9,8},{10,9... | collective-permute-start | bytes 1572872 | tf_op jit(solution)/shard_map/ppermute | solution.py:440
  29.0 12.5 %collective-permute-start.10 = (f32[4,8,256]{2,1,0:T(8,128)S(1)}, f32[4,8,256]{2,1,0:T(8,128)S(1)}, u32[]{:S(2)}, u32[]{:S(2)}) collective-permute-start(f32[4,8,256]{2,1,0:T(8,128)S(1)} %get-tuple-element.45), channel_id=1, source_target_pairs={{0,16},{8,24},{16,32},{24,40},{32,48},{40,56},{48,64},{56,72},{64,... | collective-permute-start | bytes 98312 | tf_op jit(solution)/shard_map/ppermute | solution.py:440
  29.1 12.4 %collective-permute-start.8 = (f32[4,32,512]{2,1,0:T(8,128)S(1)}, f32[4,32,512]{2,1,0:T(8,128)S(1)}, u32[]{:S(2)}, u32[]{:S(2)}) collective-permute-start(f32[4,32,512]{2,1,0:T(8,128)S(1)} %get-tuple-element.43), channel_id=1, source_target_pairs={{0,8},{8,16},{16,24},{24,32},{32,40},{40,48},{48,56},{56,64},{64,7... | collective-permute-start | bytes 786440 | tf_op jit(solution)/shard_map/ppermute | solution.py:440
  33.8 10.2 %collective-permute-start.9 = (f32[4,32,512]{2,1,0:T(8,128)S(1)}, f32[4,32,512]{2,1,0:T(8,128)S(1)}, u32[]{:S(2)}, u32[]{:S(2)}) collective-permute-start(f32[4,32,512]{2,1,0:T(8,128)S(1)} %shard_map.178), channel_id=1, source_target_pairs={{0,248},{8,0},{16,8},{24,16},{32,24},{40,32},{48,40},{56,48},{64,5... | collective-permute-start | bytes 786440 | tf_op jit(solution)/shard_map/ppermute | solution.py:440
  38.2 5.8 %collective-permute-start.11 = (f32[4,8,256]{2,1,0:T(8,128)S(1)}, f32[4,8,256]{2,1,0:T(8,128)S(1)}, u32[]{:S(2)}, u32[]{:S(2)}) collective-permute-start(f32[4,8,256]{2,1,0:T(8,128)S(1)} %shard_map.179), channel_id=1, source_target_pairs={{0,240},{8,248},{16,0},{24,8},{32,16},{40,24},{48,32},{56,40},{64,... | collective-permute-start | bytes 98312 | tf_op jit(solution)/shard_map/ppermute | solution.py:440
  38.2 5.8 %copy-start = (bf16[512,512]{1,0:T(8,128)(2,1)S(1)}, bf16[512,512]{1,0:T(8,128)(2,1)}, u32[]{:S(2)}) copy-start(bf16[512,512]{1,0:T(8,128)(2,1)} %constant.37.clone.t1l) | copy-start | bytes 1572868
  38.2 5.8 %copy-start.1 = (bf16[512,512]{1,0:T(8,128)(2,1)S(1)}, bf16[512,512]{1,0:T(8,128)(2,1)}, u32[]{:S(2)}) copy-start(bf16[512,512]{1,0:T(8,128)(2,1)} %constant.36.clone.t1h) | copy-start | bytes 1572868
  38.2 5.8 %copy-start.2 = (bf16[64,48]{1,0:T(8,128)(2,1)S(1)}, bf16[64,48]{1,0:T(8,128)(2,1)}, u32[]{:S(2)}) copy-start(bf16[64,48]{1,0:T(8,128)(2,1)} %constant.47.clone.g1l) | copy-start | bytes 18436
  38.2 5.8 %copy-start.3 = (bf16[64,48]{1,0:T(8,128)(2,1)S(1)}, bf16[64,48]{1,0:T(8,128)(2,1)}, u32[]{:S(2)}) copy-start(bf16[64,48]{1,0:T(8,128)(2,1)} %constant.46.clone.g1h) | copy-start | bytes 18436
  38.2 5.8 %copy-start.4 = (bf16[16,48]{1,0:T(8,128)(2,1)S(1)}, bf16[16,48]{1,0:T(8,128)(2,1)}, u32[]{:S(2)}) copy-start(bf16[16,48]{1,0:T(8,128)(2,1)} %constant.49.clone.g2l) | copy-start | bytes 4612
  (5 other events, 24.9 us)

commit v7 on v6

--- a/solution.py
+++ b/solution.py
@@ -509,12 +509,12 @@
         [pltpu.VMEM((comps, 64, half), F32)],
         flops=1 << 31,
     )
+    y_from_right = move(y1_left, "gy", -1)
+    y_from_right2 = move(y2_left, "gy", -2)
+    (y1_right,) = call(hand_on_kernel, [z0_from_left, y1_right], [((comps, 32, half), F32)])
+    (y2_right,) = call(hand_on_kernel, [z0_from_right, y2_right], [((comps, 8, quarter), F32)])
     y_from_left = move(y1_right, "gy", 1)
     y_from_left2 = move(y2_right, "gy", 2)
-    (y1_left,) = call(hand_on_kernel, [z0_from_left, y1_left], [((comps, 32, half), F32)])
-    (y2_left,) = call(hand_on_kernel, [z0_from_right, y2_left], [((comps, 8, quarter), F32)])
-    y_from_right = move(y1_left, "gy", -1)
-    y_from_right2 = move(y2_left, "gy", -2)
 
     whole = ((comps, ROWS * ROWS, nx), F32)
     result, even = call(

time: 46.2 us -> 48.3 us (1.045)
  waiting for transfers between devices: 11 us -> 12.7 us
  starting transfers between devices: 17 us -> 17.7 us
    ppermute x12, waiting for transfers between devices: 11 us -> 12.7 us  [move(): lax.ppermute(value, axis, [(i, (i + step) % count) for i in range(count)])]
    ppermute x12, starting transfers between devices: 17 us -> 17.7 us  [move(): lax.ppermute(value, axis, [(i, (i + step) % count) for i in range(count)])]
  transfers between devices with their start and end apart: 12 -> 12, of which waited for: 4 -> 6; matrix products, arithmetic and copies ran while one was open for 0% -> 0% of each run, Pallas kernels for 29% -> 28%
where the time goes in v7:
time: 48.3 us; the launch traced here: 48.2 us
  starting transfers between devices  17.7 us (37%)
  Pallas kernels  17.4 us (36%)
  waiting for transfers between devices  12.7 us (26%)
    ppermute x12, starting transfers between devices, move(): lax.ppermute(value, axis, [(i, (i + step) % count) for i in range(count)])  17.7 us
    pallas_call x9, Pallas kernels, call(): pl.pallas_call(body, in_specs=[spec(n, hbm_in) for n in range(len(ins))],...  17.4 us
    ppermute x12, waiting for transfers between devices, move(): lax.ppermute(value, axis, [(i, (i + step) % count) for i in range(count)])  12.7 us
  transfers between devices with their start and end apart: 12, of which 6 were waited for; matrix products, arithmetic and copies ran while one was open for 0% of the time, Pallas kernels for 28%

profile of v7, /device:TPU:2, one launch (start us, length us, event | category | flops | bytes accessed | tf_op | source)
XLA Modules:
  0.0 48.2 jit_solution(12749288596313697734)
XLA Ops:
  0.1 2.0 %shard_map.172 = (f32[4,2,16,1024]{3,2,1,0:T(8,128)S(1)}, f32[4,2,16,1024]{3,2,1,0:T(8,128)S(1)}, f32[16,16,1024]{2,1,0:T(8,128)S(1)}) custom-call(f32[4,16,16,1024]{3,2,1,0:T(8,128)} %x_ref.1), custom_call_target="tpu_custom_call" | custom-call | bytes 6291456 | tf_op jit(solution)/shard_map/pallas_call | solution.py:426
  2.1 1.7 %collective-permute-start.2 = (f32[4,2,16,1024]{3,2,1,0:T(8,128)S(1)}, f32[4,2,16,1024]{3,2,1,0:T(8,128)S(1)}, u32[]{:S(2)}, u32[]{:S(2)}) collective-permute-start(f32[4,2,16,1024]{3,2,1,0:T(8,128)S(1)} %get-tuple-element.30), channel_id=1, source_target_pairs={{0,8},{8,16},{16,24},{24,32},{32,40},{40,48},{48,56},{56,64},{64,7... | collective-permute-start | bytes 1572872 | tf_op jit(solution)/shard_map/ppermute | solution.py:440
  3.8 6.8 %collective-permute-start.3 = (f32[4,2,16,1024]{3,2,1,0:T(8,128)S(1)}, f32[4,2,16,1024]{3,2,1,0:T(8,128)S(1)}, u32[]{:S(2)}, u32[]{:S(2)}) collective-permute-start(f32[4,2,16,1024]{3,2,1,0:T(8,128)S(1)} %get-tuple-element.31), channel_id=1, source_target_pairs={{0,248},{8,0},{16,8},{24,16},{32,24},{40,32},{48,40},{56,48},{64,5... | collective-permute-start | bytes 1572872 | tf_op jit(solution)/shard_map/ppermute | solution.py:440
  10.6 5.5 %shard_map.173 = (f32[4,8,256,128]{3,2,1,0:T(8,128)S(1)}, f32[4,112,512]{2,1,0:T(8,128)S(1)}, f32[4,64,256]{2,1,0:T(8,128)S(1)}, f32[4,64,512]{2,1,0:T(8,128)S(1...) custom-call(f32[4,256,1024]{2,1,0:T(8,128)} %bitcast.5, ...), custom_call_target="tpu_custom_call" | custom-call | flops 8589934592 | bytes 13385728 | tf_op jit(solution)/shard_map/pallas_call | solution.py:426
  16.1 1.6 %collective-permute-start = (f32[4,16,512]{2,1,0:T(8,128)S(1)}, f32[4,16,512]{2,1,0:T(8,128)S(1)}, u32[]{:S(2)}, u32[]{:S(2)}) collective-permute-start(f32[4,16,512]{2,1,0:T(8,128)S(1)} %get-tuple-element.27), channel_id=1, source_target_pairs={{0,2},{1,3},{2,4},{3,5},{4,6},{5,7},{6,0},{7,1},{8,10},{9,11},{10,... | collective-permute-start | bytes 393224 | tf_op jit(solution)/shard_map/ppermute | solution.py:440
  17.6 0.5 %collective-permute-start.1 = (f32[4,16,512]{2,1,0:T(8,128)S(1)}, f32[4,16,512]{2,1,0:T(8,128)S(1)}, u32[]{:S(2)}, u32[]{:S(2)}) collective-permute-start(f32[4,16,512]{2,1,0:T(8,128)S(1)} %get-tuple-element.28), channel_id=1, source_target_pairs={{0,6},{1,7},{2,0},{3,1},{4,2},{5,3},{6,4},{7,5},{8,14},{9,15},{10,... | collective-permute-start | bytes 393224 | tf_op jit(solution)/shard_map/ppermute | solution.py:440
  18.2 2.9 %collective-permute-done._.l2_ref = f32[4,16,512]{2,1,0:T(8,128)S(1)} collective-permute-done((f32[4,16,512]{2,1,0:T(8,128)S(1)}, f32[4,16,512]{2,1,0:T(8,128)S(1)}, u32[]{:S(2)}, u32[]{:S(2)}) %collective-permute-start) | collective-permute-done | bytes 131104 | tf_op jit(solution)/shard_map/ppermute | solution.py:440
  21.1 0.1 collective-permute-start.7
  21.2 1.9 %shard_map.174.own_ref = f32[4,8,256,128]{3,2,1,0:T(8,128)S(1)} custom-call(f32[4,8,256,128]{3,2,1,0:T(8,128)S(1)} %get-tuple-element.29.u_ref), custom_call_target="tpu_custom_call" | custom-call | flops 2147483648 | bytes 8388608 | tf_op jit(solution)/shard_map/pallas_call | solution.py:426
  23.2 1.9 %shard_map.175 = (f32[4,8,256,128]{3,2,1,0:T(8,128)S(1)}, f32[4,8,2,16,128]{4,3,2,1,0:T(8,128)S(1)}, f32[4,8,2,16,128]{4,3,2,1,0:T(8,128)S(1)}) custom-call(f32[4,16,512]{2,1,0:T(8,128)S(1)} %collective-permute-done._.l2_ref, f32[4,16,512]{2,1,0:T(8,128)S(1)} %collective-permute-done.1._2.r2_ref, f32[4,8,256,128]{3,2,1,0:T(8,128)S(1)} %shard_map.174.own_ref, ...), custom_call_target="tpu_custom_call" | custom-call | flops 2147483648 | bytes 11272192 | tf_op jit(solution)/shard_map/pallas_call | solution.py:426
  25.1 0.5 collective-permute-start.4
  25.5 1.4 %collective-permute-start.5 = (f32[4,8,2,16,128]{4,3,2,1,0:T(8,128)S(1)}, f32[4,8,2,16,128]{4,3,2,1,0:T(8,128)S(1)}, u32[]{:S(2)}, u32[]{:S(2)}) collective-permute-start(f32[4,8,2,16,128]{4,3,2,1,0:T(8,128)S(1)} %get-tuple-element.34), channel_id=1, source_target_pairs={{0,7},{1,0},{2,1},{3,2},{4,3},{5,4},{6,5},{7,6},{8,15},{9,8},{10,9... | collective-permute-start | bytes 1572872 | tf_op jit(solution)/shard_map/ppermute | solution.py:440
  26.9 1.0 %collective-permute-done.7.r1_ref = f32[4,64,512]{2,1,0:T(8,128)S(1)} collective-permute-done((f32[4,64,512]{2,1,0:T(8,128)S(1)}, f32[4,64,512]{2,1,0:T(8,128)S(1)}, u32[]{:S(2)}, u32[]{:S(2)}) %collective-permute-start.7) | collective-permute-done | bytes 524320 | tf_op jit(solution)/shard_map/ppermute | solution.py:440
  27.9 1.1 %shard_map.177 = (f32[4,64,512]{2,1,0:T(8,128)S(1)}, f32[4,16,256]{2,1,0:T(8,128)S(1)}, f32[4,32,512]{2,1,0:T(8,128)S(1)}, f32[4,32,512]{2,1,0:T(8,128)S(1)}, f3...) custom-call(f32[4,112,512]{2,1,0:T(8,128)S(1)} %get-tuple-element.37.first_ref, ...), custom_call_target="tpu_custom_call" | custom-call | flops 2147483648 | bytes 4294656 | tf_op jit(solution)/shard_map/pallas_call | solution.py:426
  29.0 2.1 %collective-permute-start.11 = (f32[4,8,256]{2,1,0:T(8,128)S(1)}, f32[4,8,256]{2,1,0:T(8,128)S(1)}, u32[]{:S(2)}, u32[]{:S(2)}) collective-permute-start(f32[4,8,256]{2,1,0:T(8,128)S(1)} %get-tuple-element.46), channel_id=1, source_target_pairs={{0,240},{8,248},{16,0},{24,8},{32,16},{40,24},{48,32},{56,40},{64,... | collective-permute-start | bytes 98312 | tf_op jit(solution)/shard_map/ppermute | solution.py:440
  31.1 1.4 %collective-permute-start.9 = (f32[4,32,512]{2,1,0:T(8,128)S(1)}, f32[4,32,512]{2,1,0:T(8,128)S(1)}, u32[]{:S(2)}, u32[]{:S(2)}) collective-permute-start(f32[4,32,512]{2,1,0:T(8,128)S(1)} %get-tuple-element.44), channel_id=1, source_target_pairs={{0,248},{8,0},{16,8},{24,16},{32,24},{40,32},{48,40},{56,48},{64,5... | collective-permute-start | bytes 786440 | tf_op jit(solution)/shard_map/ppermute | solution.py:440
  32.5 1.3 %collective-permute-done.4.l_ref._ = f32[4,8,2,16,128]{4,3,2,1,0:T(8,128)S(1)} collective-permute-done((f32[4,8,2,16,128]{4,3,2,1,0:T(8,128)S(1)}, f32[4,8,2,16,128]{4,3,2,1,0:T(8,128)S(1)}, u32[]{:S(2)}, u32[]{:S(2)}) %collective-permute-start.4) | collective-permute-done | bytes 524320 | tf_op jit(solution)/shard_map/ppermute | solution.py:440
  33.8 0.1 collective-permute-start.8
  33.9 1.7 %collective-permute-start.10 = (f32[4,8,256]{2,1,0:T(8,128)S(1)}, f32[4,8,256]{2,1,0:T(8,128)S(1)}, u32[]{:S(2)}, u32[]{:S(2)}) collective-permute-start(f32[4,8,256]{2,1,0:T(8,128)S(1)} %shard_map.179), channel_id=1, source_target_pairs={{0,16},{8,24},{16,32},{24,40},{32,48},{40,56},{48,64},{56,72},{64,... | collective-permute-start | bytes 98312 | tf_op jit(solution)/shard_map/ppermute | solution.py:440
  35.6 3.2 %shard_map.176 = (f32[4,256,1024]{2,1,0:T(8,128)}, f32[4,4,8,16,128]{4,3,2,1,0:T(8,128)S(1)}) custom-call(f32[4,8,256,128]{3,2,1,0:T(8,128)S(1)} %get-tuple-element.32.b_ref, f32[4,8,2,16,128]{4,3,2,1,0:T(8,128)S(1)} %collective-permute-done.4.l_ref._, f32[4,8,2,16,128]{4,3,2,1,0:T(8,128)S(1)} %collective-permute-done.5.r_ref._), custom_call_target="tpu_custom_call" | custom-call | flops 4294967296 | bytes 10485760 | tf_op jit(solution)/shard_map/pallas_call | solution.py:426
  38.8 0.9 %collective-permute-done.9.r1_ref = f32[4,32,512]{2,1,0:T(8,128)S(1)} collective-permute-done((f32[4,32,512]{2,1,0:T(8,128)S(1)}, f32[4,32,512]{2,1,0:T(8,128)S(1)}, u32[]{:S(2)}, u32[]{:S(2)}) %collective-permute-start.9) | collective-permute-done | bytes 262176 | tf_op jit(solution)/shard_map/ppermute | solution.py:440
  39.7 2.2 %collective-permute-done.10.l2_ref = f32[4,8,256]{2,1,0:T(8,128)S(1)} collective-permute-done((f32[4,8,256]{2,1,0:T(8,128)S(1)}, f32[4,8,256]{2,1,0:T(8,128)S(1)}, u32[]{:S(2)}, u32[]{:S(2)}) %collective-permute-start.10) | collective-permute-done | bytes 32800 | tf_op jit(solution)/shard_map/ppermute | solution.py:440
  41.9 4.4 %collective-permute-done.8.l1_ref = f32[4,32,512]{2,1,0:T(8,128)S(1)} collective-permute-done((f32[4,32,512]{2,1,0:T(8,128)S(1)}, f32[4,32,512]{2,1,0:T(8,128)S(1)}, u32[]{:S(2)}, u32[]{:S(2)}) %collective-permute-start.8) | collective-permute-done | bytes 262176 | tf_op jit(solution)/shard_map/ppermute | solution.py:440
  46.4 1.8 %shard_map.180 = f32[4,8,2,16,1024]{4,3,2,1,0:T(8,128)} custom-call(f32[4,8,2,16,1024]{4,3,2,1,0:T(8,128)} %bitcast.6, f32[4,4,8,16,128]{4,3,2,1,0:T(8,128)S(1)} %get-tuple-element.36.even_ref, f32[4,64,512]{2,1,0:T(8,128)S(1)} %get-tuple-element.41.o1_ref, f32[4,16,256]{2,1,0:T(8,128)S(1)} %get-tuple-element.42.o2_ref, ...), custom_call_target="tpu_custom_call", output_to_operand_aliasing={{}: (0, {})} | custom-call | flops 1073741824 | bytes 11680768 | tf_op jit(solution)/shard_map/pallas_call | solution.py:426
  (43 shorter events, 0.1 us)
Async XLA Ops:
  0.0 10.6 %copy-start.8 = (bf16[128,1024]{1,0:T(8,128)(2,1)S(1)}, bf16[128,1024]{1,0:T(8,128)(2,1)}, u32[]{:S(2)}) copy-start(bf16[128,1024]{1,0:T(8,128)(2,1)} %constant.50.clone.rims) | copy-start | bytes 786436
  0.0 10.6 %copy-start.6 = (bf16[512,256]{1,0:T(8,128)(2,1)S(1)}, bf16[512,256]{1,0:T(8,128)(2,1)}, u32[]{:S(2)}) copy-start(bf16[512,256]{1,0:T(8,128)(2,1)} %constant.39.clone.t12l) | copy-start | bytes 786436
  0.0 10.6 %copy-start.7 = (bf16[512,256]{1,0:T(8,128)(2,1)S(1)}, bf16[512,256]{1,0:T(8,128)(2,1)}, u32[]{:S(2)}) copy-start(bf16[512,256]{1,0:T(8,128)(2,1)} %constant.38.clone.t12h) | copy-start | bytes 786436
  0.0 10.6 %copy-start.11 = (bf16[256,256]{1,0:T(8,128)(2,1)S(1)}, bf16[256,256]{1,0:T(8,128)(2,1)}, u32[]{:S(2)}) copy-start(bf16[256,256]{1,0:T(8,128)(2,1)} %constant.35.clone.txl) | copy-start | bytes 393220
  0.0 10.6 %copy-start.12 = (bf16[256,256]{1,0:T(8,128)(2,1)S(1)}, bf16[256,256]{1,0:T(8,128)(2,1)}, u32[]{:S(2)}) copy-start(bf16[256,256]{1,0:T(8,128)(2,1)} %constant.34.clone.txh) | copy-start | bytes 393220
  0.0 10.6 %copy-start.9 = (bf16[400,256]{1,0:T(8,128)(2,1)S(1)}, bf16[400,256]{1,0:T(8,128)(2,1)}, u32[]{:S(2)}) copy-start(bf16[400,256]{1,0:T(8,128)(2,1)} %constant.41.clone.zsl) | copy-start | bytes 614404
  2.1 21.1 %collective-permute-start.2 = (f32[4,2,16,1024]{3,2,1,0:T(8,128)S(1)}, f32[4,2,16,1024]{3,2,1,0:T(8,128)S(1)}, u32[]{:S(2)}, u32[]{:S(2)}) collective-permute-start(f32[4,2,16,1024]{3,2,1,0:T(8,128)S(1)} %get-tuple-element.30), channel_id=1, source_target_pairs={{0,8},{8,16},{16,24},{24,32},{32,40},{40,48},{48,56},{56,64},{64,7... | collective-permute-start | bytes 1572872 | tf_op jit(solution)/shard_map/ppermute | solution.py:440
  3.8 19.4 %collective-permute-start.3 = (f32[4,2,16,1024]{3,2,1,0:T(8,128)S(1)}, f32[4,2,16,1024]{3,2,1,0:T(8,128)S(1)}, u32[]{:S(2)}, u32[]{:S(2)}) collective-permute-start(f32[4,2,16,1024]{3,2,1,0:T(8,128)S(1)} %get-tuple-element.31), channel_id=1, source_target_pairs={{0,248},{8,0},{16,8},{24,16},{32,24},{40,32},{48,40},{56,48},{64,5... | collective-permute-start | bytes 1572872 | tf_op jit(solution)/shard_map/ppermute | solution.py:440
  16.1 5.0 %collective-permute-start = (f32[4,16,512]{2,1,0:T(8,128)S(1)}, f32[4,16,512]{2,1,0:T(8,128)S(1)}, u32[]{:S(2)}, u32[]{:S(2)}) collective-permute-start(f32[4,16,512]{2,1,0:T(8,128)S(1)} %get-tuple-element.27), channel_id=1, source_target_pairs={{0,2},{1,3},{2,4},{3,5},{4,6},{5,7},{6,0},{7,1},{8,10},{9,11},{10,... | collective-permute-start | bytes 393224 | tf_op jit(solution)/shard_map/ppermute | solution.py:440
  17.6 5.5 %collective-permute-start.1 = (f32[4,16,512]{2,1,0:T(8,128)S(1)}, f32[4,16,512]{2,1,0:T(8,128)S(1)}, u32[]{:S(2)}, u32[]{:S(2)}) collective-permute-start(f32[4,16,512]{2,1,0:T(8,128)S(1)} %get-tuple-element.28), channel_id=1, source_target_pairs={{0,6},{1,7},{2,0},{3,1},{4,2},{5,3},{6,4},{7,5},{8,14},{9,15},{10,... | collective-permute-start | bytes 393224 | tf_op jit(solution)/shard_map/ppermute | solution.py:440
  18.2 8.7 %collective-permute-start.6 = (f32[4,64,512]{2,1,0:T(8,128)S(1)}, f32[4,64,512]{2,1,0:T(8,128)S(1)}, u32[]{:S(2)}, u32[]{:S(2)}) collective-permute-start(f32[4,64,512]{2,1,0:T(8,128)S(1)} %get-tuple-element.39), channel_id=1, source_target_pairs={{0,1},{1,2},{2,3},{3,4},{4,5},{5,6},{6,7},{7,0},{8,9},{9,10},{10,1... | collective-permute-start | bytes 1572872 | tf_op jit(solution)/shard_map/ppermute | solution.py:440
  21.1 6.8 %collective-permute-start.7 = (f32[4,64,512]{2,1,0:T(8,128)S(1)}, f32[4,64,512]{2,1,0:T(8,128)S(1)}, u32[]{:S(2)}, u32[]{:S(2)}) collective-permute-start(f32[4,64,512]{2,1,0:T(8,128)S(1)} %get-tuple-element.40), channel_id=1, source_target_pairs={{0,7},{1,0},{2,1},{3,2},{4,3},{5,4},{6,5},{7,6},{8,15},{9,8},{10,9... | collective-permute-start | bytes 1572872 | tf_op jit(solution)/shard_map/ppermute | solution.py:440
  25.1 8.7 %collective-permute-start.4 = (f32[4,8,2,16,128]{4,3,2,1,0:T(8,128)S(1)}, f32[4,8,2,16,128]{4,3,2,1,0:T(8,128)S(1)}, u32[]{:S(2)}, u32[]{:S(2)}) collective-permute-start(f32[4,8,2,16,128]{4,3,2,1,0:T(8,128)S(1)} %get-tuple-element.33), channel_id=1, source_target_pairs={{0,1},{1,2},{2,3},{3,4},{4,5},{5,6},{6,7},{7,0},{8,9},{9,10},{10,1... | collective-permute-start | bytes 1572872 | tf_op jit(solution)/shard_map/ppermute | solution.py:440
  25.5 8.3 %collective-permute-start.5 = (f32[4,8,2,16,128]{4,3,2,1,0:T(8,128)S(1)}, f32[4,8,2,16,128]{4,3,2,1,0:T(8,128)S(1)}, u32[]{:S(2)}, u32[]{:S(2)}) collective-permute-start(f32[4,8,2,16,128]{4,3,2,1,0:T(8,128)S(1)} %get-tuple-element.34), channel_id=1, source_target_pairs={{0,7},{1,0},{2,1},{3,2},{4,3},{5,4},{6,5},{7,6},{8,15},{9,8},{10,9... | collective-permute-start | bytes 1572872 | tf_op jit(solution)/shard_map/ppermute | solution.py:440
  29.0 9.8 %collective-permute-start.11 = (f32[4,8,256]{2,1,0:T(8,128)S(1)}, f32[4,8,256]{2,1,0:T(8,128)S(1)}, u32[]{:S(2)}, u32[]{:S(2)}) collective-permute-start(f32[4,8,256]{2,1,0:T(8,128)S(1)} %get-tuple-element.46), channel_id=1, source_target_pairs={{0,240},{8,248},{16,0},{24,8},{32,16},{40,24},{48,32},{56,40},{64,... | collective-permute-start | bytes 98312 | tf_op jit(solution)/shard_map/ppermute | solution.py:440
  31.1 8.6 %collective-permute-start.9 = (f32[4,32,512]{2,1,0:T(8,128)S(1)}, f32[4,32,512]{2,1,0:T(8,128)S(1)}, u32[]{:S(2)}, u32[]{:S(2)}) collective-permute-start(f32[4,32,512]{2,1,0:T(8,128)S(1)} %get-tuple-element.44), channel_id=1, source_target_pairs={{0,248},{8,0},{16,8},{24,16},{32,24},{40,32},{48,40},{56,48},{64,5... | collective-permute-start | bytes 786440 | tf_op jit(solution)/shard_map/ppermute | solution.py:440
  33.8 12.6 %collective-permute-start.8 = (f32[4,32,512]{2,1,0:T(8,128)S(1)}, f32[4,32,512]{2,1,0:T(8,128)S(1)}, u32[]{:S(2)}, u32[]{:S(2)}) collective-permute-start(f32[4,32,512]{2,1,0:T(8,128)S(1)} %shard_map.178), channel_id=1, source_target_pairs={{0,8},{8,16},{16,24},{24,32},{32,40},{40,48},{48,56},{56,64},{64,7... | collective-permute-start | bytes 786440 | tf_op jit(solution)/shard_map/ppermute | solution.py:440
  33.9 8.0 %collective-permute-start.10 = (f32[4,8,256]{2,1,0:T(8,128)S(1)}, f32[4,8,256]{2,1,0:T(8,128)S(1)}, u32[]{:S(2)}, u32[]{:S(2)}) collective-permute-start(f32[4,8,256]{2,1,0:T(8,128)S(1)} %shard_map.179), channel_id=1, source_target_pairs={{0,16},{8,24},{16,32},{24,40},{32,48},{40,56},{48,64},{56,72},{64,... | collective-permute-start | bytes 98312 | tf_op jit(solution)/shard_map/ppermute | solution.py:440
  35.5 10.8 %copy-start = (bf16[512,512]{1,0:T(8,128)(2,1)S(1)}, bf16[512,512]{1,0:T(8,128)(2,1)}, u32[]{:S(2)}) copy-start(bf16[512,512]{1,0:T(8,128)(2,1)} %constant.37.clone.t1l) | copy-start | bytes 1572868
  35.5 10.8 %copy-start.1 = (bf16[512,512]{1,0:T(8,128)(2,1)S(1)}, bf16[512,512]{1,0:T(8,128)(2,1)}, u32[]{:S(2)}) copy-start(bf16[512,512]{1,0:T(8,128)(2,1)} %constant.36.clone.t1h) | copy-start | bytes 1572868
  35.5 10.8 %copy-start.2 = (bf16[64,48]{1,0:T(8,128)(2,1)S(1)}, bf16[64,48]{1,0:T(8,128)(2,1)}, u32[]{:S(2)}) copy-start(bf16[64,48]{1,0:T(8,128)(2,1)} %constant.47.clone.g1l) | copy-start | bytes 18436
  35.6 10.8 %copy-start.3 = (bf16[64,48]{1,0:T(8,128)(2,1)S(1)}, bf16[64,48]{1,0:T(8,128)(2,1)}, u32[]{:S(2)}) copy-start(bf16[64,48]{1,0:T(8,128)(2,1)} %constant.46.clone.g1h) | copy-start | bytes 18436
  35.6 10.8 %copy-start.4 = (bf16[16,48]{1,0:T(8,128)(2,1)S(1)}, bf16[16,48]{1,0:T(8,128)(2,1)}, u32[]{:S(2)}) copy-start(bf16[16,48]{1,0:T(8,128)(2,1)} %constant.49.clone.g2l) | copy-start | bytes 4612
  35.6 10.8 %copy-start.5 = (bf16[16,48]{1,0:T(8,128)(2,1)S(1)}, bf16[16,48]{1,0:T(8,128)(2,1)}, u32[]{:S(2)}) copy-start(bf16[16,48]{1,0:T(8,128)(2,1)} %constant.48.clone.g2h) | copy-start | bytes 4612
  (5 other events, 29.6 us)
